TPU v7x, 32 devices: a whole 2x2x4 slice. The times are simulated.
32 devices in a mesh: dp: 4 (over x, core), seq: 8 (over z, y).
Axes of the slice: x: 2, y: 2, z: 4, core: 2. Of those that a mesh axis runs over, the one named last changes fastest.
Arguments:
- tokens: bfloat16 [4, 2048, 1024], P('dp', 'seq'), may hold values from -6 to 6
- target: bfloat16 [4, 2048, 1024], P('dp', 'seq'), may hold values from -6 to 6
- valid: int32 [4, 2048], P('dp', 'seq'), may hold values from 0 to 1
- in_weight: bfloat16 [1024, 4608], P('seq'), may hold values from -0.1875 to 0.1875
- small_weight: bfloat16 [1024, 12], P('seq'), may hold values from -0.1875 to 0.1875
- out_weight: bfloat16 [1024, 1536], P('seq'), may hold values from -0.15625 to 0.15625
- ffn_in: bfloat16 [1024, 5632], P('seq'), may hold values from -0.1875 to 0.1875
- ffn_out: bfloat16 [1024, 2816], P('seq'), may hold values from -0.109375 to 0.109375
- gain_first: float32 [1024], replicated, may hold values from 0.5 to 1.5
- gain_second: float32 [1024], replicated, may hold values from 0.5 to 1.5
- gain_out: float32 [256], replicated, may hold values from 0.5 to 1.5
- conv_weight: float32 [4, 3072], replicated, may hold values from -2.5 to 2.5
- decay_log: float32 [6], replicated, may hold values from -10 to -2.5
- decay_bias: float32 [6], replicated, may hold values from -1 to 1
Outputs:
- block_out: bfloat16 [4, 2048, 1024], P('dp', 'seq')
- loss_value: float32 [], replicated
- grad_tokens: float32 [4, 2048, 1024], P('dp', 'seq')
- grad_in_weight: float32 [1024, 4608], P('seq')
- grad_small_weight: float32 [1024, 12], P('seq')
- grad_out_weight: float32 [1024, 1536], P('seq')
- grad_ffn_in: float32 [1024, 5632], P('seq')
- grad_ffn_out: float32 [1024, 2816], P('seq')
- grad_gain_first: float32 [1024], replicated
- grad_gain_second: float32 [1024], replicated
- grad_gain_out: float32 [256], replicated
- grad_conv_weight: float32 [4, 3072], replicated
- grad_decay_log: float32 [6], replicated
- grad_decay_bias: float32 [6], replicated
All inputs are finite; a program needn't handle non-finite values.
Results may differ from a plain program's by a relative error of at most 0.019.
The roundings to bfloat16 on the way count: a program that leaves them out, or rounds other values in their place, can miss the bound.
Values may be sent and summed in bfloat16 or wider, within the bound.
A program may use at most 256 MiB of HBM per device.

v0:
```python
import jax
import jax.numpy as jnp
from jax import lax
from jax.sharding import PartitionSpec as P

HEADS = 6
DK = 128
DV = 256
FF = 2816
CONV = 4
BLOCK = 64
KEYS = 768
VALUES = 1536


precise = lax.Precision.HIGHEST
epsilon = 1e-06


def shifted(value, axis, steps):
    count = lax.axis_size(axis)
    leading, last = (max(0, -steps), min(count, count - steps))
    return lax.ppermute(value, axis, [(source, source + steps) for source in range(leading, last)])


def rms_scale(field_in, gain_vec):
    return (
        field_in
        * lax.rsqrt(jnp.mean(field_in * field_in, axis=-1, keepdims=True) + epsilon)
        * gain_vec
    )


def unit_rows(field_in):
    return field_in * lax.rsqrt(jnp.sum(field_in * field_in, axis=-1, keepdims=True) + epsilon)


def block_frame(key_rows, strength, forget):
    block_size = forget.shape[1]
    cumulative = jnp.cumsum(forget, axis=1)
    row_ids = lax.broadcasted_iota(jnp.int32, (block_size, block_size), 0)
    col_ids = lax.broadcasted_iota(jnp.int32, (block_size, block_size), 1)
    lower_mask = (row_ids >= col_ids).astype(jnp.float32)
    strict = (row_ids > col_ids).astype(jnp.float32)
    decays = jnp.exp((cumulative[:, :, None] - cumulative[:, None, :]) * lower_mask) * lower_mask
    keys_dot = jnp.einsum("hid,hjd->hij", key_rows, key_rows, precision=precise)
    system = (
        jnp.eye(block_size, dtype=jnp.float32) + strength[:, :, None] * keys_dot * decays * strict
    )
    return (cumulative, decays, system)


def block_step(memory, pieces):
    queries, key_rows, values, strength, forget = pieces
    cumulative, decays, system = block_frame(key_rows, strength, forget)
    growth = jnp.exp(cumulative)
    projected = jnp.einsum("hcd,hdv->hcv", key_rows, memory, precision=precise)
    wanted = strength[:, :, None] * (values - growth[:, :, None] * projected)
    update = jax.scipy.linalg.solve_triangular(system, wanted, lower=True, unit_diagonal=True)
    scores = jnp.einsum("hid,hjd->hij", queries, key_rows, precision=precise) * decays
    read_out = jnp.einsum("hcd,hdv->hcv", queries, memory, precision=precise)
    output = growth[:, :, None] * read_out + jnp.einsum(
        "hij,hjv->hiv", scores, update, precision=precise
    )
    final_log = cumulative[:, -1]
    weights = jnp.exp(final_log[:, None] - cumulative)
    new_memory = jnp.exp(final_log)[:, None, None] * memory + jnp.einsum(
        "hcd,hcv->hdv", key_rows * weights[:, :, None], update, precision=precise
    )
    return (new_memory, output)


def block_map(carry, pieces):
    mapping, offset = carry
    key_rows, values, strength, forget = pieces
    cumulative, decays, system = block_frame(key_rows, strength, forget)
    growth = jnp.exp(cumulative)
    final_log = cumulative[:, -1]
    weights = jnp.exp(final_log[:, None] - cumulative)
    wanted = jnp.concatenate(
        [(strength * growth)[:, :, None] * key_rows, strength[:, :, None] * values], axis=2
    )
    solved = jax.scipy.linalg.solve_triangular(system, wanted, lower=True, unit_diagonal=True)
    swept = jnp.einsum("hcd,hce->hde", key_rows * weights[:, :, None], solved, precision=precise)
    step_map = jnp.exp(final_log)[:, None, None] * jnp.eye(DK, dtype=jnp.float32) - swept[:, :, :DK]
    new_mapping = jnp.einsum("hde,hef->hdf", step_map, mapping, precision=precise)
    new_offset = jnp.einsum("hde,hev->hdv", step_map, offset, precision=precise) + swept[:, :, DK:]
    return ((new_mapping, new_offset), None)


def to_blocks(field_in):
    blocks = field_in.shape[0] // BLOCK
    return jnp.swapaxes(field_in.reshape((blocks, BLOCK) + field_in.shape[1:]), 1, 2)


def run_blocks(entering, queries, key_rows, values, strength, forget):
    length = queries.shape[0]
    pieces = (
        to_blocks(queries),
        to_blocks(key_rows),
        to_blocks(values),
        to_blocks(strength),
        to_blocks(forget),
    )
    leaving, outputs = lax.scan(block_step, entering, pieces)
    return (jnp.swapaxes(outputs, 1, 2).reshape(length, HEADS, DV), leaving)


def prepare(padded, little, conv_weight, decay_log, decay_bias):
    length = padded.shape[0] - (CONV - 1)
    convolved = conv_weight[0] * padded[0:length]
    for offset in range(1, CONV):
        convolved = convolved + conv_weight[offset] * padded[offset : offset + length]
    active = jax.nn.silu(convolved)
    queries = unit_rows(active[:, :KEYS].reshape(length, HEADS, DK)) * DK ** (-0.5)
    key_rows = unit_rows(active[:, KEYS : 2 * KEYS].reshape(length, HEADS, DK))
    values = active[:, 2 * KEYS :].reshape(length, HEADS, DV)
    strength = jax.nn.sigmoid(little[:, :HEADS])
    forget = -jnp.exp(decay_log) * jax.nn.softplus(little[:, HEADS:] + decay_bias)
    return (queries, key_rows, values, strength, forget)


def gated_norm(mixed_out, gate_pre, gain_out):
    length = mixed_out.shape[0]
    return (
        rms_scale(mixed_out, gain_out) * jax.nn.silu(gate_pre.reshape(length, HEADS, DV))
    ).reshape(length, VALUES)


def swiglu(gate_up):
    return jax.nn.silu(gate_up[:, :FF]) * gate_up[:, FF:]


def on_device(
    tokens,
    target,
    valid,
    in_weight,
    small_weight,
    out_weight,
    ffn_in,
    ffn_out,
    gain_first,
    gain_second,
    gain_out,
    conv_weight,
    decay_log,
    decay_bias,
):
    inputs = tokens[0].astype(jnp.float32)
    length = inputs.shape[0]
    w_in, w_small = (
        lax.all_gather(in_weight, "seq", axis=0, tiled=True),
        lax.all_gather(small_weight, "seq", axis=0, tiled=True),
    )
    normed_f, first_pull = jax.vjp(rms_scale, inputs, gain_first)
    normed = normed_f.astype(jnp.bfloat16)
    project = jnp.dot(normed, w_in, preferred_element_type=jnp.float32)
    little = jnp.dot(normed, w_small, preferred_element_type=jnp.float32)
    mixed_in = project[:, : 2 * KEYS + VALUES].astype(jnp.bfloat16)
    gate_pre = project[:, 2 * KEYS + VALUES :]
    rim_rows = shifted(mixed_in[length - (CONV - 1) :], "seq", 1)
    padded = jnp.concatenate([rim_rows, mixed_in], axis=0).astype(jnp.float32)
    prepared, local_pull = jax.vjp(prepare, padded, little, conv_weight, decay_log, decay_bias)
    queries, key_rows, values, strength, forget = prepared
    eye_stack = jnp.broadcast_to(jnp.eye(DK, dtype=jnp.float32), (HEADS, DK, DK))
    zero_state = jnp.zeros((HEADS, DK, DV), jnp.float32)
    (mapping, offset), unused = lax.scan(
        block_map,
        (eye_stack, zero_state),
        (to_blocks(key_rows), to_blocks(values), to_blocks(strength), to_blocks(forget)),
    )

    def relay_step(turn_index, incoming):
        outgoing = jnp.einsum("hde,hev->hdv", mapping, incoming, precision=precise) + offset
        return shifted(outgoing, "seq", 1)

    entering = lax.fori_loop(0, lax.axis_size("seq") - 1, relay_step, zero_state)
    (mixed_out, leaving), delta_pull = jax.vjp(
        run_blocks, entering, queries, key_rows, values, strength, forget
    )
    branch_f, gated_pull = jax.vjp(gated_norm, mixed_out, gate_pre, gain_out)
    branch = branch_f.astype(jnp.bfloat16)
    w_out, w_up, w_down = (
        lax.all_gather(out_weight, "seq", axis=0, tiled=True),
        lax.all_gather(ffn_in, "seq", axis=0, tiled=True),
        lax.all_gather(ffn_out, "seq", axis=0, tiled=True),
    )
    attended = jnp.einsum("tv,dv->td", branch, w_out, preferred_element_type=jnp.float32)
    hidden = inputs + attended
    second_f, second_pull = jax.vjp(rms_scale, hidden, gain_second)
    second = second_f.astype(jnp.bfloat16)
    gate_up = jnp.dot(second, w_up, preferred_element_type=jnp.float32)
    active_f, swiglu_pull = jax.vjp(swiglu, gate_up)
    active = active_f.astype(jnp.bfloat16)
    feed_out = jnp.einsum("tf,df->td", active, w_down, preferred_element_type=jnp.float32)
    summed = hidden + feed_out
    mask_row = valid[0].astype(jnp.float32)
    errors = summed - target[0].astype(jnp.float32)
    totals = lax.psum(
        (jnp.sum(mask_row * jnp.mean(errors * errors, axis=-1)), jnp.sum(mask_row)), ("dp", "seq")
    )
    valid_count = jnp.maximum(totals[1], 1.0)
    loss_value = totals[0] / valid_count
    all_tokens = length * lax.axis_size("dp") * lax.axis_size("seq")
    grad_summed = all_tokens / valid_count * mask_row[:, None] * errors
    grad_feed = grad_summed.astype(jnp.bfloat16)
    grad_active = jnp.dot(grad_feed, w_down, preferred_element_type=jnp.float32)
    grad_ffn_out = jnp.einsum("td,tf->df", grad_feed, active, preferred_element_type=jnp.float32)
    grad_gate_up = swiglu_pull(grad_active)[0].astype(jnp.bfloat16)
    grad_ffn_in = jnp.einsum("td,tf->df", second, grad_gate_up, preferred_element_type=jnp.float32)
    grad_second = jnp.einsum("tf,df->td", grad_gate_up, w_up, preferred_element_type=jnp.float32)
    hidden_part, grad_gain_second = second_pull(grad_second)
    grad_hidden = grad_summed + hidden_part
    grad_attn = grad_hidden.astype(jnp.bfloat16)
    grad_out_weight = jnp.einsum("td,tv->dv", grad_attn, branch, preferred_element_type=jnp.float32)
    grad_branch = jnp.dot(grad_attn, w_out, preferred_element_type=jnp.float32)
    grad_mixed, grad_gate_pre, grad_gain_out = gated_pull(grad_branch)
    first_terms = delta_pull((grad_mixed, jnp.zeros_like(leaving)))
    mapping_t = jnp.swapaxes(mapping, 1, 2)

    def relay_back(turn_index, arriving):
        going = jnp.einsum("hde,hev->hdv", mapping_t, arriving, precision=precise) + first_terms[0]
        return shifted(going, "seq", -1)

    grad_leaving = lax.fori_loop(0, lax.axis_size("seq") - 1, relay_back, zero_state)
    later_terms = delta_pull((jnp.zeros_like(mixed_out), grad_leaving))
    grad_prepared = (
        first_terms[1] + later_terms[1],
        first_terms[2] + later_terms[2],
        first_terms[3] + later_terms[3],
        first_terms[4] + later_terms[4],
        first_terms[5] + later_terms[5],
    )
    grad_padded, grad_little, grad_conv, grad_decay_log, grad_decay_bias = local_pull(grad_prepared)
    rim_grad = shifted(grad_padded[: CONV - 1].astype(jnp.bfloat16), "seq", -1).astype(jnp.float32)
    grad_mixed_in = grad_padded[CONV - 1 :] + jnp.concatenate(
        [jnp.zeros((length - (CONV - 1), grad_padded.shape[1]), jnp.float32), rim_grad], axis=0
    )
    grad_project = jnp.concatenate([grad_mixed_in, grad_gate_pre], axis=1).astype(jnp.bfloat16)
    grad_little_b = grad_little.astype(jnp.bfloat16)
    grad_in_weight = jnp.einsum(
        "td,tp->dp", normed, grad_project, preferred_element_type=jnp.float32
    )
    grad_small_weight = jnp.einsum(
        "td,ts->ds", normed, grad_little_b, preferred_element_type=jnp.float32
    )
    grad_normed = jnp.einsum(
        "tp,dp->td", grad_project, w_in, preferred_element_type=jnp.float32
    ) + jnp.einsum("ts,ds->td", grad_little_b, w_small, preferred_element_type=jnp.float32)
    input_part, grad_gain_first = first_pull(grad_normed)
    grad_tokens = grad_hidden + input_part
    stored = (
        lax.psum_scatter(
            grad_in_weight.astype(jnp.bfloat16), "seq", scatter_dimension=0, tiled=True
        ).astype(jnp.float32),
        lax.psum_scatter(
            grad_small_weight.astype(jnp.bfloat16), "seq", scatter_dimension=0, tiled=True
        ).astype(jnp.float32),
        lax.psum_scatter(
            grad_out_weight.astype(jnp.bfloat16), "seq", scatter_dimension=0, tiled=True
        ).astype(jnp.float32),
        lax.psum_scatter(
            grad_ffn_in.astype(jnp.bfloat16), "seq", scatter_dimension=0, tiled=True
        ).astype(jnp.float32),
        lax.psum_scatter(
            grad_ffn_out.astype(jnp.bfloat16), "seq", scatter_dimension=0, tiled=True
        ).astype(jnp.float32),
    )
    stored = (
        lax.psum(stored[0].astype(jnp.bfloat16), "dp").astype(jnp.float32),
        lax.psum(stored[1].astype(jnp.bfloat16), "dp").astype(jnp.float32),
        lax.psum(stored[2].astype(jnp.bfloat16), "dp").astype(jnp.float32),
        lax.psum(stored[3].astype(jnp.bfloat16), "dp").astype(jnp.float32),
        lax.psum(stored[4].astype(jnp.bfloat16), "dp").astype(jnp.float32),
    )
    smalls = lax.psum(
        (
            grad_gain_first,
            grad_gain_second,
            grad_gain_out,
            grad_conv,
            grad_decay_log,
            grad_decay_bias,
        ),
        ("dp", "seq"),
    )
    return (
        summed.astype(jnp.bfloat16)[None],
        loss_value,
        grad_tokens[None],
        stored[0],
        stored[1],
        stored[2],
        stored[3],
        stored[4],
        smalls[0],
        smalls[1],
        smalls[2],
        smalls[3],
        smalls[4],
        smalls[5],
    )


def solution(mesh):
    placed = (
        P("dp", "seq", None),
        P("dp", "seq", None),
        P("dp", "seq"),
        P("seq", None),
        P("seq", None),
        P("seq", None),
        P("seq", None),
        P("seq", None),
        P(),
        P(),
        P(),
        P(),
        P(),
        P(),
    )
    return jax.shard_map(
        on_device,
        mesh=mesh,
        in_specs=placed,
        out_specs=(
            P("dp", "seq", None),
            P(),
            P("dp", "seq", None),
            P("seq", None),
            P("seq", None),
            P("seq", None),
            P("seq", None),
            P("seq", None),
            P(),
            P(),
            P(),
            P(),
            P(),
            P(),
        ),
        check_vma=False,
    )
```

profile of v0, /device:TPU:0, one launch (start us, length us, event | category | flops | bytes accessed | tf_op | source)
XLA Modules:
  0.0 2181.4 jit_solution(4750612536897988892)
XLA Ops:
  10.7 28.2 %all_gather.15 = bf16[1024,12]{0,1:T(8,128)(2,1)S(1)} all-gather(bf16[128,12]{0,1:T(8,128)(2,1)S(1)} %copy-done.103), channel_id=1, replica_groups=mesh['dp'=4,'seq'=8] {'seq'}, dimensions={0}, use_global_device_ids=true | all-gather | bytes 27648 | tf_op jit(solution)/shard_map/all_gather | solution.py:154
  40.3 40.2 %psum.92 = f32[]{:T(128)} all-reduce(f32[]{:T(128)} %convert_reduce_fusion), channel_id=1, replica_groups=mesh['dp'=4,'seq'=8] {'dp','seq'}, use_global_device_ids=true, to_apply=%region_17.18 | all-reduce | flops 1 | bytes 8 | tf_op jit(solution)/shard_map/psum | solution.py:200
  82.4 70.1 %all-gather.5.cloned.1.call-done = bf16[1024,4608]{1,0:T(8,128)(2,1)} async-done(((bf16[128,4608]{1,0:T(8,128)(2,1)}), bf16[1024,4608]{1,0:T(8,128)(2,1)}) %all-gather.5.cloned.1.call-update) | async-done | bytes 9437200 | tf_op jit(solution)/shard_map/all_gather | solution.py:153
  189.6 174.6 %while.151 = (s32[]{:T(128)}, f32[6,128,128]{2,1,0:T(8,128)}, f32[6,128,256]{2,1,0:T(8,128)}, f32[4,6,64]{2,1,0:T(8,128)}, f32[4,6,64,128]{3,2,1,0:T(8,128)S(1)}...) while((s32[]{:T(128)}, f32[6,128,128]{2,1,0:T(8,128)}, ...), condition=%wide.region_4.5_spmd.clone, body=%wide.region_2.0_spmd.clone.sunk | while | flops 831918528 | bytes 14858323 | solution.py:168
  195.1 29.5 %custom-call.43 = f32[6,1,64,64]{2,3,1,0:T(8,128)S(1)} custom-call(f32[6,1,64,64]{3,2,1,0:T(8,128)S(1)} %fusion.575), custom_call_target="InvertDiagBlocksLowerTriangular" | custom-call | tf_op jit(solution)/shard_map/while/body/eval_jaxpr/jit(_solve_triangular)/vmap()/triangular_solve | solution.py:83
  238.5 29.5 %custom-call.43 = f32[6,1,64,64]{2,3,1,0:T(8,128)S(1)} custom-call(f32[6,1,64,64]{3,2,1,0:T(8,128)S(1)} %fusion.575), custom_call_target="InvertDiagBlocksLowerTriangular" | custom-call | tf_op jit(solution)/shard_map/while/body/eval_jaxpr/jit(_solve_triangular)/vmap()/triangular_solve | solution.py:83
  282.3 29.5 %custom-call.43 = f32[6,1,64,64]{2,3,1,0:T(8,128)S(1)} custom-call(f32[6,1,64,64]{3,2,1,0:T(8,128)S(1)} %fusion.575), custom_call_target="InvertDiagBlocksLowerTriangular" | custom-call | tf_op jit(solution)/shard_map/while/body/eval_jaxpr/jit(_solve_triangular)/vmap()/triangular_solve | solution.py:83
  326.0 29.5 %custom-call.43 = f32[6,1,64,64]{2,3,1,0:T(8,128)S(1)} custom-call(f32[6,1,64,64]{3,2,1,0:T(8,128)S(1)} %fusion.575), custom_call_target="InvertDiagBlocksLowerTriangular" | custom-call | tf_op jit(solution)/shard_map/while/body/eval_jaxpr/jit(_solve_triangular)/vmap()/triangular_solve | solution.py:83
  368.9 212.7 %while.147 = (s32[]{:T(128)}, f32[6,128,256]{2,1,0:T(8,128)S(1)}, f32[6,128,128]{2,1,0:T(8,128)}, f32[6,128,256]{2,1,0:T(8,128)}, s32[]{:T(128)}) while((s32[]{:T(128)}, f32[6,128,256]{2,1,0:T(8,128)S(1)}, f32[6,128,128]{2,1,0:T(8,128)}, f32[6,128,256]{2,1,0:T(8,128)}, s32[]{:T(128)}) %tuple.324), condition=%wide.region_6.7_spmd, body=%wide.region_5.6_spmd.sunk | while | flops 302186496 | bytes 5898341 | solution.py:178
  437.7 33.6 %collective-permute-done = f32[6,128,256]{2,1,0:T(8,128)S(1)} collective-permute-done((f32[6,128,256]{2,1,0:T(8,128)}, f32[6,128,256]{2,1,0:T(8,128)S(1)}, u32[]{:S(2)}, u32[]{:S(2)}) %collective-permute-start) | collective-permute-done | bytes 786464 | tf_op jit(solution)/shard_map/while/body/eval_jaxpr/ppermute | solution.py:23
  588.3 216.5 %while.149 = (s32[]{:T(128)}, f32[6,128,256]{2,1,0:T(8,128)S(1)}, f32[4,6,64,256]{3,2,1,0:T(8,128)}, f32[4,6,64,64]{3,2,1,0:T(8,128)}, f32[4,6,64,64]{3,2,1,0:T(...) while((s32[]{:T(128)}, f32[6,128,256]{2,1,0:T(8,128)S(1)}, ...), condition=%wide.region_10.11_spmd.clone.clone, body=%wide.region_8.10_spmd.clone.clone.sunk | while | flops 681308992 | bytes 16525905 | solution.py:105
  600.9 30.9 %custom-call.41 = f32[6,1,64,64]{2,3,1,0:T(8,128)} custom-call(f32[6,1,64,64]{3,2,1,0:T(8,128)} %get-tuple-element.3849), custom_call_target="InvertDiagBlocksLowerTriangular" | custom-call | tf_op jit(solution)/shard_map/jvp()/while/body/eval_jaxpr/jit(_solve_triangular)/vmap()/triangular_solve | solution.py:59
  654.9 30.9 %custom-call.41 = f32[6,1,64,64]{2,3,1,0:T(8,128)} custom-call(f32[6,1,64,64]{3,2,1,0:T(8,128)} %get-tuple-element.3849), custom_call_target="InvertDiagBlocksLowerTriangular" | custom-call | tf_op jit(solution)/shard_map/jvp()/while/body/eval_jaxpr/jit(_solve_triangular)/vmap()/triangular_solve | solution.py:59
  708.9 30.9 %custom-call.41 = f32[6,1,64,64]{2,3,1,0:T(8,128)} custom-call(f32[6,1,64,64]{3,2,1,0:T(8,128)} %get-tuple-element.3849), custom_call_target="InvertDiagBlocksLowerTriangular" | custom-call | tf_op jit(solution)/shard_map/jvp()/while/body/eval_jaxpr/jit(_solve_triangular)/vmap()/triangular_solve | solution.py:59
  762.9 30.9 %custom-call.41 = f32[6,1,64,64]{2,3,1,0:T(8,128)} custom-call(f32[6,1,64,64]{3,2,1,0:T(8,128)} %get-tuple-element.3849), custom_call_target="InvertDiagBlocksLowerTriangular" | custom-call | tf_op jit(solution)/shard_map/jvp()/while/body/eval_jaxpr/jit(_solve_triangular)/vmap()/triangular_solve | solution.py:59
  898.2 247.8 %while.152 = (s32[]{:T(128)}, f32[6,128,256]{2,1,0:T(8,128)S(1)}, f32[4,6,64,128]{3,2,0,1:T(8,128)}, f32[4,6,64,128]{3,2,0,1:T(8,128)}, f32[4,6,64,256]{3,2,1,0:...) while((s32[]{:T(128)}, f32[6,128,256]{2,1,0:T(8,128)S(1)}, ...), condition=%wide.region_31.33_spmd.clone.clone, body=%wide.region_20.32_spmd.clone.clone.sunk | while | flops 1382356608 | bytes 50387104 | solution.py:105
  912.3 29.5 %custom-call.44 = f32[6,1,64,64]{2,3,1,0:T(8,128)S(1)} custom-call(f32[6,1,64,64]{3,2,1,0:T(8,128)S(1)} %fusion.607), custom_call_target="InvertDiagBlocksLowerTriangular" | custom-call | tf_op jit(solution)/shard_map/transpose(jvp())/while/body/eval_jaxpr/jit(_solve_triangular)/vmap()/triangular_solve | solution.py:59
  974.2 29.5 %custom-call.44 = f32[6,1,64,64]{2,3,1,0:T(8,128)S(1)} custom-call(f32[6,1,64,64]{3,2,1,0:T(8,128)S(1)} %fusion.607), custom_call_target="InvertDiagBlocksLowerTriangular" | custom-call | tf_op jit(solution)/shard_map/transpose(jvp())/while/body/eval_jaxpr/jit(_solve_triangular)/vmap()/triangular_solve | solution.py:59
  1036.1 29.5 %custom-call.44 = f32[6,1,64,64]{2,3,1,0:T(8,128)S(1)} custom-call(f32[6,1,64,64]{3,2,1,0:T(8,128)S(1)} %fusion.607), custom_call_target="InvertDiagBlocksLowerTriangular" | custom-call | tf_op jit(solution)/shard_map/transpose(jvp())/while/body/eval_jaxpr/jit(_solve_triangular)/vmap()/triangular_solve | solution.py:59
  1097.8 29.5 %custom-call.44 = f32[6,1,64,64]{2,3,1,0:T(8,128)S(1)} custom-call(f32[6,1,64,64]{3,2,1,0:T(8,128)S(1)} %fusion.607), custom_call_target="InvertDiagBlocksLowerTriangular" | custom-call | tf_op jit(solution)/shard_map/transpose(jvp())/while/body/eval_jaxpr/jit(_solve_triangular)/vmap()/triangular_solve | solution.py:59
  1152.8 179.0 %while.148 = (s32[]{:T(128)}, f32[6,128,256]{2,1,0:T(8,128)S(1)}, f32[6,128,128]{2,1,0:T(8,128)S(1)}, f32[6,128,256]{2,1,0:T(8,128)S(1)}, s32[]{:T(128)}) while((s32[]{:T(128)}, f32[6,128,256]{2,1,0:T(8,128)S(1)}, f32[6,128,128]{2,1,0:T(8,128)S(1)}, f32[6,128,256]{2,1,0:T(8,128)S(1)}, s32[]{:T(128)}) %tuple.370), condition=%wide.region_33.35_spmd, body=%wide.region_32.34_spmd.sunk | while | flops 302186496 | bytes 5898341 | solution.py:226
  1185.5 28.9 %collective-permute-done.1 = f32[6,128,256]{2,1,0:T(8,128)S(1)} collective-permute-done((f32[6,128,256]{2,1,0:T(8,128)}, f32[6,128,256]{2,1,0:T(8,128)S(1)}, u32[]{:S(2)}, u32[]{:S(2)}) %collective-permute-start.1) | collective-permute-done | bytes 786464 | tf_op jit(solution)/shard_map/while/body/eval_jaxpr/ppermute | solution.py:23
  1217.3 36.4 %collective-permute-done.1 = f32[6,128,256]{2,1,0:T(8,128)S(1)} collective-permute-done((f32[6,128,256]{2,1,0:T(8,128)}, f32[6,128,256]{2,1,0:T(8,128)S(1)}, u32[]{:S(2)}, u32[]{:S(2)}) %collective-permute-start.1) | collective-permute-done | bytes 786464 | tf_op jit(solution)/shard_map/while/body/eval_jaxpr/ppermute | solution.py:23
  1336.3 255.3 %while.150 = (s32[]{:T(128)}, f32[6,128,256]{2,1,0:T(8,128)S(1)}, f32[4,6,64,128]{3,2,0,1:T(8,128)}, f32[4,6,64,128]{3,2,0,1:T(8,128)}, f32[4,6,64,256]{3,2,1,0:...) while((s32[]{:T(128)}, f32[6,128,256]{2,1,0:T(8,128)S(1)}, ...), condition=%wide.region_45.47_spmd.clone.clone, body=%wide.region_34.46_spmd.clone.clone.sunk | while | flops 1381373824 | bytes 34255912 | solution.py:105
  1349.3 29.5 %custom-call.42 = f32[6,1,64,64]{2,3,1,0:T(8,128)S(1)} custom-call(f32[6,1,64,64]{3,2,1,0:T(8,128)S(1)} %fusion.550), custom_call_target="InvertDiagBlocksLowerTriangular" | custom-call | tf_op jit(solution)/shard_map/transpose(jvp())/while/body/eval_jaxpr/jit(_solve_triangular)/vmap()/triangular_solve | solution.py:59
  1413.1 29.5 %custom-call.42 = f32[6,1,64,64]{2,3,1,0:T(8,128)S(1)} custom-call(f32[6,1,64,64]{3,2,1,0:T(8,128)S(1)} %fusion.550), custom_call_target="InvertDiagBlocksLowerTriangular" | custom-call | tf_op jit(solution)/shard_map/transpose(jvp())/while/body/eval_jaxpr/jit(_solve_triangular)/vmap()/triangular_solve | solution.py:59
  1476.9 29.5 %custom-call.42 = f32[6,1,64,64]{2,3,1,0:T(8,128)S(1)} custom-call(f32[6,1,64,64]{3,2,1,0:T(8,128)S(1)} %fusion.550), custom_call_target="InvertDiagBlocksLowerTriangular" | custom-call | tf_op jit(solution)/shard_map/transpose(jvp())/while/body/eval_jaxpr/jit(_solve_triangular)/vmap()/triangular_solve | solution.py:59
  1540.6 29.5 %custom-call.42 = f32[6,1,64,64]{2,3,1,0:T(8,128)S(1)} custom-call(f32[6,1,64,64]{3,2,1,0:T(8,128)S(1)} %fusion.550), custom_call_target="InvertDiagBlocksLowerTriangular" | custom-call | tf_op jit(solution)/shard_map/transpose(jvp())/while/body/eval_jaxpr/jit(_solve_triangular)/vmap()/triangular_solve | solution.py:59
  1663.7 162.6 %reduce-scatter.8.cloned.1.call-done = bf16[128,4608]{1,0:T(8,128)(2,1)} async-done(((bf16[1024,4608]{1,0:T(8,128)(2,1)}), bf16[128,4608]{1,0:T(8,128)(2,1)}) %reduce-scatter.8.cloned.1.call-update) | async-done | bytes 1179664 | tf_op jit(solution)/shard_map/reduce_scatter | solution.py:254
  1826.3 195.5 %reduce-scatter.12.cloned.1.call-done = bf16[128,5632]{1,0:T(8,128)(2,1)} async-done(((bf16[1024,5632]{1,0:T(8,128)(2,1)}), bf16[128,5632]{1,0:T(8,128)(2,1)}) %reduce-scatter.12.cloned.1.call-update) | async-done | bytes 1441808 | tf_op jit(solution)/shard_map/reduce_scatter | solution.py:263
  2030.4 40.6 %all-reduce.18 = (f32[]{:T(128)}, f32[1024]{0:T(1024)}, f32[1024]{0:T(1024)}, f32[256]{0:T(256)}, f32[4,3072]{1,0:T(4,128)}, /*index=5*/f32[6]{0:T(128)}, f32[6]{0:T(128)}) all-reduce(f32[]{:T(128)} %multiply_reduce_fusion.14, f32[1024]{0:T(1024)S(1)} %get-tuple-element.2889, ...), channel_id=1, replica_groups=mesh['dp'=4,'seq'=8] {'dp','seq'}, use_global_device_ids=true, to_apply=%region_15.16 | all-reduce | flops 14605 | bytes 116840 | tf_op jit(solution)/shard_map/psum | solution.py:200
  2093.2 73.0 %all-reduce.22.cloned.1.call-done = (bf16[128,4608]{1,0:T(8,128)(2,1)}, bf16[128,1536]{1,0:T(8,128)(2,1)}, bf16[128,5632]{1,0:T(8,128)(2,1)}, bf16[128,2816]{1,0:T(8,128)(2,1)}) async-done(((bf16[128,4608]{1,0:T(8,128)(2,1)}, bf16[128,1536]{1,0:T(8,128)(2,1)}, bf16[128,5632]{1,0:T(8,128)(2,1)}, bf16[128,2816]{1,0:T(8,128)(2,1)}), (bf16[128,4608]{1,0:T(8,128)(2,1)}, bf16[128,1536]{1,0:T(8,128)(2,1)}, ...) | async-done | bytes 3735568 | tf_op jit(solution)/shard_map/psum | solution.py:271
  (1055 shorter events, 973.3 us)
Async XLA Ops:
  7.2 145.3 %all-gather.5.cloned.1.call-start = ((), (), s32[]{:S(2)}) async-start(), calls=%async_computation.5 | async-start | bytes 10616832 | tf_op jit(solution)/shard_map/all_gather | solution.py:153
  8.0 817.1 %all-gather.7.cloned.1.call-start = ((), (), s32[]{:S(2)}) async-start(), calls=%async_computation.6 | async-start | bytes 3538944 | tf_op jit(solution)/shard_map/all_gather | solution.py:185
  8.7 820.5 %all-gather.9.cloned.1.call-start = ((), (), s32[]{:S(2)}) async-start(), calls=%async_computation.7 | async-start | bytes 12976128 | tf_op jit(solution)/shard_map/all_gather | solution.py:186
  9.5 831.4 %all-gather.11.cloned.1.call-start = ((), (), s32[]{:S(2)}) async-start(), calls=%async_computation.8 | async-start | bytes 6488064 | tf_op jit(solution)/shard_map/all_gather | solution.py:187
  10.1 1653.6 %reduce-scatter.10.cloned.1.call-start = ((), (), s32[]{:S(2)}) async-start(), calls=%async_computation.10 | async-start | bytes 3538944 | tf_op jit(solution)/shard_map/reduce_scatter | solution.py:260
  10.1 150.4 %copy-start.97 = (f32[1,256]{1,0:T(1,128)}, f32[1,256]{1,0:T(1,128)S(1)}, u32[]{:S(2)}) copy-start(f32[1,256]{1,0:T(1,128)S(1)} %convert_element_type.189) | copy-start | bytes 3076
  40.2 127.2 %copy-start.62 = (f32[1,3072]{1,0:T(1,128)}, f32[1,3072]{1,0:T(1,128)S(1)}, u32[]{:S(2)}) copy-start(f32[1,3072]{1,0:T(1,128)S(1)} %get-tuple-element.3190) | copy-start | bytes 36868
  40.2 127.2 %copy-start.64 = (f32[1,3072]{1,0:T(1,128)}, f32[1,3072]{1,0:T(1,128)S(1)}, u32[]{:S(2)}) copy-start(f32[1,3072]{1,0:T(1,128)S(1)} %get-tuple-element.3191) | copy-start | bytes 36868
  40.2 127.2 %copy-start.66 = (f32[1,3072]{1,0:T(1,128)}, f32[1,3072]{1,0:T(1,128)S(1)}, u32[]{:S(2)}) copy-start(f32[1,3072]{1,0:T(1,128)S(1)} %get-tuple-element.3192) | copy-start | bytes 36868
  162.0 4.9 collective-permute-start.2
  371.8 25.3 %collective-permute-start = (f32[6,128,256]{2,1,0:T(8,128)}, f32[6,128,256]{2,1,0:T(8,128)S(1)}, u32[]{:S(2)}, u32[]{:S(2)}) collective-permute-start(f32[6,128,256]{2,1,0:T(8,128)} %convolution_add_fusion.32), channel_id=1, source_target_pairs={{0,1},{1,2},{2,3},{3,4},{4,5},{5,6},{6,7},{8,9},{9,10},{10,11},{11... | collective-permute-start | bytes 2359304 | tf_op jit(solution)/shard_map/while/body/eval_jaxpr/ppermute | solution.py:23
  400.0 15.9 collective-permute-start
  418.9 52.5 %collective-permute-start = (f32[6,128,256]{2,1,0:T(8,128)}, f32[6,128,256]{2,1,0:T(8,128)S(1)}, u32[]{:S(2)}, u32[]{:S(2)}) collective-permute-start(f32[6,128,256]{2,1,0:T(8,128)} %convolution_add_fusion.32), channel_id=1, source_target_pairs={{0,1},{1,2},{2,3},{3,4},{4,5},{5,6},{6,7},{8,9},{9,10},{10,11},{11... | collective-permute-start | bytes 2359304 | tf_op jit(solution)/shard_map/while/body/eval_jaxpr/ppermute | solution.py:23
  474.3 24.6 %collective-permute-start = (f32[6,128,256]{2,1,0:T(8,128)}, f32[6,128,256]{2,1,0:T(8,128)S(1)}, u32[]{:S(2)}, u32[]{:S(2)}) collective-permute-start(f32[6,128,256]{2,1,0:T(8,128)} %convolution_add_fusion.32), channel_id=1, source_target_pairs={{0,1},{1,2},{2,3},{3,4},{4,5},{5,6},{6,7},{8,9},{9,10},{10,11},{11... | collective-permute-start | bytes 2359304 | tf_op jit(solution)/shard_map/while/body/eval_jaxpr/ppermute | solution.py:23
  501.8 29.0 %collective-permute-start = (f32[6,128,256]{2,1,0:T(8,128)}, f32[6,128,256]{2,1,0:T(8,128)S(1)}, u32[]{:S(2)}, u32[]{:S(2)}) collective-permute-start(f32[6,128,256]{2,1,0:T(8,128)} %convolution_add_fusion.32), channel_id=1, source_target_pairs={{0,1},{1,2},{2,3},{3,4},{4,5},{5,6},{6,7},{8,9},{9,10},{10,11},{11... | collective-permute-start | bytes 2359304 | tf_op jit(solution)/shard_map/while/body/eval_jaxpr/ppermute | solution.py:23
  533.7 17.0 collective-permute-start
  553.6 27.9 %collective-permute-start = (f32[6,128,256]{2,1,0:T(8,128)}, f32[6,128,256]{2,1,0:T(8,128)S(1)}, u32[]{:S(2)}, u32[]{:S(2)}) collective-permute-start(f32[6,128,256]{2,1,0:T(8,128)} %convolution_add_fusion.32), channel_id=1, source_target_pairs={{0,1},{1,2},{2,3},{3,4},{4,5},{5,6},{6,7},{8,9},{9,10},{10,11},{11... | collective-permute-start | bytes 2359304 | tf_op jit(solution)/shard_map/while/body/eval_jaxpr/ppermute | solution.py:23
  893.8 769.9 %reduce-scatter.14.cloned.1.call-start = ((), (), s32[]{:S(2)}) async-start(), calls=%async_computation.12 | async-start | bytes 6488064 | tf_op jit(solution)/shard_map/reduce_scatter | solution.py:266
  1151.8 674.4 %reduce-scatter.8.cloned.1.call-start = ((), (), s32[]{:S(2)}) async-start(), calls=%async_computation.9 | async-start | bytes 10616832 | tf_op jit(solution)/shard_map/reduce_scatter | solution.py:254
  1154.6 27.8 %collective-permute-start.1 = (f32[6,128,256]{2,1,0:T(8,128)}, f32[6,128,256]{2,1,0:T(8,128)S(1)}, u32[]{:S(2)}, u32[]{:S(2)}) collective-permute-start(f32[6,128,256]{2,1,0:T(8,128)} %convolution_add_fusion.33), channel_id=1, source_target_pairs={{1,0},{2,1},{3,2},{4,3},{5,4},{6,5},{7,6},{9,8},{10,9},{11,10},{12... | collective-permute-start | bytes 2359304 | tf_op jit(solution)/shard_map/while/body/eval_jaxpr/ppermute | solution.py:23
  1184.2 30.2 %collective-permute-start.1 = (f32[6,128,256]{2,1,0:T(8,128)}, f32[6,128,256]{2,1,0:T(8,128)S(1)}, u32[]{:S(2)}, u32[]{:S(2)}) collective-permute-start(f32[6,128,256]{2,1,0:T(8,128)} %convolution_add_fusion.33), channel_id=1, source_target_pairs={{1,0},{2,1},{3,2},{4,3},{5,4},{6,5},{7,6},{9,8},{10,9},{11,10},{12... | collective-permute-start | bytes 2359304 | tf_op jit(solution)/shard_map/while/body/eval_jaxpr/ppermute | solution.py:23
  1216.0 37.7 %collective-permute-start.1 = (f32[6,128,256]{2,1,0:T(8,128)}, f32[6,128,256]{2,1,0:T(8,128)S(1)}, u32[]{:S(2)}, u32[]{:S(2)}) collective-permute-start(f32[6,128,256]{2,1,0:T(8,128)} %convolution_add_fusion.33), channel_id=1, source_target_pairs={{1,0},{2,1},{3,2},{4,3},{5,4},{6,5},{7,6},{9,8},{10,9},{11,10},{12... | collective-permute-start | bytes 2359304 | tf_op jit(solution)/shard_map/while/body/eval_jaxpr/ppermute | solution.py:23
  1255.4 17.2 collective-permute-start.1
  1274.3 14.1 collective-permute-start.1
  1290.0 18.5 collective-permute-start.1
  1310.2 21.6 collective-permute-start.1
  1618.1 25.5 %collective-permute-start.3 = (bf16[3,3072]{1,0:T(4,128)(2,1)S(1)}, bf16[3,3072]{1,0:T(4,128)(2,1)S(1)}, u32[]{:S(2)}, u32[]{:S(2)}) collective-permute-start(bf16[3,3072]{1,0:T(4,128)(2,1)S(1)} %slice.195), channel_id=1, source_target_pairs={{1,0},{2,1},{3,2},{4,3},{5,4},{6,5},{7,6},{9,8},{10,9},{11,10},{12... | collective-permute-start | bytes 55304 | tf_op jit(solution)/shard_map/ppermute | solution.py:23
  1650.6 371.1 %reduce-scatter.12.cloned.1.call-start = ((), (), s32[]{:S(2)}) async-start(), calls=%async_computation.11 | async-start | bytes 12976128 | tf_op jit(solution)/shard_map/reduce_scatter | solution.py:263
  1660.9 425.2 %reduce-scatter.16.cloned.1.call-start = ((), (), s32[]{:S(2)}) async-start(), calls=%async_computation.13 | async-start | bytes 294912
  1663.2 358.5 %copy-start.98 = (f32[1,256]{1,0:T(1,128)S(1)}, f32[1,256]{1,0:T(1,128)}, u32[]{:S(2)}) copy-start(f32[1,256]{1,0:T(1,128)} %copy-done.97) | copy-start | bytes 3076
  1663.2 358.5 %copy-start.101 = (f32[256]{0:T(256)S(1)}, f32[256]{0:T(256)}, u32[]{:S(2)}) copy-start(f32[256]{0:T(256)} %get-tuple-element.3188) | copy-start | bytes 3076
  1663.6 502.6 %all-reduce.22.cloned.1.call-start = ((), (), s32[]{:S(2)}) async-start(), calls=%async_computation.14 | async-start | bytes 7471104 | tf_op jit(solution)/shard_map/psum | solution.py:271
  (169 other events, 1761.4 us)
Sparse Core Ops, SparseCore 0:
  10.3 142.1 all-gather.4
  154.7 59.2 all-gather.6
  216.2 162.5 all-gather.8
  380.8 123.0 all-gather.10
  893.9 82.9 reduce-scatter.9
  1151.9 218.0 reduce-scatter.13
  1650.7 175.5 reduce-scatter.7
  1829.8 191.8 reduce-scatter.11
  2025.6 60.4 reduce-scatter.15
  2088.5 77.5 all-reduce.21
where the time goes:
time: 2190 us; the launch traced here: 2180 us
  waiting for transfers between devices  823 us (38%)
  other arithmetic  617 us (28%)
  matrix products  370 us (17%)
  local copies, waits for them, and re-layouts  155 us (7%)
  blocking collectives  115 us (5%)
  starting transfers between devices  80.4 us (4%)
    another operation x52, other arithmetic, block_step(): jax.scipy.linalg.solve_triangular(system, wanted, lower=True, unit_diagon...  368 us
    ppermute x16, waiting for transfers between devices, shifted(): lax.ppermute(value, axis, [(source, source + steps) for source in range(l...  307 us
    reduce_scatter x1, waiting for transfers between devices, on_device(): lax.psum_scatter(grad_ffn_in.astype(jnp.bfloat16), 'seq', scatter_dimensi...  195 us
    reduce_scatter x1, waiting for transfers between devices, on_device(): lax.psum_scatter(grad_in_weight.astype(jnp.bfloat16), 'seq', scatter_dime...  163 us
    another operation x16, other arithmetic, block_map(): jax.scipy.linalg.solve_triangular(system, wanted, lower=True, unit_diagon...  118 us
    psum x2, blocking collectives, on_device(): lax.psum((jnp.sum(mask_row * jnp.mean(errors * errors, axis=-1)), jnp.sum...  80.8 us
    ppermute x16, starting transfers between devices, shifted(): lax.ppermute(value, axis, [(source, source + steps) for source in range(l...  80 us
    psum x1, waiting for transfers between devices, on_device(): lax.psum(stored[0].astype(jnp.bfloat16), 'dp').astype(jnp.float32)  73 us
  transfers between devices with their start and end apart: 26, of which 20 were waited for; matrix products, arithmetic and copies ran while one was open for 49% of the time, Pallas kernels for 0%

commit v1 on v0

--- a/solution.py
+++ b/solution.py
@@ -1,6 +1,10 @@
+import functools
+
 import jax
 import jax.numpy as jnp
 from jax import lax
+from jax.experimental import pallas as pl
+from jax.experimental.pallas import tpu as pltpu
 from jax.sharding import PartitionSpec as P
 
 HEADS = 6
@@ -33,77 +37,6 @@
 
 def unit_rows(field_in):
     return field_in * lax.rsqrt(jnp.sum(field_in * field_in, axis=-1, keepdims=True) + epsilon)
-
-
-def block_frame(key_rows, strength, forget):
-    block_size = forget.shape[1]
-    cumulative = jnp.cumsum(forget, axis=1)
-    row_ids = lax.broadcasted_iota(jnp.int32, (block_size, block_size), 0)
-    col_ids = lax.broadcasted_iota(jnp.int32, (block_size, block_size), 1)
-    lower_mask = (row_ids >= col_ids).astype(jnp.float32)
-    strict = (row_ids > col_ids).astype(jnp.float32)
-    decays = jnp.exp((cumulative[:, :, None] - cumulative[:, None, :]) * lower_mask) * lower_mask
-    keys_dot = jnp.einsum("hid,hjd->hij", key_rows, key_rows, precision=precise)
-    system = (
-        jnp.eye(block_size, dtype=jnp.float32) + strength[:, :, None] * keys_dot * decays * strict
-    )
-    return (cumulative, decays, system)
-
-
-def block_step(memory, pieces):
-    queries, key_rows, values, strength, forget = pieces
-    cumulative, decays, system = block_frame(key_rows, strength, forget)
-    growth = jnp.exp(cumulative)
-    projected = jnp.einsum("hcd,hdv->hcv", key_rows, memory, precision=precise)
-    wanted = strength[:, :, None] * (values - growth[:, :, None] * projected)
-    update = jax.scipy.linalg.solve_triangular(system, wanted, lower=True, unit_diagonal=True)
-    scores = jnp.einsum("hid,hjd->hij", queries, key_rows, precision=precise) * decays
-    read_out = jnp.einsum("hcd,hdv->hcv", queries, memory, precision=precise)
-    output = growth[:, :, None] * read_out + jnp.einsum(
-        "hij,hjv->hiv", scores, update, precision=precise
-    )
-    final_log = cumulative[:, -1]
-    weights = jnp.exp(final_log[:, None] - cumulative)
-    new_memory = jnp.exp(final_log)[:, None, None] * memory + jnp.einsum(
-        "hcd,hcv->hdv", key_rows * weights[:, :, None], update, precision=precise
-    )
-    return (new_memory, output)
-
-
-def block_map(carry, pieces):
-    mapping, offset = carry
-    key_rows, values, strength, forget = pieces
-    cumulative, decays, system = block_frame(key_rows, strength, forget)
-    growth = jnp.exp(cumulative)
-    final_log = cumulative[:, -1]
-    weights = jnp.exp(final_log[:, None] - cumulative)
-    wanted = jnp.concatenate(
-        [(strength * growth)[:, :, None] * key_rows, strength[:, :, None] * values], axis=2
-    )
-    solved = jax.scipy.linalg.solve_triangular(system, wanted, lower=True, unit_diagonal=True)
-    swept = jnp.einsum("hcd,hce->hde", key_rows * weights[:, :, None], solved, precision=precise)
-    step_map = jnp.exp(final_log)[:, None, None] * jnp.eye(DK, dtype=jnp.float32) - swept[:, :, :DK]
-    new_mapping = jnp.einsum("hde,hef->hdf", step_map, mapping, precision=precise)
-    new_offset = jnp.einsum("hde,hev->hdv", step_map, offset, precision=precise) + swept[:, :, DK:]
-    return ((new_mapping, new_offset), None)
-
-
-def to_blocks(field_in):
-    blocks = field_in.shape[0] // BLOCK
-    return jnp.swapaxes(field_in.reshape((blocks, BLOCK) + field_in.shape[1:]), 1, 2)
-
-
-def run_blocks(entering, queries, key_rows, values, strength, forget):
-    length = queries.shape[0]
-    pieces = (
-        to_blocks(queries),
-        to_blocks(key_rows),
-        to_blocks(values),
-        to_blocks(strength),
-        to_blocks(forget),
-    )
-    leaving, outputs = lax.scan(block_step, entering, pieces)
-    return (jnp.swapaxes(outputs, 1, 2).reshape(length, HEADS, DV), leaving)
 
 
 def prepare(padded, little, conv_weight, decay_log, decay_bias):
@@ -129,6 +62,299 @@
 
 def swiglu(gate_up):
     return jax.nn.silu(gate_up[:, :FF]) * gate_up[:, FF:]
+
+
+MESH = pl.DeviceIdType.MESH
+NN = (((1,), (0,)), ((), ()))
+NT = (((1,), (1,)), ((), ()))
+TN = (((0,), (0,)), ((), ()))
+
+
+def exact(left, right, dims=NN):
+    return lax.dot_general(
+        left, right, dims, precision=precise, preferred_element_type=jnp.float32
+    )
+
+
+def iotas(rows, columns):
+    return (
+        lax.broadcasted_iota(jnp.int32, (rows, columns), 0),
+        lax.broadcasted_iota(jnp.int32, (rows, columns), 1),
+    )
+
+
+def lower_inverse(system):
+    size = system.shape[0]
+    row, col = iotas(size, size)
+    inverse = (row == col).astype(jnp.float32) - jnp.where(row // 2 == col // 2, system, 0.0)
+    width = 2
+    while width < size:
+        joined = (row // (2 * width) == col // (2 * width)) & (row // width != col // width)
+        inverse = inverse - exact(inverse, exact(jnp.where(joined, system, 0.0), inverse))
+        width *= 2
+    return inverse
+
+
+def decay_table(gcol, grow):
+    size = gcol.shape[0]
+    row, col = iotas(size, size)
+    keep = row >= col
+    return jnp.where(keep, jnp.exp(jnp.where(keep, gcol - grow, 0.0)), 0.0)
+
+
+def local_kernel(q_ref, k_ref, v_ref, cols_ref, rows_ref, t_ref, u_ref, w_ref, m_ref, b_ref, o_ref, e_ref):
+    queries, keys, values = q_ref[0], k_ref[0], v_ref[0]
+    cols = cols_ref[0, 0]
+    gcol, beta = cols[:, 0:1], cols[:, 1:2]
+    grow = rows_ref[0, 0][0:1, :]
+    size = keys.shape[0]
+    half = size // 2
+    decays = decay_table(gcol, grow)
+    row, col = iotas(size, size)
+    system = jnp.where(row > col, beta * exact(keys, keys, NT) * decays, 0.0)
+    first = lower_inverse(system[:half, :half])
+    second = lower_inverse(system[half:, half:])
+    corner = -exact(second, exact(system[half:, :half], first))
+    t_ref[0, 0, :half, :half] = first
+    t_ref[0, 0, :half, half:] = jnp.zeros((half, half), jnp.float32)
+    t_ref[0, 0, half:, :half] = corner
+    t_ref[0, 0, half:, half:] = second
+    solve = t_ref[0, 0]
+    growth = jnp.exp(gcol)
+    last = gcol[size - 1 :, :]
+    weights = jnp.exp(last - gcol)
+    update = exact(solve, beta * values)
+    back = exact(solve, (beta * growth) * keys)
+    scores = exact(queries, keys, NT) * decays
+    weighted = keys * weights
+    drow, dcol = iotas(DK, DK)
+    u_ref[0, 0] = update
+    w_ref[0, 0] = back
+    m_ref[0, 0] = jnp.where(drow == dcol, jnp.exp(last), 0.0) - exact(weighted, back, TN)
+    b_ref[0, 0] = exact(weighted, update, TN)
+    o_ref[0, 0] = exact(scores, update)
+    e_ref[0, 0] = growth * queries - exact(scores, back)
+
+
+def per_unit(*shape):
+    return pl.BlockSpec((1, 1) + shape, lambda j, h: (j, h) + (0,) * len(shape))
+
+
+def per_head(length, width):
+    return pl.BlockSpec((1, length, width), lambda j, h: (j, 0, h))
+
+
+def delta_local(queries, keys, values, cols, rows):
+    seqs, length = queries.shape[:2]
+    heads = cols.shape[1]
+
+    def out(*shape):
+        return jax.ShapeDtypeStruct((seqs, heads) + shape, jnp.float32)
+
+    return pl.pallas_call(
+        local_kernel,
+        grid=(seqs, heads),
+        in_specs=[
+            per_head(length, DK),
+            per_head(length, DK),
+            per_head(length, DV),
+            per_unit(length, 8),
+            per_unit(8, length),
+        ],
+        out_specs=[
+            per_unit(length, length),
+            per_unit(length, DV),
+            per_unit(length, DK),
+            per_unit(DK, DK),
+            per_unit(DK, DV),
+            per_unit(length, DV),
+            per_unit(length, DK),
+        ],
+        out_shape=[
+            out(length, length),
+            out(length, DV),
+            out(length, DK),
+            out(DK, DK),
+            out(DK, DV),
+            out(length, DV),
+            out(length, DK),
+        ],
+        compiler_params=pltpu.CompilerParams(vmem_limit_bytes=48 * 2**20),
+        name="delta_local",
+    )(queries, keys, values, cols, rows)
+
+
+def grads_kernel(
+    q_ref, k_ref, v_ref, cols_ref, rows_ref, t_ref, u_ref, w_ref, s_ref, do_ref, ds_ref,
+    dq_ref, dk_ref, dv_ref, dcols_ref, drows_ref,
+):
+    queries, keys, values = q_ref[0], k_ref[0], v_ref[0]
+    cols = cols_ref[0, 0]
+    gcol, beta = cols[:, 0:1], cols[:, 1:2]
+    grow = rows_ref[0, 0][0:1, :]
+    size = keys.shape[0]
+    decays = decay_table(gcol, grow)
+    row, col = iotas(size, size)
+    strict = row > col
+    memory, after = s_ref[0, 0], ds_ref[0, 0]
+    grad_out = do_ref[0]
+    growth = jnp.exp(gcol)
+    last = gcol[size - 1 :, :]
+    weights = jnp.exp(last - gcol)
+    update = u_ref[0, 0] - exact(w_ref[0, 0], memory)
+    scores = exact(queries, keys, NT) * decays
+    keys_dot = jnp.where(strict, exact(keys, keys, NT) * decays, 0.0)
+    grad_update = exact(scores, grad_out, TN) + exact(keys * weights, after)
+    grad_wanted = exact(t_ref[0, 0], grad_update, TN)
+    grad_system = -exact(grad_wanted, update, NT)
+    grad_scores = exact(grad_out, update, NT)
+    through = keys_dot * grad_system
+    total = grad_scores * scores + beta * through
+    query_part = growth * exact(grad_out, memory, NT)
+    key_read = growth * exact(grad_wanted, memory, NT)
+    key_part = beta * key_read
+    end_part = weights * exact(update, after, NT)
+    grad_dot = grad_scores * decays
+    grad_keys_dot = jnp.where(strict, grad_system * decays, 0.0) * beta
+    dq_ref[0] = query_part + exact(grad_dot, keys)
+    dk_ref[0] = (
+        end_part - key_part + exact(grad_dot, queries, TN)
+        + exact(grad_keys_dot, keys) + exact(grad_keys_dot, keys, TN)
+    )
+    dv_ref[0] = beta * grad_wanted
+    key_line = jnp.sum(keys * key_part, axis=1, keepdims=True)
+    end_line = jnp.sum(keys * end_part, axis=1, keepdims=True)
+    grad_beta = (
+        jnp.sum(grad_wanted * values, axis=1, keepdims=True)
+        - jnp.sum(keys * key_read, axis=1, keepdims=True)
+        + jnp.sum(through, axis=1, keepdims=True)
+    )
+    grad_log = (
+        jnp.sum(queries * query_part, axis=1, keepdims=True)
+        - key_line
+        - end_line
+        + jnp.sum(total, axis=1, keepdims=True)
+    )
+    grad_last = jnp.sum(end_line) + jnp.sum(jnp.exp(last) * jnp.sum(memory * after, axis=1, keepdims=True))
+    line = lax.broadcasted_iota(jnp.int32, (size, 1), 0)
+    grad_log = grad_log + jnp.where(line == size - 1, grad_last, 0.0)
+    lane = lax.broadcasted_iota(jnp.int32, (size, 8), 1)
+    dcols_ref[0, 0] = jnp.where(lane == 0, grad_log, jnp.where(lane == 1, grad_beta, 0.0))
+    drows_ref[0, 0] = jnp.broadcast_to(jnp.sum(total, axis=0, keepdims=True), (8, size))
+
+
+def delta_grads(queries, keys, values, cols, rows, solve, update, back, entering, grad_out, after):
+    seqs, length = queries.shape[:2]
+    heads = cols.shape[1]
+    return pl.pallas_call(
+        grads_kernel,
+        grid=(seqs, heads),
+        in_specs=[
+            per_head(length, DK),
+            per_head(length, DK),
+            per_head(length, DV),
+            per_unit(length, 8),
+            per_unit(8, length),
+            per_unit(length, length),
+            per_unit(length, DV),
+            per_unit(length, DK),
+            per_unit(DK, DV),
+            per_head(length, DV),
+            per_unit(DK, DV),
+        ],
+        out_specs=[
+            per_head(length, DK),
+            per_head(length, DK),
+            per_head(length, DV),
+            per_unit(length, 8),
+            per_unit(8, length),
+        ],
+        out_shape=[
+            jax.ShapeDtypeStruct(queries.shape, jnp.float32),
+            jax.ShapeDtypeStruct(keys.shape, jnp.float32),
+            jax.ShapeDtypeStruct(values.shape, jnp.float32),
+            jax.ShapeDtypeStruct(cols.shape, jnp.float32),
+            jax.ShapeDtypeStruct(rows.shape, jnp.float32),
+        ],
+        compiler_params=pltpu.CompilerParams(vmem_limit_bytes=48 * 2**20),
+        name="delta_grads",
+    )(queries, keys, values, cols, rows, solve, update, back, entering, grad_out, after)
+
+
+def relay_kernel(count, ahead, m_ref, b_ref, s_ref, sending, arriving, send_sem, recv_sem):
+    place, group = lax.axis_index("seq"), lax.axis_index("dp")
+    units = m_ref.shape[0]
+    if ahead:
+        is_first, is_last = place == 0, place == count - 1
+        before, beyond = lax.rem(place + count - 1, count), lax.rem(place + 1, count)
+    else:
+        is_first, is_last = place == count - 1, place == 0
+        before, beyond = lax.rem(place + 1, count), lax.rem(place + count - 1, count)
+    barrier = pltpu.get_barrier_semaphore()
+
+    @pl.when(jnp.logical_not(is_first))
+    def _():
+        pl.semaphore_signal(barrier, inc=1, device_id=(group, before), device_id_type=MESH)
+
+    @pl.when(jnp.logical_not(is_last))
+    def _():
+        pl.semaphore_wait(barrier, 1)
+
+    def copy_of(unit):
+        return pltpu.make_async_remote_copy(
+            src_ref=sending.at[unit],
+            dst_ref=arriving.at[unit],
+            send_sem=send_sem.at[unit],
+            recv_sem=recv_sem.at[unit],
+            device_id=(group, beyond),
+            device_id_type=MESH,
+        )
+
+    for unit in range(units):
+
+        @pl.when(is_first)
+        def _():
+            s_ref[unit] = jnp.zeros_like(s_ref[unit])
+
+        @pl.when(jnp.logical_not(is_first))
+        def _():
+            copy_of(unit).wait_recv()
+            s_ref[unit] = arriving[unit].astype(jnp.float32)
+
+        @pl.when(jnp.logical_not(is_last))
+        def _():
+            step = exact(m_ref[unit], s_ref[unit], NN if ahead else TN) + b_ref[unit]
+            sending[unit] = step.astype(jnp.bfloat16)
+            copy_of(unit).start()
+
+    @pl.when(jnp.logical_not(is_last))
+    def _():
+        for unit in range(units):
+            copy_of(unit).wait_send()
+
+
+def relay(mapping, offset, ahead):
+    count = lax.axis_size("seq")
+    seqs, heads = mapping.shape[:2]
+    units = seqs * heads
+    whole = pl.BlockSpec(memory_space=pltpu.VMEM)
+    found = pl.pallas_call(
+        functools.partial(relay_kernel, count, ahead),
+        out_shape=jax.ShapeDtypeStruct((units, DK, DV), jnp.float32),
+        in_specs=[whole, whole],
+        out_specs=whole,
+        scratch_shapes=[
+            pltpu.VMEM((units, DK, DV), jnp.bfloat16),
+            pltpu.VMEM((units, DK, DV), jnp.bfloat16),
+            pltpu.SemaphoreType.DMA((units,)),
+            pltpu.SemaphoreType.DMA((units,)),
+        ],
+        compiler_params=pltpu.CompilerParams(
+            collective_id=1 if ahead else 2, has_side_effects=True, vmem_limit_bytes=48 * 2**20
+        ),
+        name="relay_ahead" if ahead else "relay_back",
+    )(mapping.reshape(units, DK, DK), offset.reshape(units, DK, DV))
+    return found.reshape(seqs, heads, DK, DV)
 
 
 def on_device(
@@ -163,21 +389,19 @@
     padded = jnp.concatenate([rim_rows, mixed_in], axis=0).astype(jnp.float32)
     prepared, local_pull = jax.vjp(prepare, padded, little, conv_weight, decay_log, decay_bias)
     queries, key_rows, values, strength, forget = prepared
-    eye_stack = jnp.broadcast_to(jnp.eye(DK, dtype=jnp.float32), (HEADS, DK, DK))
-    zero_state = jnp.zeros((HEADS, DK, DV), jnp.float32)
-    (mapping, offset), unused = lax.scan(
-        block_map,
-        (eye_stack, zero_state),
-        (to_blocks(key_rows), to_blocks(values), to_blocks(strength), to_blocks(forget)),
-    )
-
-    def relay_step(turn_index, incoming):
-        outgoing = jnp.einsum("hde,hev->hdv", mapping, incoming, precision=precise) + offset
-        return shifted(outgoing, "seq", 1)
-
-    entering = lax.fori_loop(0, lax.axis_size("seq") - 1, relay_step, zero_state)
-    (mixed_out, leaving), delta_pull = jax.vjp(
-        run_blocks, entering, queries, key_rows, values, strength, forget
+    cumulative = jnp.cumsum(forget, axis=0).T
+    strength_t = strength.T
+    cols = jnp.stack([cumulative, strength_t] + [jnp.zeros_like(cumulative)] * 6, axis=-1)[None]
+    rows = jnp.stack([cumulative] * 8, axis=1)[None]
+    flat_q, flat_k = queries.reshape(1, length, KEYS), key_rows.reshape(1, length, KEYS)
+    flat_v = values.reshape(1, length, VALUES)
+    solve, update, back, mapping, offset, own_out, reach = delta_local(
+        flat_q, flat_k, flat_v, cols, rows
+    )
+    entering = relay(mapping, offset, True)
+    mixed_out = jnp.transpose(
+        own_out[0] + jnp.einsum("htk,hkv->htv", reach[0], entering[0], precision=precise),
+        (1, 0, 2),
     )
     branch_f, gated_pull = jax.vjp(gated_norm, mixed_out, gate_pre, gain_out)
     branch = branch_f.astype(jnp.bfloat16)
@@ -216,21 +440,20 @@
     grad_out_weight = jnp.einsum("td,tv->dv", grad_attn, branch, preferred_element_type=jnp.float32)
     grad_branch = jnp.dot(grad_attn, w_out, preferred_element_type=jnp.float32)
     grad_mixed, grad_gate_pre, grad_gain_out = gated_pull(grad_branch)
-    first_terms = delta_pull((grad_mixed, jnp.zeros_like(leaving)))
-    mapping_t = jnp.swapaxes(mapping, 1, 2)
-
-    def relay_back(turn_index, arriving):
-        going = jnp.einsum("hde,hev->hdv", mapping_t, arriving, precision=precise) + first_terms[0]
-        return shifted(going, "seq", -1)
-
-    grad_leaving = lax.fori_loop(0, lax.axis_size("seq") - 1, relay_back, zero_state)
-    later_terms = delta_pull((jnp.zeros_like(mixed_out), grad_leaving))
+    returning = jnp.einsum("htk,thv->hkv", reach[0], grad_mixed, precision=precise)[None]
+    after = relay(mapping, returning, False)
+    grad_q, grad_k, grad_v, grad_cols, grad_rows = delta_grads(
+        flat_q, flat_k, flat_v, cols, rows, solve, update, back, entering,
+        grad_mixed.reshape(1, length, VALUES), after,
+    )
+    grad_log = grad_cols[0, :, :, 0] - grad_rows[0, :, 0, :]
+    grad_forget = lax.cumsum(grad_log, axis=1, reverse=True).T
     grad_prepared = (
-        first_terms[1] + later_terms[1],
-        first_terms[2] + later_terms[2],
-        first_terms[3] + later_terms[3],
-        first_terms[4] + later_terms[4],
-        first_terms[5] + later_terms[5],
+        grad_q.reshape(length, HEADS, DK),
+        grad_k.reshape(length, HEADS, DK),
+        grad_v.reshape(length, HEADS, DV),
+        grad_cols[0, :, :, 1].T,
+        grad_forget,
     )
     grad_padded, grad_little, grad_conv, grad_decay_log, grad_decay_bias = local_pull(grad_prepared)
     rim_grad = shifted(grad_padded[: CONV - 1].astype(jnp.bfloat16), "seq", -1).astype(jnp.float32)

time: 2190 us -> 1230 us (0.56)
  other arithmetic: 617 us -> 57.3 us
  matrix products: 370 us -> 81.2 us
  Pallas kernels: 0 us -> 135 us
  local copies, waits for them, and re-layouts: 155 us -> 60 us
  starting transfers between devices: 80.4 us -> 4.71 us
  waiting for transfers between devices: 823 us -> 752 us
    another operation x107 -> x6, other arithmetic: 503 us -> 11.8 us  [the longest x52 368 us: block_step(): jax.scipy.linalg.solve_triangular(system, wanted, lower=True, unit_diagon...]
    ppermute x16 -> x2, waiting for transfers between devices: 307 us -> 1.56 us  [shifted(): lax.ppermute(value, axis, [(source, source + steps) for source in range(l...]
    dot_general x158 -> x2, matrix products: 256 us -> 4.45 us  [the longest x1 2.87 us: on_device(): jnp.einsum('htk,thv->hkv', reach[0], grad_mixed, precision=precise)[None]]
    pallas_call x0 -> x4, Pallas kernels: none -> 135 us  [the longest x2 57 us: relay(): pl.pallas_call(functools.partial(relay_kernel, count, ahead), out_shape=j...]
    all_gather x1, waiting for transfers between devices: 0.02 us -> 129 us  [on_device(): lax.all_gather(ffn_in, 'seq', axis=0, tiled=True)]
    all_gather x1, waiting for transfers between devices: 0.01 us -> 81.7 us  [on_device(): lax.all_gather(ffn_out, 'seq', axis=0, tiled=True)]
    ppermute x16 -> x2, starting transfers between devices: 80 us -> 4.14 us  [shifted(): lax.ppermute(value, axis, [(source, source + steps) for source in range(l...]
    another operation x24 -> x0, matrix products: 37.6 us -> none  [the longest x20 34.9 us: block_step(): jax.scipy.linalg.solve_triangular(system, wanted, lower=True, unit_diagon...]
  transfers between devices with their start and end apart: 26 -> 12, of which waited for: 20 -> 9; matrix products, arithmetic and copies ran while one was open for 49% -> 12% of each run, Pallas kernels for 0% -> 11%
where the time goes in v1:
time: 1230 us
  waiting for transfers between devices  752 us (61%)
  Pallas kernels  135 us (11%)
  blocking collectives  118 us (10%)
  matrix products  81.2 us (7%)
  local copies, waits for them, and re-layouts  60 us (5%)
  other arithmetic  57.3 us (5%)
  between operations  18 us (1%)
    reduce_scatter x1, waiting for transfers between devices, on_device(): lax.psum_scatter(grad_ffn_in.astype(jnp.bfloat16), 'seq', scatter_dimensi...  195 us
    reduce_scatter x1, waiting for transfers between devices, on_device(): lax.psum_scatter(grad_in_weight.astype(jnp.bfloat16), 'seq', scatter_dime...  167 us
    all_gather x1, waiting for transfers between devices, on_device(): lax.all_gather(ffn_in, 'seq', axis=0, tiled=True)  129 us
    psum x2, blocking collectives, on_device(): lax.psum((jnp.sum(mask_row * jnp.mean(errors * errors, axis=-1)), jnp.sum...  85.9 us
    all_gather x1, waiting for transfers between devices, on_device(): lax.all_gather(ffn_out, 'seq', axis=0, tiled=True)  81.7 us
    psum x1, waiting for transfers between devices, on_device(): lax.psum(stored[0].astype(jnp.bfloat16), 'dp').astype(jnp.float32)  73 us
    all_gather x1, waiting for transfers between devices, on_device(): lax.all_gather(in_weight, 'seq', axis=0, tiled=True)  64.5 us
    pallas_call x2, Pallas kernels, relay(): pl.pallas_call(functools.partial(relay_kernel, count, ahead), out_shape=j...  57 us
  transfers between devices with their start and end apart: 12, of which 9 were waited for; matrix products, arithmetic and copies ran while one was open for 12% of the time, Pallas kernels for 11%

profile of v1, /device:TPU:0, one launch (start us, length us, event | category | flops | bytes accessed | tf_op | source)
XLA Modules:
  0.0 1226.0 jit_solution(354516554202714913)
XLA Ops:
  10.7 45.4 %psum.92 = f32[]{:T(128)} all-reduce(f32[]{:T(128)} %convert_reduce_fusion), channel_id=1, replica_groups=mesh['dp'=4,'seq'=8] {'dp','seq'}, use_global_device_ids=true, to_apply=%region_11.12 | all-reduce | flops 1 | bytes 8 | tf_op jit(solution)/shard_map/psum | solution.py:424
  56.3 26.5 %all_gather.16 = bf16[1024,12]{0,1:T(8,128)(2,1)S(1)} all-gather(bf16[128,12]{0,1:T(8,128)(2,1)S(1)} %copy-done.80), channel_id=1, replica_groups=mesh['dp'=4,'seq'=8] {'seq'}, dimensions={0}, use_global_device_ids=true | all-gather | bytes 27648 | tf_op jit(solution)/shard_map/all_gather | solution.py:380
  87.8 64.5 %all-gather.5.cloned.1.call-done = bf16[1024,4608]{1,0:T(8,128)(2,1)} async-done(((bf16[128,4608]{1,0:T(8,128)(2,1)}), bf16[1024,4608]{1,0:T(8,128)(2,1)}) %all-gather.5.cloned.1.call-update) | async-done | bytes 9437200 | tf_op jit(solution)/shard_map/all_gather | solution.py:379
  152.3 5.3 fusion.67
  163.9 3.2 copy.149
  182.4 44.8 %delta_local.1 = (f32[1,6,256,256]{3,2,1,0:T(8,128)}, f32[1,6,256,256]{3,2,1,0:T(8,128)}, f32[1,6,256,128]{3,2,1,0:T(8,128)S(1)}, f32[1,6,128,128]{3,2,1,0:T(8,1...) custom-call(f32[1,256,768]{2,1,0:T(8,128)S(1)} %get-tuple-element.76.q_ref, ...), custom_call_target="tpu_custom_call" | custom-call | tf_op jit(solution)/shard_map/delta_local/pallas_call | solution.py:154
  227.2 18.4 %relay_ahead.1 = f32[6,128,256]{2,1,0:T(8,128)S(1)} custom-call(f32[6,128,128]{2,1,0:T(8,128)S(1)} %bitcast.161, f32[6,128,256]{2,1,0:T(8,128)S(1)} %bitcast.163), custom_call_target="tpu_custom_call" | custom-call | tf_op jit(solution)/shard_map/relay_ahead/pallas_call | solution.py:341
  252.1 4.3 multiply_reduce_fusion.8
  256.4 129.4 %all-gather.9.cloned.1.call-done = bf16[1024,5632]{1,0:T(8,128)(2,1)} async-done(((bf16[128,5632]{1,0:T(8,128)(2,1)}), bf16[1024,5632]{1,0:T(8,128)(2,1)}) %all-gather.9.cloned.1.call-update) | async-done | bytes 11534352 | tf_op jit(solution)/shard_map/all_gather | solution.py:410
  385.8 6.8 fusion.55
  397.0 81.7 %all-gather.11.cloned.1.call-done = bf16[1024,2816]{1,0:T(8,128)(2,1)} async-done(((bf16[128,2816]{1,0:T(8,128)(2,1)}), bf16[1024,2816]{1,0:T(8,128)(2,1)}) %all-gather.11.cloned.1.call-update) | async-done | bytes 5767184 | tf_op jit(solution)/shard_map/all_gather | solution.py:411
  478.7 6.3 multiply_convert_fusion.3
  485.0 6.7 fusion.29
  493.3 10.1 multiply_reduce_fusion.5
  503.4 3.9 fusion.20
  511.2 5.5 convolution_convert_fusion.2
  516.9 4.7 fusion.32
  524.8 4.5 multiply_reduce_fusion.4
  537.0 38.7 %relay_back.1 = f32[6,128,256]{2,1,0:T(8,128)S(1)} custom-call(f32[6,128,128]{2,1,0:T(8,128)S(1)} %bitcast.162, f32[6,128,256]{2,1,0:T(8,128)S(1)} %fusion.25.b_ref), custom_call_target="tpu_custom_call" | custom-call | tf_op jit(solution)/shard_map/relay_back/pallas_call | solution.py:341
  580.7 32.8 %delta_grads.1 = (f32[1,256,768]{2,1,0:T(8,128)S(1)}, f32[1,256,768]{2,1,0:T(8,128)S(1)}, f32[1,256,1536]{2,1,0:T(8,128)}, f32[1,6,256,8]{3,2,1,0:T(8,128)S(1)}, f32[1,6,8,256]{3,2,1,0:T(8,128)S(1)}) custom-call(f32[1,256,768]{2,1,0:T(8,128)S(1)} %get-tuple-element.76.q_ref, f32[1,256,768]{2,1,0:T(8,128)S(1)} %get-tuple-element.75.k_ref, ...), custom_call_target="tpu_custom_call" | custom-call | tf_op jit(solution)/shard_map/delta_grads/pallas_call | solution.py:249
  632.6 3.9 multiply_reduce_fusion.3
  650.7 5.4 convolution_convert_fusion.1
  657.4 9.0 convolution_convert_fusion
  667.2 7.6 reduce-window.16
  678.0 24.9 %reduce-scatter.14.cloned.1.call-done = bf16[128,2816]{1,0:T(8,128)(2,1)} async-done(((bf16[1024,2816]{1,0:T(8,128)(2,1)}), bf16[128,2816]{1,0:T(8,128)(2,1)}) %reduce-scatter.14.cloned.1.call-update) | async-done | bytes 720912 | tf_op jit(solution)/shard_map/reduce_scatter | solution.py:489
  702.9 166.8 %reduce-scatter.8.cloned.1.call-done = bf16[128,4608]{1,0:T(8,128)(2,1)} async-done(((bf16[1024,4608]{1,0:T(8,128)(2,1)}), bf16[128,4608]{1,0:T(8,128)(2,1)}) %reduce-scatter.8.cloned.1.call-update) | async-done | bytes 1179664 | tf_op jit(solution)/shard_map/reduce_scatter | solution.py:477
  869.8 195.4 %reduce-scatter.12.cloned.1.call-done = bf16[128,5632]{1,0:T(8,128)(2,1)} async-done(((bf16[1024,5632]{1,0:T(8,128)(2,1)}), bf16[128,5632]{1,0:T(8,128)(2,1)}) %reduce-scatter.12.cloned.1.call-update) | async-done | bytes 1441808 | tf_op jit(solution)/shard_map/reduce_scatter | solution.py:486
  1066.0 7.9 fusion.19
  1073.9 40.5 %all-reduce.16 = (f32[]{:T(128)}, f32[1024]{0:T(1024)}, f32[1024]{0:T(1024)}, f32[256]{0:T(256)}, f32[4,3072]{1,0:T(4,128)}, /*index=5*/f32[6]{0:T(128)}, f32[6]{0:T(128)}) all-reduce(f32[]{:T(128)} %multiply_reduce_fusion.13, f32[1024]{0:T(1024)S(1)} %get-tuple-element.46, ...), channel_id=1, replica_groups=mesh['dp'=4,'seq'=8] {'dp','seq'}, use_global_device_ids=true, to_apply=%region_9.10 | all-reduce | flops 14605 | bytes 116840 | tf_op jit(solution)/shard_map/psum | solution.py:424
  1117.6 11.9 reduce-scatter.16.cloned.1.call-done
  1130.4 5.7 psum.94
  1136.6 73.0 %all-reduce.20.cloned.1.call-done = (bf16[128,4608]{1,0:T(8,128)(2,1)}, bf16[128,1536]{1,0:T(8,128)(2,1)}, bf16[128,5632]{1,0:T(8,128)(2,1)}, bf16[128,2816]{1,0:T(8,128)(2,1)}) async-done(((bf16[128,4608]{1,0:T(8,128)(2,1)}, bf16[128,1536]{1,0:T(8,128)(2,1)}, bf16[128,5632]{1,0:T(8,128)(2,1)}, bf16[128,2816]{1,0:T(8,128)(2,1)}), (bf16[128,4608]{1,0:T(8,128)(2,1)}, bf16[128,1536]{1,0:T(8,128)(2,1)}, ...) | async-done | bytes 3735568 | tf_op jit(solution)/shard_map/psum | solution.py:494
  (310 shorter events, 112.5 us)
Async XLA Ops:
  7.2 49.1 %copy-start.80 = (bf16[128,12]{0,1:T(8,128)(2,1)S(1)}, bf16[128,12]{0,1:T(8,128)(2,1)}, u32[]{:S(2)}) copy-start(bf16[128,12]{0,1:T(8,128)(2,1)} %param.18) | copy-start | bytes 9220
  7.2 75.5 %copy-start.27 = (bf16[1,256,1024]{2,1,0:T(8,128)(2,1)S(1)}, bf16[1,256,1024]{2,1,0:T(8,128)(2,1)}, u32[]{:S(2)}) copy-start(bf16[1,256,1024]{2,1,0:T(8,128)(2,1)} %param.14) | copy-start | bytes 1572868
  7.2 75.7 %copy-start.88 = (f32[6]{0:T(128)S(1)}, f32[6]{0:T(128)}, u32[]{:S(2)}) copy-start(f32[6]{0:T(128)} %param.26) | copy-start | bytes 76
  7.2 75.7 %copy-start.47 = (f32[1024]{0:T(1024)S(1)}, f32[1024]{0:T(1024)}, u32[]{:S(2)}) copy-start(f32[1024]{0:T(1024)} %param.22) | copy-start | bytes 12292
  7.2 76.1 %copy-start.83 = (f32[6]{0:T(128)S(1)}, f32[6]{0:T(128)}, u32[]{:S(2)}) copy-start(f32[6]{0:T(128)} %param.27) | copy-start | bytes 76
  7.2 145.1 %all-gather.5.cloned.1.call-start = ((), (), s32[]{:S(2)}) async-start(), calls=%async_computation.5 | async-start | bytes 10616832 | tf_op jit(solution)/shard_map/all_gather | solution.py:379
  8.0 244.1 %all-gather.7.cloned.1.call-start = ((), (), s32[]{:S(2)}) async-start(), calls=%async_computation.6 | async-start | bytes 3538944 | tf_op jit(solution)/shard_map/all_gather | solution.py:409
  8.7 377.1 %all-gather.9.cloned.1.call-start = ((), (), s32[]{:S(2)}) async-start(), calls=%async_computation.7 | async-start | bytes 12976128 | tf_op jit(solution)/shard_map/all_gather | solution.py:410
  9.5 469.3 %all-gather.11.cloned.1.call-start = ((), (), s32[]{:S(2)}) async-start(), calls=%async_computation.8 | async-start | bytes 6488064 | tf_op jit(solution)/shard_map/all_gather | solution.py:411
  10.0 77.7 %copy-start.67 = (f32[4,3072]{1,0:T(4,128)S(1)}, f32[4,3072]{1,0:T(4,128)}, u32[]{:S(2)}) copy-start(f32[4,3072]{1,0:T(4,128)} %param.25) | copy-start | bytes 147460
  10.1 667.9 %reduce-scatter.10.cloned.1.call-start = ((), (), s32[]{:S(2)}) async-start(), calls=%async_computation.10 | async-start | bytes 3538944 | tf_op jit(solution)/shard_map/reduce_scatter | solution.py:483
  56.1 104.2 %copy-start.74 = (f32[1,256]{1,0:T(1,128)}, f32[1,256]{1,0:T(1,128)S(1)}, u32[]{:S(2)}) copy-start(f32[1,256]{1,0:T(1,128)S(1)} %convert_element_type.108) | copy-start | bytes 3076
  83.0 74.6 %copy-start.70 = (f32[256]{0:T(256)}, f32[256]{0:T(256)S(1)}, u32[]{:S(2)}) copy-start(f32[256]{0:T(256)S(1)} %fusion.47) | copy-start | bytes 3076
  87.8 79.8 %copy-start.51 = (f32[1,3072]{1,0:T(1,128)}, f32[1,3072]{1,0:T(1,128)S(1)}, u32[]{:S(2)}) copy-start(f32[1,3072]{1,0:T(1,128)S(1)} %get-tuple-element.82) | copy-start | bytes 36868
  87.8 79.8 %copy-start.53 = (f32[1,3072]{1,0:T(1,128)}, f32[1,3072]{1,0:T(1,128)S(1)}, u32[]{:S(2)}) copy-start(f32[1,3072]{1,0:T(1,128)S(1)} %get-tuple-element.83) | copy-start | bytes 36868
  87.8 79.8 %copy-start.55 = (f32[1,3072]{1,0:T(1,128)}, f32[1,3072]{1,0:T(1,128)S(1)}, u32[]{:S(2)}) copy-start(f32[1,3072]{1,0:T(1,128)S(1)} %get-tuple-element.84) | copy-start | bytes 36868
  87.8 79.8 %copy-start.57 = (f32[1,3072]{1,0:T(1,128)}, f32[1,3072]{1,0:T(1,128)S(1)}, u32[]{:S(2)}) copy-start(f32[1,3072]{1,0:T(1,128)S(1)} %get-tuple-element.85) | copy-start | bytes 36868
  157.7 9.4 collective-permute-start
  252.1 133.7 %copy-start.48 = (f32[1024]{0:T(1024)S(1)}, f32[1024]{0:T(1024)}, u32[]{:S(2)}) copy-start(f32[1024]{0:T(1024)} %param.23) | copy-start | bytes 12292
  256.4 247.0 %copy-start.68 = (f32[256]{0:T(256)}, f32[256]{0:T(256)S(1)}, u32[]{:S(2)}) copy-start(f32[256]{0:T(256)S(1)} %fusion.48) | copy-start | bytes 3076
  395.0 83.7 %copy-start.79 = (f32[256]{0:T(256)S(1)}, f32[256]{0:T(256)}, u32[]{:S(2)}) copy-start(f32[256]{0:T(256)} %broadcast_multiply_fusion.6) | copy-start | bytes 3076
  511.1 191.8 %reduce-scatter.14.cloned.1.call-start = ((), (), s32[]{:S(2)}) async-start(), calls=%async_computation.12 | async-start | bytes 6488064 | tf_op jit(solution)/shard_map/reduce_scatter | solution.py:489
  516.7 353.0 %reduce-scatter.8.cloned.1.call-start = ((), (), s32[]{:S(2)}) async-start(), calls=%async_computation.9 | async-start | bytes 10616832 | tf_op jit(solution)/shard_map/reduce_scatter | solution.py:477
  641.5 5.7 collective-permute-start.1
  656.2 409.0 %reduce-scatter.12.cloned.1.call-start = ((), (), s32[]{:S(2)}) async-start(), calls=%async_computation.11 | async-start | bytes 12976128 | tf_op jit(solution)/shard_map/reduce_scatter | solution.py:486
  666.4 463.1 %reduce-scatter.16.cloned.1.call-start = ((), (), s32[]{:S(2)}) async-start(), calls=%async_computation.13 | async-start | bytes 294912
  675.7 389.5 %copy-start.75 = (f32[1,256]{1,0:T(1,128)S(1)}, f32[1,256]{1,0:T(1,128)}, u32[]{:S(2)}) copy-start(f32[1,256]{1,0:T(1,128)} %copy-done.74) | copy-start | bytes 3076
  675.7 389.6 %copy-start.78 = (f32[256]{0:T(256)S(1)}, f32[256]{0:T(256)}, u32[]{:S(2)}) copy-start(f32[256]{0:T(256)} %get-tuple-element.80) | copy-start | bytes 3076
  675.7 390.2 %copy-start.37 = (bf16[256,3072]{1,0:T(8,128)(2,1)S(1)}, bf16[256,3072]{1,0:T(8,128)(2,1)}, u32[]{:S(2)}) copy-start(bf16[256,3072]{1,0:T(8,128)(2,1)} %copy-done.36) | copy-start | bytes 4718596
  677.9 531.7 %all-reduce.20.cloned.1.call-start = ((), (), s32[]{:S(2)}) async-start(), calls=%async_computation.14 | async-start | bytes 7471104 | tf_op jit(solution)/shard_map/psum | solution.py:494
  1065.9 49.2 %copy-start.73 = (f32[256]{0:T(256)S(1)}, f32[256]{0:T(256)}, u32[]{:S(2)}) copy-start(f32[256]{0:T(256)} %copy-done.72) | copy-start | bytes 3076
  1065.9 49.2 %copy-start.23 = (f32[256,1024]{1,0:T(8,128)S(1)}, f32[256,1024]{1,0:T(8,128)}, u32[]{:S(2)}) copy-start(f32[256,1024]{1,0:T(8,128)} %copy-done.22) | copy-start | bytes 3145732
  (70 other events, 409.0 us)
Sparse Core Ops, SparseCore 0:
  10.3 142.0 all-gather.4
  154.5 58.5 all-gather.6
  215.3 170.4 all-gather.8
  387.9 90.8 all-gather.10
  511.2 79.0 reduce-scatter.9
  593.8 109.0 reduce-scatter.13
  706.5 163.1 reduce-scatter.7
  873.4 191.7 reduce-scatter.11
  1069.1 60.3 reduce-scatter.15
  1132.0 77.5 all-reduce.19

commit v2 on v1

--- a/solution.py
+++ b/solution.py
@@ -21,12 +21,6 @@
 epsilon = 1e-06
 
 
-def shifted(value, axis, steps):
-    count = lax.axis_size(axis)
-    leading, last = (max(0, -steps), min(count, count - steps))
-    return lax.ppermute(value, axis, [(source, source + steps) for source in range(leading, last)])
-
-
 def rms_scale(field_in, gain_vec):
     return (
         field_in
@@ -37,31 +31,6 @@
 
 def unit_rows(field_in):
     return field_in * lax.rsqrt(jnp.sum(field_in * field_in, axis=-1, keepdims=True) + epsilon)
-
-
-def prepare(padded, little, conv_weight, decay_log, decay_bias):
-    length = padded.shape[0] - (CONV - 1)
-    convolved = conv_weight[0] * padded[0:length]
-    for offset in range(1, CONV):
-        convolved = convolved + conv_weight[offset] * padded[offset : offset + length]
-    active = jax.nn.silu(convolved)
-    queries = unit_rows(active[:, :KEYS].reshape(length, HEADS, DK)) * DK ** (-0.5)
-    key_rows = unit_rows(active[:, KEYS : 2 * KEYS].reshape(length, HEADS, DK))
-    values = active[:, 2 * KEYS :].reshape(length, HEADS, DV)
-    strength = jax.nn.sigmoid(little[:, :HEADS])
-    forget = -jnp.exp(decay_log) * jax.nn.softplus(little[:, HEADS:] + decay_bias)
-    return (queries, key_rows, values, strength, forget)
-
-
-def gated_norm(mixed_out, gate_pre, gain_out):
-    length = mixed_out.shape[0]
-    return (
-        rms_scale(mixed_out, gain_out) * jax.nn.silu(gate_pre.reshape(length, HEADS, DV))
-    ).reshape(length, VALUES)
-
-
-def swiglu(gate_up):
-    return jax.nn.silu(gate_up[:, :FF]) * gate_up[:, FF:]
 
 
 MESH = pl.DeviceIdType.MESH
@@ -357,6 +326,641 @@
     return found.reshape(seqs, heads, DK, DV)
 
 
+def tile_start(start):
+    return pl.multiple_of(start, 128)
+
+
+class Place:
+    def __init__(self, groups, count):
+        self.groups, self.count, self.half = groups, count, count // 2
+        self.group, self.place = lax.axis_index("dp"), lax.axis_index("seq")
+        self.pair, self.side = self.place // 2, self.place % 2
+        self.plane = (self.group // 2) % 2
+        self.group_swap = self.group + 1 - 2 * (self.group % 2)
+        self.across = self.group + 2 - 4 * self.plane
+        self.beside = self.place + 1 - 2 * self.side
+
+    def shard(self, pair, side):
+        return 2 * pair + side
+
+    def ahead(self, step):
+        return lax.rem(self.pair + step, self.half)
+
+    def behind(self, step):
+        return lax.rem(self.pair + self.half - step, self.half)
+
+    def partners(self):
+        along = [(self.group, self.shard(self.ahead(step), self.side)) for step in range(1, self.half)]
+        return along + [(self.group, self.beside), (self.across, self.place)]
+
+
+def greet(signalled, awaited):
+    barrier = pltpu.get_barrier_semaphore()
+    for device in signalled:
+        pl.semaphore_signal(barrier, inc=1, device_id=device, device_id_type=MESH)
+    pl.semaphore_wait(barrier, awaited)
+
+
+def remote(source, target, sends, receives, index, device):
+    return pltpu.make_async_remote_copy(
+        src_ref=source,
+        dst_ref=target,
+        send_sem=sends.at[index],
+        recv_sem=receives.at[index],
+        device_id=device,
+        device_id_type=MESH,
+    )
+
+
+class Gather:
+    def __init__(self, at, source, target, share, sends, receives, local):
+        self.at, self.source, self.target = at, source, target
+        self.sends, self.receives, self.local = sends, receives, local
+        width = source.shape[1]
+        self.own = pl.ds(tile_start(at.plane * share), width - share)
+        self.lent = pl.ds(tile_start(at.plane * (width - share)), share)
+        self.borrowed = pl.ds(tile_start((1 - at.plane) * (width - share)), share)
+        self.started = []
+
+    def copy(self, index, shard, columns, device, from_source=False):
+        there = self.target.at[shard, :, columns]
+        here = self.source.at[:, columns] if from_source else there
+        return remote(here, there, self.sends, self.receives, index, device)
+
+    def along(self, step):
+        at = self.at
+        device = (at.group, at.shard(at.ahead(step), at.side))
+        return self.copy(step - 1, at.place, self.own, device, True)
+
+    def beside(self, step):
+        at = self.at
+        shard = at.shard(at.behind(step), at.side)
+        return self.copy(at.half - 1 + step, shard, self.own, (at.group, at.beside), step == 0)
+
+    def across(self, step, side):
+        at = self.at
+        shard = at.shard(at.behind(step), at.side if side == 0 else 1 - at.side)
+        return self.copy(2 * at.half - 1 + 2 * step + side - 1, shard, self.lent, (at.across, at.place))
+
+    def keep(self):
+        return pltpu.make_async_copy(self.source, self.target.at[self.at.place], self.local)
+
+    def launch(self, copy):
+        copy.start()
+        self.started.append(copy)
+
+    def begin(self):
+        self.keep().start()
+        for step in range(1, self.at.half):
+            self.launch(self.along(step))
+        self.launch(self.beside(0))
+
+    def arrived(self, index, shard, columns):
+        self.copy(index, shard, columns, (self.at.group, self.at.place)).wait_recv()
+
+    def pass_along(self, step):
+        at = self.at
+        self.arrived(step - 1, at.shard(at.behind(step), at.side), self.own)
+        self.launch(self.beside(step))
+        self.launch(self.across(step, 0))
+
+    def pass_beside(self, step):
+        at = self.at
+        self.arrived(at.half - 1 + step, at.shard(at.behind(step), 1 - at.side), self.own)
+        self.launch(self.across(step, 1))
+
+    def finish(self):
+        at = self.at
+        for step in range(at.half):
+            for side in range(2):
+                if step or side:
+                    shard = at.shard(at.behind(step), at.side if side == 0 else 1 - at.side)
+                    self.arrived(2 * at.half - 1 + 2 * step + side - 1, shard, self.borrowed)
+        for copy in self.started:
+            copy.wait_send()
+        self.keep().wait()
+
+    def stages(self):
+        half = self.at.half
+        first = [functools.partial(self.pass_along, step) for step in range(1, half)]
+        second = [functools.partial(self.pass_beside, step) for step in range(half)]
+        return first, second
+
+
+def copies_of_gather(count):
+    return 2 * count - 2
+
+
+def lagged(plans):
+    depth = max(len(plan) for plan in plans)
+    turns = []
+    for turn in range(len(plans) + depth - 1):
+        steps = []
+        for index, plan in enumerate(plans):
+            if 0 <= turn - index < len(plan):
+                steps = plan[turn - index] + steps
+        turns.append(steps)
+    return turns
+
+
+class Reduce:
+    def __init__(self, at, given, total, other, share, buffers, sems):
+        self.at, self.given, self.total, self.other, self.share = at, given, total, other, share
+        self.acc, self.from_across, self.from_beside, self.from_along, self.part, self.from_plane, self.far = buffers
+        self.sends, self.receives, self.local = sems
+        width = total.shape[1]
+        self.wide = width - share
+        self.own = pl.ds(tile_start(at.plane * share), self.wide)
+        self.lent = pl.ds(tile_start((1 - at.plane) * self.wide), share)
+        self.inner = pl.ds(tile_start(at.plane * (width - 2 * share)), share)
+        self.theirs = pl.ds(tile_start((1 - at.plane) * share), self.wide)
+        self.started = []
+
+    def launch(self, copy):
+        copy.start()
+        self.started.append(copy)
+
+    def across(self, shard, index):
+        at = self.at
+        return remote(
+            self.given.at[shard, :, self.lent], self.from_across.at[shard],
+            self.sends, self.receives, index, (at.across, at.place),
+        )
+
+    def beside(self, pair):
+        at = self.at
+        return remote(
+            self.acc.at[at.shard(pair, 1 - at.side)], self.from_beside.at[pair],
+            self.sends, self.receives, at.count + pair, (at.group, at.beside),
+        )
+
+    def along(self, step):
+        at = self.at
+        shard = at.shard(at.ahead(step), at.side)
+        return remote(
+            self.acc.at[shard], self.from_along.at[step - 1],
+            self.sends, self.receives, at.count + at.half + step - 1, (at.group, shard),
+        )
+
+    def plane(self):
+        at = self.at
+        return remote(
+            self.part, self.from_plane, self.sends, self.receives,
+            at.count + 2 * at.half - 1, (at.across, at.place),
+        )
+
+    def further(self, index, distance):
+        at = self.at
+        group = at.group + distance - 2 * distance * ((at.group // distance) % 2)
+        return remote(
+            self.total, self.far.at[index], self.sends, self.receives,
+            at.count + 2 * at.half + 1 + index, (group, at.place),
+        )
+
+    def core(self):
+        at = self.at
+        return remote(
+            self.total, self.other, self.sends, self.receives,
+            at.count + 2 * at.half, (at.group_swap, at.place),
+        )
+
+    def load(self, shard, index):
+        return pltpu.make_async_copy(self.given.at[shard, :, self.own], self.acc.at[shard], self.local.at[index])
+
+    def order(self, side):
+        at = self.at
+        return [(pair, at.shard(pair, at.side if side else 1 - at.side)) for pair in range(at.half)]
+
+    def begin(self):
+        for side in range(2):
+            for pair, shard in self.order(side):
+                self.load(shard, 2 * pair + side).start()
+                self.launch(self.across(shard, 2 * pair + side))
+
+    def add_across(self, side):
+        for pair, shard in self.order(side):
+            self.load(shard, 2 * pair + side).wait()
+            self.across(shard, 2 * pair + side).wait_recv()
+            mine = self.acc[shard, :, self.inner].astype(jnp.float32)
+            got = self.from_across[shard].astype(jnp.float32)
+            self.acc[shard, :, self.inner] = (mine + got).astype(jnp.bfloat16)
+            if side == 0:
+                self.launch(self.beside(pair))
+
+    def add_beside(self):
+        at = self.at
+        for step in range(1, at.half + 1):
+            pair = at.ahead(step)
+            shard = at.shard(pair, at.side)
+            self.beside(pair).wait_recv()
+            mine = self.acc[shard].astype(jnp.float32)
+            self.acc[shard] = (mine + self.from_beside[pair].astype(jnp.float32)).astype(jnp.bfloat16)
+            if step < at.half:
+                self.launch(self.along(step))
+
+    def add_along(self):
+        at = self.at
+        value = self.acc[at.place].astype(jnp.float32)
+        for step in range(1, at.half):
+            self.along(step).wait_recv()
+            value = value + self.from_along[step - 1].astype(jnp.float32)
+        self.part[...] = value.astype(jnp.bfloat16)
+        self.launch(self.plane())
+
+    def add_plane(self):
+        self.plane().wait_recv()
+        self.total[...] = jnp.zeros_like(self.total)
+        self.total[:, self.own] = self.part[...]
+        mine = self.total[:, self.theirs].astype(jnp.float32)
+        got = self.from_plane[...].astype(jnp.float32)
+        self.total[:, self.theirs] = (mine + got).astype(jnp.bfloat16)
+        distance = 4
+        while distance < self.at.groups:
+            copy = self.further(distance.bit_length() - 3, distance)
+            copy.start()
+            copy.wait()
+            got = self.far[distance.bit_length() - 3].astype(jnp.float32)
+            self.total[...] = (self.total[...].astype(jnp.float32) + got).astype(jnp.bfloat16)
+            distance *= 2
+        self.launch(self.core())
+
+    def finish(self):
+        self.core().wait_recv()
+        for copy in self.started:
+            copy.wait_send()
+
+    def stages(self):
+        return [
+            [functools.partial(self.add_across, 0)],
+            [functools.partial(self.add_across, 1), self.add_beside],
+            [self.add_along],
+            [self.add_plane],
+        ]
+ANY = pl.BlockSpec(memory_space=pl.ANY)
+ROOM = pl.BlockSpec(memory_space=pltpu.VMEM)
+PAD = 16
+
+
+def neighbours(at, step):
+    place = lax.rem(at.place + at.count + step, at.count)
+    return (at.group, place), (at.group_swap, place)
+
+
+def gather_first_kernel(groups, count, share, *refs):
+    source, tokens, target, mask = refs[:4]
+    gathered, tokens_other, target_other, mask_other, rim = refs[4:9]
+    sends, receives, local, swap_send, swap_recv = refs[9:]
+    at = Place(groups, count)
+    core = (at.group_swap, at.place)
+    greet(at.partners() + [core] + list(neighbours(at, -1)), count // 2 + 4)
+    swaps = [
+        remote(here, there, swap_send, swap_recv, index, core)
+        for index, (here, there) in enumerate(
+            ((tokens, tokens_other), (target, target_other), (mask, mask_other))
+        )
+    ]
+    length = tokens.shape[0]
+    tail = tokens.at[pl.ds(length - PAD, PAD)]
+    own_next, swap_next = neighbours(at, 1)
+    rims = [
+        remote(tail, rim.at[0], swap_send, swap_recv, 3, own_next),
+        remote(tail, rim.at[1], swap_send, swap_recv, 4, swap_next),
+    ]
+    plan = Gather(at, source, gathered, share, sends, receives, local.at[0])
+
+    @pl.when(at.place < count - 1)
+    def _():
+        for copy in rims:
+            copy.start()
+
+    plan.begin()
+    for copy in swaps:
+        copy.start()
+    for stage in plan.stages():
+        for step in stage:
+            step()
+    plan.finish()
+    for copy in swaps:
+        copy.wait()
+
+    @pl.when(at.place == 0)
+    def _():
+        rim[...] = jnp.zeros_like(rim)
+
+    @pl.when(at.place > 0)
+    def _():
+        for copy in rims:
+            copy.wait_recv()
+
+    @pl.when(at.place < count - 1)
+    def _():
+        for copy in rims:
+            copy.wait_send()
+
+
+def gather_first(source, tokens, target, mask, share):
+    groups, count = lax.axis_size("dp"), lax.axis_size("seq")
+    rows, width = source.shape
+    return pl.pallas_call(
+        functools.partial(gather_first_kernel, groups, count, share),
+        out_shape=[
+            jax.ShapeDtypeStruct((count, rows, width), source.dtype),
+            jax.ShapeDtypeStruct(tokens.shape, tokens.dtype),
+            jax.ShapeDtypeStruct(target.shape, target.dtype),
+            jax.ShapeDtypeStruct(mask.shape, mask.dtype),
+            jax.ShapeDtypeStruct((2, PAD, tokens.shape[1]), tokens.dtype),
+        ],
+        in_specs=[ANY] * 4,
+        out_specs=[ANY] * 4 + [ROOM],
+        scratch_shapes=[
+            pltpu.SemaphoreType.DMA((copies_of_gather(count),)),
+            pltpu.SemaphoreType.DMA((copies_of_gather(count),)),
+            pltpu.SemaphoreType.DMA((1,)),
+            pltpu.SemaphoreType.DMA((5,)),
+            pltpu.SemaphoreType.DMA((5,)),
+        ],
+        compiler_params=pltpu.CompilerParams(collective_id=3, has_side_effects=True),
+        name="gather_first",
+    )(source, tokens, target, mask)
+
+
+def gather_rest_kernel(groups, count, shares, *refs):
+    number = len(shares)
+    sources, targets = refs[:number], refs[number : 2 * number]
+    sends, receives, local = refs[2 * number :]
+    at = Place(groups, count)
+    greet(at.partners(), count // 2 + 1)
+    plans = [
+        Gather(at, sources[i], targets[i], shares[i], sends.at[i], receives.at[i], local.at[i])
+        for i in range(number)
+    ]
+    for plan in plans:
+        plan.begin()
+    for turn in lagged([plan.stages() for plan in plans]):
+        for step in turn:
+            step()
+    for plan in plans:
+        plan.finish()
+
+
+def gather_rest(sources, shares):
+    groups, count = lax.axis_size("dp"), lax.axis_size("seq")
+    number = len(sources)
+    return pl.pallas_call(
+        functools.partial(gather_rest_kernel, groups, count, shares),
+        out_shape=[jax.ShapeDtypeStruct((count,) + v.shape, v.dtype) for v in sources],
+        in_specs=[ANY] * number,
+        out_specs=[ANY] * number,
+        scratch_shapes=[
+            pltpu.SemaphoreType.DMA((number, copies_of_gather(count))),
+            pltpu.SemaphoreType.DMA((number, copies_of_gather(count))),
+            pltpu.SemaphoreType.DMA((number,)),
+        ],
+        compiler_params=pltpu.CompilerParams(collective_id=4, has_side_effects=True),
+        name="gather_rest",
+    )(*sources)
+
+
+def reduce_buffers(groups, count, rows, width, share):
+    wide, half = width - share, count // 2
+    steps = max(1, (groups // 4).bit_length() - 1)
+    kind = jnp.bfloat16
+    return [
+        pltpu.VMEM((count, rows, wide), kind),
+        pltpu.VMEM((count, rows, share), kind),
+        pltpu.VMEM((half, rows, wide), kind),
+        pltpu.VMEM((half - 1, rows, wide), kind),
+        pltpu.VMEM((rows, wide), kind),
+        pltpu.VMEM((rows, wide), kind),
+        pltpu.VMEM((steps, rows, width), kind),
+    ]
+
+
+def copies_of_reduce(groups, count):
+    return 2 * count + 1 + max(1, (groups // 4).bit_length() - 1)
+
+
+def further_groups(at):
+    found, distance = [], 4
+    while distance < at.groups:
+        found.append((at.group + distance - 2 * distance * ((at.group // distance) % 2), at.place))
+        distance *= 2
+    return found
+
+
+def reduce_plans(at, givens, totals, others, shares, scratch):
+    number = len(shares)
+    sends, receives, local = scratch[7 * number : 7 * number + 3]
+    return [
+        Reduce(
+            at, givens[i], totals[i], others[i], shares[i], scratch[7 * i : 7 * i + 7],
+            (sends.at[i], receives.at[i], local.at[i]),
+        )
+        for i in range(number)
+    ]
+
+
+def reduce_scratch(groups, count, rows, widths, shares):
+    scratch = []
+    for width, share in zip(widths, shares):
+        scratch += reduce_buffers(groups, count, rows, width, share)
+    number, copies = len(widths), copies_of_reduce(groups, count)
+    return scratch + [
+        pltpu.SemaphoreType.DMA((number, copies)),
+        pltpu.SemaphoreType.DMA((number, copies)),
+        pltpu.SemaphoreType.DMA((number, count)),
+    ]
+
+
+def reduce_rest_kernel(groups, count, shares, *refs):
+    number = len(shares)
+    givens, totals, others = refs[:number], refs[number : 2 * number], refs[2 * number : 3 * number]
+    at = Place(groups, count)
+    further = further_groups(at)
+    partners = at.partners() + [(at.group_swap, at.place)] + further
+    greet(partners, count // 2 + 2 + len(further))
+    plans = reduce_plans(at, givens, totals, others, shares, refs[3 * number :])
+    for plan in plans:
+        plan.begin()
+    for turn in lagged([plan.stages() for plan in plans]):
+        for step in turn:
+            step()
+    for plan in plans:
+        plan.finish()
+
+
+def reduce_rest(givens, shares):
+    groups, count = lax.axis_size("dp"), lax.axis_size("seq")
+    number = len(givens)
+    rows = givens[0].shape[1]
+    widths = [v.shape[2] for v in givens]
+    results = [jax.ShapeDtypeStruct((rows, width), jnp.bfloat16) for width in widths]
+    return pl.pallas_call(
+        functools.partial(reduce_rest_kernel, groups, count, shares),
+        out_shape=results * 2,
+        in_specs=[ANY] * number,
+        out_specs=[ROOM] * (2 * number),
+        scratch_shapes=reduce_scratch(groups, count, rows, widths, shares),
+        compiler_params=pltpu.CompilerParams(
+            collective_id=5, has_side_effects=True, vmem_limit_bytes=56 * 2**20
+        ),
+        name="reduce_rest",
+    )(*givens)
+
+
+def reduce_first_kernel(groups, count, share, *refs):
+    given, swap, rims, small = refs[:4]
+    total, other, swap_got, rim_got, small_sum = refs[4:9]
+    scratch = refs[9:]
+    small_got, small_hold, swap_send, swap_recv, small_send, small_recv = scratch[10:]
+    at = Place(groups, count)
+    further = further_groups(at)
+    core = (at.group_swap, at.place)
+    stages = []
+    distance = 1
+    while distance < groups:
+        stages.append((at.group + distance - 2 * distance * ((at.group // distance) % 2), at.place))
+        distance *= 2
+    distance = 1
+    while distance < count:
+        stages.append((at.group, at.place + distance - 2 * distance * ((at.place // distance) % 2)))
+        distance *= 2
+    partners = at.partners() + [core] + further + stages + list(neighbours(at, 1))
+    greet(partners, count // 2 + 4 + len(further) + len(stages))
+    own_back, swap_back = neighbours(at, -1)
+    swapped = remote(swap, swap_got, swap_send, swap_recv, 0, core)
+    rim_copies = [
+        remote(rims.at[0], rim_got.at[0], swap_send, swap_recv, 1, own_back),
+        remote(rims.at[1], rim_got.at[1], swap_send, swap_recv, 2, swap_back),
+    ]
+    plan = reduce_plans(at, [given], [total], [other], [share], scratch)[0]
+    plan.begin()
+    swapped.start()
+
+    @pl.when(at.place > 0)
+    def _():
+        for copy in rim_copies:
+            copy.start()
+
+    small_hold[0] = small[...]
+
+    def add_small(index):
+        copy = remote(
+            small_hold.at[index], small_got.at[index], small_send, small_recv, index, stages[index]
+        )
+        copy.start()
+        copy.wait()
+        small_hold[index + 1] = small_hold[index] + small_got[index]
+
+    steps = [step for stage in plan.stages() for step in stage]
+    for index in range(max(len(steps), len(stages))):
+        if index < len(steps):
+            steps[index]()
+        if index < len(stages):
+            add_small(index)
+    small_sum[...] = small_hold[len(stages)]
+    swapped.wait()
+
+    @pl.when(at.place == count - 1)
+    def _():
+        rim_got[...] = jnp.zeros_like(rim_got)
+
+    @pl.when(at.place < count - 1)
+    def _():
+        for copy in rim_copies:
+            copy.wait_recv()
+
+    @pl.when(at.place > 0)
+    def _():
+        for copy in rim_copies:
+            copy.wait_send()
+
+    plan.finish()
+
+
+def reduce_first(given, swap, rims, small, share):
+    groups, count = lax.axis_size("dp"), lax.axis_size("seq")
+    unused, rows, width = given.shape
+    rounds = (groups.bit_length() - 1) + (count.bit_length() - 1)
+    result = jax.ShapeDtypeStruct((rows, width), jnp.bfloat16)
+    return pl.pallas_call(
+        functools.partial(reduce_first_kernel, groups, count, share),
+        out_shape=[
+            result,
+            result,
+            jax.ShapeDtypeStruct(swap.shape, swap.dtype),
+            jax.ShapeDtypeStruct(rims.shape, rims.dtype),
+            jax.ShapeDtypeStruct(small.shape, small.dtype),
+        ],
+        in_specs=[ANY, ROOM, ROOM, ROOM],
+        out_specs=[ROOM] * 5,
+        scratch_shapes=reduce_scratch(groups, count, rows, [width], [share])
+        + [
+            pltpu.VMEM((rounds,) + small.shape, jnp.float32),
+            pltpu.VMEM((rounds + 1,) + small.shape, jnp.float32),
+            pltpu.SemaphoreType.DMA((3,)),
+            pltpu.SemaphoreType.DMA((3,)),
+            pltpu.SemaphoreType.DMA((rounds,)),
+            pltpu.SemaphoreType.DMA((rounds,)),
+        ],
+        compiler_params=pltpu.CompilerParams(
+            collective_id=6, has_side_effects=True, vmem_limit_bytes=56 * 2**20
+        ),
+        name="reduce_first",
+    )(given, swap, rims, small)
+
+
+def third(width, weight):
+    return 128 * max(1, round(width * weight / 128))
+
+
+def prepare(padded, little, conv_weight, decay_log, decay_bias):
+    seqs, length = padded.shape[0], padded.shape[1] - (CONV - 1)
+    convolved = conv_weight[0] * padded[:, 0:length]
+    for offset in range(1, CONV):
+        convolved = convolved + conv_weight[offset] * padded[:, offset : offset + length]
+    active = jax.nn.silu(convolved)
+    heads = decay_log.shape[0]
+    keys = heads * DK
+    queries = unit_rows(active[..., :keys].reshape(seqs, length, heads, DK)) * DK ** (-0.5)
+    key_rows = unit_rows(active[..., keys : 2 * keys].reshape(seqs, length, heads, DK))
+    strength = jax.nn.sigmoid(little[..., :heads])
+    forget = -jnp.exp(decay_log) * jax.nn.softplus(little[..., heads:] + decay_bias)
+    return (
+        queries.reshape(seqs, length, keys),
+        key_rows.reshape(seqs, length, keys),
+        active[..., 2 * keys :],
+        strength,
+        forget,
+    )
+
+
+def gated_norm(mixed_out, gate_pre, gain_out):
+    rows, width = mixed_out.shape
+    split = mixed_out.reshape(rows, width // DV, DV)
+    gate = jax.nn.silu(gate_pre.reshape(split.shape))
+    return (rms_scale(split, gain_out) * gate).reshape(rows, width)
+
+
+def swiglu(gate_up):
+    hidden_units = gate_up.shape[1] // 2
+    return jax.nn.silu(gate_up[:, :hidden_units]) * gate_up[:, hidden_units:]
+
+
+def norm_parts(field_in):
+    scale = lax.rsqrt(jnp.mean(field_in * field_in, axis=-1, keepdims=True) + epsilon)
+    return scale, field_in * scale
+
+
+def norm_back(scale, unit, gain_vec, grad):
+    scaled = grad * gain_vec
+    return scale * (scaled - unit * jnp.mean(scaled * unit, axis=-1, keepdims=True))
+
+
+def dense(left, right, dims):
+    return lax.dot_general(left, right, (dims, ((), ())), preferred_element_type=jnp.float32)
+
+
 def on_device(
     tokens,
     target,
@@ -373,156 +977,243 @@
     decay_log,
     decay_bias,
 ):
-    inputs = tokens[0].astype(jnp.float32)
-    length = inputs.shape[0]
-    w_in, w_small = (
-        lax.all_gather(in_weight, "seq", axis=0, tiled=True),
-        lax.all_gather(small_weight, "seq", axis=0, tiled=True),
-    )
-    normed_f, first_pull = jax.vjp(rms_scale, inputs, gain_first)
-    normed = normed_f.astype(jnp.bfloat16)
-    project = jnp.dot(normed, w_in, preferred_element_type=jnp.float32)
-    little = jnp.dot(normed, w_small, preferred_element_type=jnp.float32)
-    mixed_in = project[:, : 2 * KEYS + VALUES].astype(jnp.bfloat16)
-    gate_pre = project[:, 2 * KEYS + VALUES :]
-    rim_rows = shifted(mixed_in[length - (CONV - 1) :], "seq", 1)
-    padded = jnp.concatenate([rim_rows, mixed_in], axis=0).astype(jnp.float32)
-    prepared, local_pull = jax.vjp(prepare, padded, little, conv_weight, decay_log, decay_bias)
+    count = lax.axis_size("seq")
+    groups = lax.axis_size("dp")
+    core = lax.axis_index("dp") % 2
+    rows = in_weight.shape[0]
+    length, model = tokens.shape[1], tokens.shape[2]
+    both = 2 * length
+    heads = HEADS // 2
+    keys, vals = KEYS // 2, VALUES // 2
+
+    def mine(array, start, width):
+        return lax.dynamic_slice_in_dim(array, start + core * width, width, array.ndim - 1)
+
+    def qkv_half(array):
+        parts = [mine(array, 0, keys), mine(array, KEYS, keys), mine(array, 2 * KEYS, vals)]
+        return jnp.concatenate(parts, axis=1)
+
+    small_half = [mine(small_weight, 0, heads), mine(small_weight, HEADS, heads)]
+    spare = jnp.zeros((rows, 128 - 2 * heads), jnp.bfloat16)
+    part_first = jnp.concatenate([qkv_half(in_weight)] + small_half + [spare], axis=1)
+    part_gate = mine(in_weight, 2 * KEYS + VALUES, vals)
+    part_out = mine(out_weight, 0, vals)
+    part_up = jnp.concatenate([mine(ffn_in, 0, FF // 2), mine(ffn_in, FF, FF // 2)], axis=1)
+    part_down = mine(ffn_out, 0, FF // 2)
+    first_width = part_first.shape[1]
+
+    mask_own = valid[0].astype(jnp.float32)
+    mask_rows = jnp.broadcast_to(mask_own[None, :], (8, length))
+    w_first, tokens_other, target_other, mask_other, rim = gather_first(
+        part_first, tokens[0], target[0], mask_rows, third(first_width, 0.33)
+    )
+    rests = [part_gate, part_out, part_up, part_down]
+    w_gate, w_out, w_up, w_down = gather_rest(rests, [third(v.shape[1], 0.33) for v in rests])
+    w_first, w_gate, w_out, w_up, w_down = (
+        v.reshape(model, v.shape[2]) for v in (w_first, w_gate, w_out, w_up, w_down)
+    )
+
+    inputs = jnp.concatenate(
+        [tokens[0], tokens_other, rim.reshape(2 * PAD, model)], axis=0
+    ).astype(jnp.float32)
+    first_scale, first_unit = norm_parts(inputs)
+    normed = (first_unit * gain_first).astype(jnp.bfloat16)
+    project = dense(normed, w_first, ((1,), (0,)))
+    gate_pre = dense(normed[:both], w_gate, ((1,), (0,)))
+    mixed_width = 2 * keys + vals
+    mixed_in = project[:, :mixed_width].astype(jnp.bfloat16).astype(jnp.float32)
+    little = project[:both, mixed_width : mixed_width + 2 * heads].reshape(2, length, 2 * heads)
+    padded = jnp.concatenate(
+        [
+            mixed_in[both:].reshape(2, PAD, mixed_width)[:, PAD - (CONV - 1) :],
+            mixed_in[:both].reshape(2, length, mixed_width),
+        ],
+        axis=1,
+    )
+    own_conv = qkv_half(conv_weight)
+    own_log, own_bias = mine(decay_log, 0, heads), mine(decay_bias, 0, heads)
+    prepared, local_pull = jax.vjp(prepare, padded, little, own_conv, own_log, own_bias)
     queries, key_rows, values, strength, forget = prepared
-    cumulative = jnp.cumsum(forget, axis=0).T
-    strength_t = strength.T
-    cols = jnp.stack([cumulative, strength_t] + [jnp.zeros_like(cumulative)] * 6, axis=-1)[None]
-    rows = jnp.stack([cumulative] * 8, axis=1)[None]
-    flat_q, flat_k = queries.reshape(1, length, KEYS), key_rows.reshape(1, length, KEYS)
-    flat_v = values.reshape(1, length, VALUES)
+    cumulative = jnp.swapaxes(jnp.cumsum(forget, axis=1), 1, 2)
+    strength_t = jnp.swapaxes(strength, 1, 2)
+    cols = jnp.stack([cumulative, strength_t] + [jnp.zeros_like(cumulative)] * 6, axis=-1)
+    table = jnp.stack([cumulative] * 8, axis=2)
     solve, update, back, mapping, offset, own_out, reach = delta_local(
-        flat_q, flat_k, flat_v, cols, rows
+        queries, key_rows, values, cols, table
     )
     entering = relay(mapping, offset, True)
-    mixed_out = jnp.transpose(
-        own_out[0] + jnp.einsum("htk,hkv->htv", reach[0], entering[0], precision=precise),
-        (1, 0, 2),
-    )
+    mixed_out = jnp.swapaxes(
+        own_out + jnp.einsum("jhtk,jhkv->jhtv", reach, entering, precision=precise), 1, 2
+    ).reshape(both, vals)
     branch_f, gated_pull = jax.vjp(gated_norm, mixed_out, gate_pre, gain_out)
     branch = branch_f.astype(jnp.bfloat16)
-    w_out, w_up, w_down = (
-        lax.all_gather(out_weight, "seq", axis=0, tiled=True),
-        lax.all_gather(ffn_in, "seq", axis=0, tiled=True),
-        lax.all_gather(ffn_out, "seq", axis=0, tiled=True),
-    )
-    attended = jnp.einsum("tv,dv->td", branch, w_out, preferred_element_type=jnp.float32)
-    hidden = inputs + attended
-    second_f, second_pull = jax.vjp(rms_scale, hidden, gain_second)
-    second = second_f.astype(jnp.bfloat16)
-    gate_up = jnp.dot(second, w_up, preferred_element_type=jnp.float32)
+
+    def core_sum(part):
+        pairs = [(group, group ^ 1) for group in range(groups)]
+        got = lax.ppermute(part.astype(jnp.bfloat16), "dp", pairs)
+        return part + jnp.concatenate([got[length:], got[:length]], axis=0).astype(jnp.float32)
+
+    hidden = inputs[:both] + core_sum(dense(branch, w_out, ((1,), (1,))))
+    second_scale, second_unit = norm_parts(hidden)
+    second = (second_unit * gain_second).astype(jnp.bfloat16)
+    gate_up = dense(second, w_up, ((1,), (0,)))
     active_f, swiglu_pull = jax.vjp(swiglu, gate_up)
     active = active_f.astype(jnp.bfloat16)
-    feed_out = jnp.einsum("tf,df->td", active, w_down, preferred_element_type=jnp.float32)
-    summed = hidden + feed_out
-    mask_row = valid[0].astype(jnp.float32)
-    errors = summed - target[0].astype(jnp.float32)
-    totals = lax.psum(
-        (jnp.sum(mask_row * jnp.mean(errors * errors, axis=-1)), jnp.sum(mask_row)), ("dp", "seq")
-    )
-    valid_count = jnp.maximum(totals[1], 1.0)
-    loss_value = totals[0] / valid_count
-    all_tokens = length * lax.axis_size("dp") * lax.axis_size("seq")
-    grad_summed = all_tokens / valid_count * mask_row[:, None] * errors
+    summed = hidden + core_sum(dense(active, w_down, ((1,), (1,))))
+    mask = jnp.concatenate([mask_own, mask_other[0]])
+    errors = summed - jnp.concatenate([target[0], target_other]).astype(jnp.float32)
+    own_errors = errors[:length]
+    loss_part = jnp.sum(mask_own * jnp.mean(own_errors * own_errors, axis=-1))
+
+    grad_summed = mask[:, None] * errors
     grad_feed = grad_summed.astype(jnp.bfloat16)
-    grad_active = jnp.dot(grad_feed, w_down, preferred_element_type=jnp.float32)
-    grad_ffn_out = jnp.einsum("td,tf->df", grad_feed, active, preferred_element_type=jnp.float32)
+    grad_active = dense(grad_feed, w_down, ((1,), (0,)))
+    grad_down = dense(grad_feed, active, ((0,), (0,))).astype(jnp.bfloat16)
     grad_gate_up = swiglu_pull(grad_active)[0].astype(jnp.bfloat16)
-    grad_ffn_in = jnp.einsum("td,tf->df", second, grad_gate_up, preferred_element_type=jnp.float32)
-    grad_second = jnp.einsum("tf,df->td", grad_gate_up, w_up, preferred_element_type=jnp.float32)
-    hidden_part, grad_gain_second = second_pull(grad_second)
-    grad_hidden = grad_summed + hidden_part
+    grad_up = dense(second, grad_gate_up, ((0,), (0,))).astype(jnp.bfloat16)
+    grad_second = core_sum(dense(grad_gate_up, w_up, ((1,), (1,))))
+    grad_gain_second = jnp.sum((grad_second * second_unit)[:length], axis=0)
+    grad_hidden = grad_summed + norm_back(second_scale, second_unit, gain_second, grad_second)
     grad_attn = grad_hidden.astype(jnp.bfloat16)
-    grad_out_weight = jnp.einsum("td,tv->dv", grad_attn, branch, preferred_element_type=jnp.float32)
-    grad_branch = jnp.dot(grad_attn, w_out, preferred_element_type=jnp.float32)
+    grad_out = dense(grad_attn, branch, ((0,), (0,))).astype(jnp.bfloat16)
+    grad_branch = dense(grad_attn, w_out, ((1,), (0,)))
     grad_mixed, grad_gate_pre, grad_gain_out = gated_pull(grad_branch)
-    returning = jnp.einsum("htk,thv->hkv", reach[0], grad_mixed, precision=precise)[None]
+    grad_gate_pre = grad_gate_pre.astype(jnp.bfloat16)
+    grad_gate = dense(normed[:both], grad_gate_pre, ((0,), (0,))).astype(jnp.bfloat16)
+
+    grad_rests = [grad_down, grad_up, grad_out, grad_gate]
+    reduced = reduce_rest(
+        [v.reshape(count, rows, v.shape[1]) for v in grad_rests],
+        [third(v.shape[1], 0.28) for v in grad_rests],
+    )
+
+    split_mixed = grad_mixed.reshape(2, length, heads, DV)
+    returning = jnp.einsum("jhtk,jthv->jhkv", reach, split_mixed, precision=precise)
     after = relay(mapping, returning, False)
     grad_q, grad_k, grad_v, grad_cols, grad_rows = delta_grads(
-        flat_q, flat_k, flat_v, cols, rows, solve, update, back, entering,
-        grad_mixed.reshape(1, length, VALUES), after,
-    )
-    grad_log = grad_cols[0, :, :, 0] - grad_rows[0, :, 0, :]
-    grad_forget = lax.cumsum(grad_log, axis=1, reverse=True).T
-    grad_prepared = (
-        grad_q.reshape(length, HEADS, DK),
-        grad_k.reshape(length, HEADS, DK),
-        grad_v.reshape(length, HEADS, DV),
-        grad_cols[0, :, :, 1].T,
-        grad_forget,
-    )
+        queries, key_rows, values, cols, table, solve, update, back, entering,
+        grad_mixed.reshape(2, length, vals), after,
+    )
+    grad_log = grad_cols[..., 0] - grad_rows[:, :, 0, :]
+    grad_forget = jnp.swapaxes(lax.cumsum(grad_log, axis=2, reverse=True), 1, 2)
+    grad_prepared = (grad_q, grad_k, grad_v, jnp.swapaxes(grad_cols[..., 1], 1, 2), grad_forget)
     grad_padded, grad_little, grad_conv, grad_decay_log, grad_decay_bias = local_pull(grad_prepared)
-    rim_grad = shifted(grad_padded[: CONV - 1].astype(jnp.bfloat16), "seq", -1).astype(jnp.float32)
-    grad_mixed_in = grad_padded[CONV - 1 :] + jnp.concatenate(
-        [jnp.zeros((length - (CONV - 1), grad_padded.shape[1]), jnp.float32), rim_grad], axis=0
-    )
-    grad_project = jnp.concatenate([grad_mixed_in, grad_gate_pre], axis=1).astype(jnp.bfloat16)
-    grad_little_b = grad_little.astype(jnp.bfloat16)
-    grad_in_weight = jnp.einsum(
-        "td,tp->dp", normed, grad_project, preferred_element_type=jnp.float32
-    )
-    grad_small_weight = jnp.einsum(
-        "td,ts->ds", normed, grad_little_b, preferred_element_type=jnp.float32
-    )
-    grad_normed = jnp.einsum(
-        "tp,dp->td", grad_project, w_in, preferred_element_type=jnp.float32
-    ) + jnp.einsum("ts,ds->td", grad_little_b, w_small, preferred_element_type=jnp.float32)
-    input_part, grad_gain_first = first_pull(grad_normed)
-    grad_tokens = grad_hidden + input_part
-    stored = (
-        lax.psum_scatter(
-            grad_in_weight.astype(jnp.bfloat16), "seq", scatter_dimension=0, tiled=True
-        ).astype(jnp.float32),
-        lax.psum_scatter(
-            grad_small_weight.astype(jnp.bfloat16), "seq", scatter_dimension=0, tiled=True
-        ).astype(jnp.float32),
-        lax.psum_scatter(
-            grad_out_weight.astype(jnp.bfloat16), "seq", scatter_dimension=0, tiled=True
-        ).astype(jnp.float32),
-        lax.psum_scatter(
-            grad_ffn_in.astype(jnp.bfloat16), "seq", scatter_dimension=0, tiled=True
-        ).astype(jnp.float32),
-        lax.psum_scatter(
-            grad_ffn_out.astype(jnp.bfloat16), "seq", scatter_dimension=0, tiled=True
-        ).astype(jnp.float32),
-    )
-    stored = (
-        lax.psum(stored[0].astype(jnp.bfloat16), "dp").astype(jnp.float32),
-        lax.psum(stored[1].astype(jnp.bfloat16), "dp").astype(jnp.float32),
-        lax.psum(stored[2].astype(jnp.bfloat16), "dp").astype(jnp.float32),
-        lax.psum(stored[3].astype(jnp.bfloat16), "dp").astype(jnp.float32),
-        lax.psum(stored[4].astype(jnp.bfloat16), "dp").astype(jnp.float32),
-    )
-    smalls = lax.psum(
-        (
-            grad_gain_first,
-            grad_gain_second,
-            grad_gain_out,
-            grad_conv,
-            grad_decay_log,
-            grad_decay_bias,
-        ),
-        ("dp", "seq"),
-    )
+    grad_little = jnp.concatenate(
+        [grad_little.reshape(both, 2 * heads), jnp.zeros((2 * PAD, 2 * heads), jnp.float32)], axis=0
+    )
+    rim_part = jnp.concatenate(
+        [
+            jnp.zeros((2, PAD - (CONV - 1), mixed_width), jnp.float32),
+            grad_padded[:, : CONV - 1],
+        ],
+        axis=1,
+    )
+    grad_first = jnp.concatenate(
+        [
+            jnp.concatenate(
+                [
+                    grad_padded[:, CONV - 1 :].reshape(both, mixed_width),
+                    rim_part.reshape(2 * PAD, mixed_width),
+                ],
+                axis=0,
+            ),
+            grad_little,
+            jnp.zeros((both + 2 * PAD, 128 - 2 * heads), jnp.float32),
+        ],
+        axis=1,
+    ).astype(jnp.bfloat16)
+    grad_w_first = dense(normed, grad_first, ((0,), (0,))).astype(jnp.bfloat16)
+    normed_part = dense(grad_first, w_first, ((1,), (1,)))
+    normed_part = jnp.concatenate(
+        [normed_part[:both] + dense(grad_gate_pre, w_gate, ((1,), (1,))), normed_part[both:]], axis=0
+    )
+    grad_gain_first = jnp.sum(normed_part * first_unit, axis=0)
+
+    def place_half(array, start, width, values_):
+        at = array.ndim - 1
+        return lax.dynamic_update_slice_in_dim(array, values_, start + core * width, at)
+
+    all_conv = jnp.zeros(conv_weight.shape, jnp.float32)
+    all_conv = place_half(all_conv, 0, keys, grad_conv[:, :keys])
+    all_conv = place_half(all_conv, KEYS, keys, grad_conv[:, keys : 2 * keys])
+    all_conv = place_half(all_conv, 2 * KEYS, vals, grad_conv[:, 2 * keys :])
+    no_heads = jnp.zeros((HEADS,), jnp.float32)
+    smalls = [
+        grad_gain_first,
+        grad_gain_second,
+        grad_gain_out,
+        all_conv.reshape(-1),
+        place_half(no_heads, 0, heads, grad_decay_log),
+        place_half(no_heads, 0, heads, grad_decay_bias),
+        loss_part[None],
+        jnp.sum(mask_own)[None],
+    ]
+    sizes = [v.shape[0] for v in smalls]
+    extra = -sum(sizes) % 1024
+    packed = jnp.concatenate(smalls + [jnp.zeros((extra,), jnp.float32)]).reshape(-1, 128)
+    total_first, other_first, swap_got, rim_got, small_sum = reduce_first(
+        grad_w_first.reshape(count, rows, first_width),
+        normed_part[length:both].astype(jnp.bfloat16),
+        normed_part[both:].reshape(2, PAD, model).astype(jnp.bfloat16),
+        packed,
+        third(first_width, 0.28),
+    )
+    small_flat = small_sum.reshape(-1)
+    found, start = [], 0
+    for size in sizes:
+        found.append(small_flat[start : start + size])
+        start += size
+    valid_count = jnp.maximum(found[7][0], 1.0)
+    loss_value = found[6][0] / valid_count
+    factor = length * groups * count / valid_count
+
+    rim_rows = jnp.sum(rim_got.astype(jnp.float32), axis=0)
+    grad_normed = normed_part[:length] + swap_got.astype(jnp.float32)
+    grad_normed = jnp.concatenate(
+        [grad_normed[: length - PAD], grad_normed[length - PAD :] + rim_rows], axis=0
+    )
+    grad_tokens = grad_hidden[:length] + norm_back(
+        first_scale[:length], first_unit[:length], gain_first, grad_normed
+    )
+
+    def join(own, other, start, width):
+        own_part, other_part = own[:, start : start + width], other[:, start : start + width]
+        low = jnp.where(core == 0, own_part, other_part)
+        high = jnp.where(core == 0, other_part, own_part)
+        return [low, high]
+
+    def joined(parts):
+        return jnp.concatenate(parts, axis=1).astype(jnp.float32) * factor
+
+    pair_first = (total_first, other_first)
+    pair_down, pair_up, pair_out, pair_gate = ((reduced[i], reduced[4 + i]) for i in range(4))
+    result_in = joined(
+        join(*pair_first, 0, keys)
+        + join(*pair_first, keys, keys)
+        + join(*pair_first, 2 * keys, vals)
+        + join(*pair_gate, 0, vals)
+    )
+    result_small = joined(
+        join(*pair_first, mixed_width, heads) + join(*pair_first, mixed_width + heads, heads)
+    )
+    result_out = joined(join(*pair_out, 0, vals))
+    result_up = joined(join(*pair_up, 0, FF // 2) + join(*pair_up, FF // 2, FF // 2))
+    result_down = joined(join(*pair_down, 0, FF // 2))
     return (
-        summed.astype(jnp.bfloat16)[None],
+        summed[:length].astype(jnp.bfloat16)[None],
         loss_value,
-        grad_tokens[None],
-        stored[0],
-        stored[1],
-        stored[2],
-        stored[3],
-        stored[4],
-        smalls[0],
-        smalls[1],
-        smalls[2],
-        smalls[3],
-        smalls[4],
-        smalls[5],
+        (grad_tokens * factor)[None],
+        result_in,
+        result_small,
+        result_out,
+        result_up,
+        result_down,
+        found[0] * factor,
+        found[1] * factor,
+        found[2] * factor,
+        found[3].reshape(conv_weight.shape) * factor,
+        found[4] * factor,
+        found[5] * factor,
     )
 
 

time: 1230 us -> 760 us (0.62)
  waiting for transfers between devices: 752 us -> 2.2 us
  Pallas kernels: 135 us -> 524 us
  blocking collectives: 118 us -> 0 us
  matrix products: 81.2 us -> 54.5 us
  other arithmetic: 57.3 us -> 80.9 us
  local copies, waits for them, and re-layouts: 60 us -> 79.7 us
  between operations: 18 us -> 4.76 us
    pallas_call x0 -> x4, Pallas kernels: none -> 390 us  [the longest x1 140 us: reduce_rest(): pl.pallas_call(functools.partial(reduce_rest_kernel, groups, count, share...]
    reduce_scatter x4 -> x0, waiting for transfers between devices: 387 us -> none  [the longest x1 195 us: on_device(): lax.psum_scatter(grad_ffn_in.astype(jnp.bfloat16), 'seq', scatter_dimensi...]
    all_gather x4 -> x0, waiting for transfers between devices: 276 us -> none  [the longest x1 129 us: on_device(): lax.all_gather(ffn_in, 'seq', axis=0, tiled=True)]
    psum x3 -> x0, blocking collectives: 91.6 us -> none  [the longest x2 85.9 us: on_device(): lax.psum((jnp.sum(mask_row * jnp.mean(errors * errors, axis=-1)), jnp.sum...]
    psum x1 -> x0, waiting for transfers between devices: 73 us -> none  [on_device(): lax.psum(stored[0].astype(jnp.bfloat16), 'dp').astype(jnp.float32)]
    dot_general x17, matrix products: 81.2 us -> 54.5 us  [the longest x15 49.6 us: dense(): lax.dot_general(left, right, (dims, ((), ())), preferred_element_type=jnp...]
    all_gather x1 -> x0, blocking collectives: 26.5 us -> none  [on_device(): lax.all_gather(small_weight, 'seq', axis=0, tiled=True)]
    unnamed x11 -> x0, waiting for transfers between devices: 14.6 us -> none
  transfers between devices with their start and end apart: 12 -> 3, of which waited for: 9 -> 1; matrix products, arithmetic and copies ran while one was open for 12% -> 2% of each run, Pallas kernels for 11% -> 0%
where the time goes in v2:
time: 760 us; the launch traced here: 747 us
  Pallas kernels  524 us (69%)
  other arithmetic  80.9 us (11%)
  local copies, waits for them, and re-layouts  79.7 us (10%)
  matrix products  54.5 us (7%)
    pallas_call x1, Pallas kernels, reduce_rest(): pl.pallas_call(functools.partial(reduce_rest_kernel, groups, count, share...  140 us
    pallas_call x1, Pallas kernels, gather_rest(): pl.pallas_call(functools.partial(gather_rest_kernel, groups, count, share...  138 us
    pallas_call x1, Pallas kernels, reduce_first(): pl.pallas_call(functools.partial(reduce_first_kernel, groups, count, shar...  64.7 us
    pallas_call x2, Pallas kernels, relay(): pl.pallas_call(functools.partial(relay_kernel, count, ahead), out_shape=j...  56.4 us
    dot_general x15, matrix products, dense(): lax.dot_general(left, right, (dims, ((), ())), preferred_element_type=jnp...  49.6 us
    pallas_call x1, Pallas kernels, gather_first(): pl.pallas_call(functools.partial(gather_first_kernel, groups, count, shar...  47.1 us
    pallas_call x1, Pallas kernels, delta_local(): pl.pallas_call(local_kernel, grid=(seqs, heads), in_specs=[per_head(lengt...  45 us
    pallas_call x1, Pallas kernels, delta_grads(): pl.pallas_call(grads_kernel, grid=(seqs, heads), in_specs=[per_head(lengt...  33.1 us
  transfers between devices with their start and end apart: 3, of which 1 were waited for; matrix products, arithmetic and copies ran while one was open for 2% of the time, Pallas kernels for 0%

profile of v2, /device:TPU:0, one launch (start us, length us, event | category | flops | bytes accessed | tf_op | source)
XLA Modules:
  0.0 746.9 jit_solution(15523782021867078342)
XLA Ops:
  6.9 47.1 %gather_first.1 = (bf16[8,128,1664]{2,1,0:T(8,128)(2,1)}, bf16[256,1024]{1,0:T(8,128)(2,1)}, bf16[256,1024]{1,0:T(8,128)(2,1)}, f32[8,256]{1,0:T(8,128)}, bf16[2,16,1024]{2,1,0:T(8,128)(2,1)}) custom-call(bf16[128,1664]{1,0:T(8,128)(2,1)} %concatenate.68.refs_0_, bf16[256,1024]{1,0:T(8,128)(2,1)} %bitcast.142, bf16[256,1024]{1,0:T(8,128)(2,1)} %bitcast.168, ...), custom_call_target="tpu_custom_call" | custom-call | tf_op jit(solution)/shard_map/gather_first/pallas_call | solution.py:664
  55.4 2.9 broadcast_multiply_fusion.4
  66.1 7.7 %fusion.4 = (f32[2,256,1536]{2,1,0:T(8,128)S(1)}, f32[2,256,1536]{2,1,0:T(8,128)}) fusion(f32[2,256,1536]{2,1,0:T(8,128)} %bitcast.139, f32[1536]{0:T(1024)S(1)} %get-tuple-element.131, f32[2,3,1536]{2,1,0:T(4,128)S(1)} %slice.311, f32[1536]{0:T(1024)S(1)} %get-tuple-element.132, f32[1536]{0:T(1024)S(1)} %get-tuple-element.133, f32[1536]{0:T(1024)S(1)} %get-tuple-element.130), kind=kLoop, calls=%fused_computation.20 | loop fusion | flops 11010048 | bytes 9498624 | tf_op jit(solution)/shard_map/jvp(jit(silu))/mul | solution.py:922
  90.6 45.0 %delta_local.1 = (f32[2,3,256,256]{3,2,1,0:T(8,128)}, f32[2,3,256,256]{3,2,1,0:T(8,128)}, f32[2,3,256,128]{3,2,1,0:T(8,128)S(1)}, f32[2,3,128,128]{3,2,1,0:T(8,1...) custom-call(f32[2,256,384]{2,1,0:T(8,128)S(1)} %get-tuple-element.157.q_ref, ...), custom_call_target="tpu_custom_call" | custom-call | tf_op jit(solution)/shard_map/delta_local/pallas_call | solution.py:123
  135.6 9.2 %relay_ahead.1 = f32[6,128,256]{2,1,0:T(8,128)S(1)} custom-call(f32[6,128,128]{2,1,0:T(8,128)S(1)} %bitcast.136, f32[6,128,256]{2,1,0:T(8,128)S(1)} %bitcast.138), custom_call_target="tpu_custom_call" | custom-call | tf_op jit(solution)/shard_map/relay_ahead/pallas_call | solution.py:310
  147.8 3.0 copy.192
  153.7 138.1 %gather_rest.1 = (bf16[8,128,768]{2,1,0:T(8,128)(2,1)}, bf16[8,128,768]{2,1,0:T(8,128)(2,1)}, bf16[8,128,2816]{2,1,0:T(8,128)(2,1)}, bf16[8,128,1408]{2,1,0:T(8,128)(2,1)}) custom-call(bf16[128,768]{1,0:T(8,128)(2,1)} %get-tuple-element.166.refs_0_, bf16[128,768]{1,0:T(8,128)(2,1)} %get-tuple-element.214.refs_1_, ...), custom_call_target="tpu_custom_call" | custom-call | tf_op jit(solution)/shard_map/gather_rest/pallas_call | solution.py:709
  291.8 2.6 copy.193
  294.4 4.6 multiply_convert_fusion.4
  307.0 3.1 fusion.31
  314.1 3.5 fusion.53
  317.8 2.7 copy.194
  323.4 2.5 convert_subtract_fusion
  327.0 4.2 fusion.32
  331.2 5.1 fusion.54
  337.4 3.6 convolution_convert_fusion.2
  340.9 5.1 convolution_convert_fusion
  350.6 3.3 multiply_reduce_fusion.7
  355.8 3.1 reshape.346
  358.8 3.8 copy.200.do_ref
  362.6 3.3 fusion.13
  365.9 47.3 %relay_back.1 = f32[6,128,256]{2,1,0:T(8,128)S(1)} custom-call(f32[6,128,128]{2,1,0:T(8,128)S(1)} %bitcast.137, f32[6,128,256]{2,1,0:T(8,128)S(1)} %bitcast.134), custom_call_target="tpu_custom_call" | custom-call | tf_op jit(solution)/shard_map/relay_back/pallas_call | solution.py:310
  414.1 33.1 %delta_grads.1 = (f32[2,256,384]{2,1,0:T(8,128)S(1)}, f32[2,256,384]{2,1,0:T(8,128)S(1)}, f32[2,256,768]{2,1,0:T(8,128)}, f32[2,3,256,8]{3,2,1,0:T(8,128)S(1)}, f32[2,3,8,256]{3,2,1,0:T(8,128)S(1)}) custom-call(f32[2,256,384]{2,1,0:T(8,128)S(1)} %get-tuple-element.157.q_ref, f32[2,256,384]{2,1,0:T(8,128)S(1)} %get-tuple-element.156.k_ref, ...), custom_call_target="tpu_custom_call" | custom-call | tf_op jit(solution)/shard_map/delta_grads/pallas_call | solution.py:218
  451.1 2.4 copy.202
  458.0 3.2 add_add_fusion.3
  465.0 2.4 copy.204
  470.0 7.6 %multiply_reduce_fusion.2 = (f32[1536]{0:T(1024)S(1)}, f32[1536]{0:T(1024)}, f32[1536]{0:T(1024)}, f32[1536]{0:T(1024)S(1)}, f32[2,256,1536]{2,1,0:T(8,128)S(1)}) fusion(f32[2,256,1536]{2,1,0:T(8,128)} %bitcast.140, f32[2,3,1536]{2,1,0:T(4,128)S(1)} %copy-done.57, f32[544,1536]{1,0:T(8,128)S(1)} %copy-done.18, f32[2,256,1536]{2,1,0:T(8,128)} %get-tuple-element.146, ...), kind=kLoop, calls=%fused_computation.17 | loop fusion | flops 17295360 | bytes 15790080 | tf_op jit(solution)/shard_map/transpose(jvp())/reduce_sum | solution.py:921
  483.3 8.0 %reduce-window.16 = f32[2,3,2,128]{3,2,1,0:T(2,128)S(1)} reduce-window(f32[2,3,2,128]{3,2,1,0:T(2,128)S(1)} %copy.209, f32[]{:T(128)} %constant.100.clone.1), window={size=1x1x1x128 pad=0_0x0_0x0_0x0_127}, to_apply=%region_11.12 | reduce-window | flops 195072 | bytes 12292 | tf_op jit(solution)/shard_map/reduce-window.2
  495.6 6.1 convolution_convert_fusion.1
  515.0 64.7 %reduce_first.1 = (bf16[128,1664]{1,0:T(8,128)(2,1)}, bf16[128,1664]{1,0:T(8,128)(2,1)}, bf16[256,1024]{1,0:T(8,128)(2,1)}, bf16[2,16,1024]{2,1,0:T(8,128)(2,1)}, f32[120,128]{1,0:T(8,128)}) custom-call(bf16[8,128,1664]{2,1,0:T(8,128)(2,1)} %bitcast.156, bf16[256,1024]{1,0:T(8,128)(2,1)} %slice.468.refs_1_, bf16[2,16,1024]{2,1,0:T(8,128)(2,1)} %bitcast.185, ...), custom_call_target="tpu_custom_call" | custom-call | tf_op jit(solution)/shard_map/reduce_first/pallas_call | solution.py:886
  593.0 139.8 %reduce_rest.1 = (bf16[128,1408]{1,0:T(8,128)(2,1)}, bf16[128,2816]{1,0:T(8,128)(2,1)}, bf16[128,768]{1,0:T(8,128)(2,1)}, bf16[128,768]{1,0:T(8,128)(2,1)}, bf16...) custom-call(bf16[8,128,1408]{2,1,0:T(8,128)(2,1)} %bitcast.166, ...), custom_call_target="tpu_custom_call" | custom-call | tf_op jit(solution)/shard_map/reduce_rest/pallas_call | solution.py:798
  737.5 2.9 fusion.18
  (396 shorter events, 121.2 us)
Async XLA Ops:
  0.6 152.3 %copy-start = (bf16[128,2816]{1,0:T(8,128)(2,1)S(1)}, bf16[128,2816]{1,0:T(8,128)(2,1)}, u32[]{:S(2)}) copy-start(bf16[128,2816]{1,0:T(8,128)(2,1)} %param.21) | copy-start | bytes 2162692
  0.7 53.3 %copy-start.19 = (bf16[1,256,1024]{2,1,0:T(8,128)(2,1)S(1)}, bf16[1,256,1024]{2,1,0:T(8,128)(2,1)}, u32[]{:S(2)}) copy-start(bf16[1,256,1024]{2,1,0:T(8,128)(2,1)} %param.14) | copy-start | bytes 1572868
  2.5 51.4 %copy-start.78 = (f32[1,256]{1,0:T(1,128)}, f32[1,256]{1,0:T(1,128)S(1)}, u32[]{:S(2)}) copy-start(f32[1,256]{1,0:T(1,128)S(1)} %convert_element_type.109) | copy-start | bytes 3076
  3.4 51.9 %copy-start.72 = (f32[1024]{0:T(1024)S(1)}, f32[1024]{0:T(1024)}, u32[]{:S(2)}) copy-start(f32[1024]{0:T(1024)} %param.22) | copy-start | bytes 12292
  66.1 7.7 %copy-start.56 = (f32[2,3,1536]{2,1,0:T(4,128)}, f32[2,3,1536]{2,1,0:T(4,128)S(1)}, u32[]{:S(2)}) copy-start(f32[2,3,1536]{2,1,0:T(4,128)S(1)} %slice.311) | copy-start | bytes 110596
  85.2 4.9 copy-start.64
  90.6 45.1 %copy-start.3 = (f32[2,3,256,8]{3,2,1,0:T(8,128)}, f32[2,3,256,8]{3,2,1,0:T(8,128)S(1)}, u32[]{:S(2)}) copy-start(f32[2,3,256,8]{3,2,1,0:T(8,128)S(1)} %maximum_maximum_fusion.cols_ref) | copy-start | bytes 147460
  135.6 10.8 %copy-start.5 = (f32[2,3,256,128]{3,2,1,0:T(8,128)}, f32[2,3,256,128]{3,2,1,0:T(8,128)S(1)}, u32[]{:S(2)}) copy-start(f32[2,3,256,128]{3,2,1,0:T(8,128)S(1)} %get-tuple-element.52) | copy-start | bytes 2359300
  135.6 10.8 %copy-start.12 = (f32[2,3,256,128]{3,2,1,0:T(8,128)}, f32[2,3,256,128]{3,2,1,0:T(8,128)S(1)}, u32[]{:S(2)}) copy-start(f32[2,3,256,128]{3,2,1,0:T(8,128)S(1)} %get-tuple-element.61.w_ref) | copy-start | bytes 2359300
  135.6 9.2 %copy-start.43 = (f32[2,3,256,256]{3,2,1,0:T(8,128)S(1)}, f32[2,3,256,256]{3,2,1,0:T(8,128)}, u32[]{:S(2)}) copy-start(f32[2,3,256,256]{3,2,1,0:T(8,128)} %get-tuple-element.51) | copy-start | bytes 4718596
  153.7 140.7 %copy-start.87 = (f32[256]{0:T(256)S(1)}, f32[256]{0:T(256)}, u32[]{:S(2)}) copy-start(f32[256]{0:T(256)} %param.24) | copy-start | bytes 3076
  300.1 2.7 collective-permute-start
  304.6 5.5 copy-start.31
  317.6 4.3 collective-permute-start.1
  317.8 5.6 copy-start.37
  317.8 5.6 copy-start.55
  321.9 5.0 slice-start
  325.9 5.2 slice-start.5
  331.2 6.2 copy-start.45
  336.3 9.7 %collective-permute-start.2 = (bf16[512,1024]{1,0:T(8,128)(2,1)S(1)}, bf16[512,1024]{1,0:T(8,128)(2,1)S(1)}, u32[]{:S(2)}, u32[]{:S(2)}) collective-permute-start(bf16[512,1024]{1,0:T(8,128)(2,1)S(1)} %get-tuple-element.211), channel_id=1, source_target_pairs={{0,8},{8,0},{16,24},{24,16},{1,9},{9,1},{17,25},{25,17},{2,10},{10... | collective-permute-start | bytes 3145736 | tf_op jit(solution)/shard_map/ppermute | solution.py:1053
  348.0 5.9 copy-start.29
  362.6 51.5 %copy-start.4 = (f32[2,3,256,8]{3,2,1,0:T(8,128)S(1)}, f32[2,3,256,8]{3,2,1,0:T(8,128)}, u32[]{:S(2)}) copy-start(f32[2,3,256,8]{3,2,1,0:T(8,128)} %copy-done.3) | copy-start | bytes 147460
  362.6 51.5 %copy-start.13 = (f32[2,3,256,128]{3,2,1,0:T(8,128)S(1)}, f32[2,3,256,128]{3,2,1,0:T(8,128)}, u32[]{:S(2)}) copy-start(f32[2,3,256,128]{3,2,1,0:T(8,128)} %copy-done.12) | copy-start | bytes 2359300
  449.0 5.7 copy-start.63
  451.1 6.9 copy-start.8
  451.1 6.9 copy-start.10
  482.4 9.2 %copy-start.69 = (f32[2,256,3]{1,0,2:T(2,128)S(1)}, f32[2,256,3]{1,0,2:T(2,128)}, u32[]{:S(2)}) copy-start(f32[2,256,3]{1,0,2:T(2,128)} %copy-done.68) | copy-start | bytes 18436
  482.4 9.2 %copy-start.76 = (f32[2,256,3]{1,0,2:T(2,128)S(1)}, f32[2,256,3]{1,0,2:T(2,128)}, u32[]{:S(2)}) copy-start(f32[2,256,3]{1,0,2:T(2,128)} %get-tuple-element.144) | copy-start | bytes 18436
  482.4 9.2 %copy-start.82 = (f32[3]{0:T(128)S(1)}, f32[3]{0:T(128)}, u32[]{:S(2)}) copy-start(f32[3]{0:T(128)} %copy-done.81) | copy-start | bytes 40
  482.4 9.2 %copy-start.84 = (f32[3]{0:T(128)S(1)}, f32[3]{0:T(128)}, u32[]{:S(2)}) copy-start(f32[3]{0:T(128)} %copy-done.83) | copy-start | bytes 40
  495.6 6.1 copy-start.38
  495.6 6.2 copy-start.91
  (74 other events, 182.9 us)

commit v3 on v2

v3 whole, which is shorter than its diff:
```python
import functools

import jax
import jax.numpy as jnp
from jax import lax
from jax.experimental import pallas as pl
from jax.experimental.pallas import tpu as pltpu
from jax.sharding import PartitionSpec as P

HEADS = 6
DK = 128
DV = 256
FF = 2816
CONV = 4
BLOCK = 64
KEYS = 768
VALUES = 1536


precise = lax.Precision.HIGHEST
epsilon = 1e-06


MESH = pl.DeviceIdType.MESH
NN = (((1,), (0,)), ((), ()))
NT = (((1,), (1,)), ((), ()))
TN = (((0,), (0,)), ((), ()))


def exact(left, right, dims=NN):
    return lax.dot_general(
        left, right, dims, precision=precise, preferred_element_type=jnp.float32
    )


def near(left, right, dims=NN):
    return lax.dot_general(
        left.astype(jnp.bfloat16),
        right.astype(jnp.bfloat16),
        dims,
        preferred_element_type=jnp.float32,
    )


def close(left, right, dims=NN):
    left_top, right_top = left.astype(jnp.bfloat16), right.astype(jnp.bfloat16)
    left_rest = (left - left_top.astype(jnp.float32)).astype(jnp.bfloat16)
    right_rest = (right - right_top.astype(jnp.float32)).astype(jnp.bfloat16)
    return (
        near(left_rest, right_top, dims) + near(left_top, right_rest, dims)
    ) + near(left_top, right_top, dims)


def iotas(rows, columns):
    return (
        lax.broadcasted_iota(jnp.int32, (rows, columns), 0),
        lax.broadcasted_iota(jnp.int32, (rows, columns), 1),
    )


def decay_table(gcol, grow):
    size = gcol.shape[0]
    row, col = iotas(size, size)
    keep = row >= col
    return jnp.where(keep, jnp.exp(jnp.where(keep, gcol - grow, 0.0)), 0.0)


def tile_start(start):
    return pl.multiple_of(start, 128)


class Place:
    def __init__(self, groups, count):
        self.groups, self.count, self.half = groups, count, count // 2
        self.group, self.place = lax.axis_index("dp"), lax.axis_index("seq")
        self.pair, self.side = self.place // 2, self.place % 2
        self.plane = (self.group // 2) % 2
        self.group_swap = self.group + 1 - 2 * (self.group % 2)
        self.across = self.group + 2 - 4 * self.plane
        self.beside = self.place + 1 - 2 * self.side

    def shard(self, pair, side):
        return 2 * pair + side

    def ahead(self, step):
        return lax.rem(self.pair + step, self.half)

    def behind(self, step):
        return lax.rem(self.pair + self.half - step, self.half)

    def partners(self):
        along = [(self.group, self.shard(self.ahead(step), self.side)) for step in range(1, self.half)]
        return along + [(self.group, self.beside), (self.across, self.place)]


def greet(signalled, awaited):
    barrier = pltpu.get_barrier_semaphore()
    for device in signalled:
        pl.semaphore_signal(barrier, inc=1, device_id=device, device_id_type=MESH)
    pl.semaphore_wait(barrier, awaited)


def remote(source, target, sends, receives, index, device):
    return pltpu.make_async_remote_copy(
        src_ref=source,
        dst_ref=target,
        send_sem=sends.at[index],
        recv_sem=receives.at[index],
        device_id=device,
        device_id_type=MESH,
    )


class Gather:
    def __init__(self, at, source, target, lines, share, sends, receives, local):
        self.at, self.source, self.target, self.lines = at, source, target, lines
        self.sends, self.receives, self.local = sends, receives, local
        width = source.shape[1]
        self.own = pl.ds(tile_start(at.plane * share), width - share)
        self.lent = pl.ds(tile_start(at.plane * (width - share)), share)
        self.borrowed = pl.ds(tile_start((1 - at.plane) * (width - share)), share)
        self.started = {}

    def copy(self, index, shard, columns, device, from_source=False):
        there = self.target.at[shard, self.lines, columns]
        here = self.source.at[self.lines, columns] if from_source else there
        return remote(here, there, self.sends, self.receives, index, device)

    def along(self, step):
        at = self.at
        device = (at.group, at.shard(at.ahead(step), at.side))
        return self.copy(step - 1, at.place, self.own, device, True)

    def beside(self, step):
        at = self.at
        shard = at.shard(at.behind(step), at.side)
        return self.copy(at.half - 1 + step, shard, self.own, (at.group, at.beside), step == 0)

    def across(self, step, side):
        at = self.at
        shard = at.shard(at.behind(step), at.side if side == 0 else 1 - at.side)
        return self.copy(2 * at.half - 1 + 2 * step + side - 1, shard, self.lent, (at.across, at.place))

    def keep(self):
        return pltpu.make_async_copy(
            self.source.at[self.lines], self.target.at[self.at.place, self.lines], self.local
        )

    def launch(self, make, *where):
        make(*where).start()
        self.started[make.__name__, where] = make

    def begin(self):
        self.keep().start()
        for step in range(1, self.at.half):
            self.launch(self.along, step)
        self.launch(self.beside, 0)

    def arrived(self, index, shard, columns):
        self.copy(index, shard, columns, (self.at.group, self.at.place)).wait_recv()

    def pass_along(self, step):
        at = self.at
        self.arrived(step - 1, at.shard(at.behind(step), at.side), self.own)
        self.launch(self.beside, step)
        self.launch(self.across, step, 0)

    def pass_beside(self, step):
        at = self.at
        self.arrived(at.half - 1 + step, at.shard(at.behind(step), 1 - at.side), self.own)
        self.launch(self.across, step, 1)

    def finish(self):
        at = self.at
        for step in range(at.half):
            for side in range(2):
                if step or side:
                    shard = at.shard(at.behind(step), at.side if side == 0 else 1 - at.side)
                    self.arrived(2 * at.half - 1 + 2 * step + side - 1, shard, self.borrowed)
        for (unused, where), make in self.started.items():
            make(*where).wait_send()
        self.keep().wait()

    def stages(self):
        half = self.at.half
        first = [functools.partial(self.pass_along, step) for step in range(1, half)]
        second = [functools.partial(self.pass_beside, step) for step in range(half)]
        return first, second


def copies_of_gather(count):
    return 2 * count - 2


def lagged(plans):
    depth = max(len(plan) for plan in plans)
    turns = []
    for turn in range(len(plans) + depth - 1):
        steps = []
        for index, plan in enumerate(plans):
            if 0 <= turn - index < len(plan):
                steps = plan[turn - index] + steps
        turns.append(steps)
    return turns


class Reduce:
    def __init__(self, at, given, total, other, lines, share, buffers, sems):
        self.at, self.given, self.total, self.other = at, given, total, other
        self.lines, self.share = lines, share
        self.acc, self.from_across, self.from_beside, self.from_along, self.part, self.from_plane, self.far = buffers
        self.sends, self.receives, self.local = sems
        width = total.shape[1]
        self.wide = width - share
        self.own = pl.ds(tile_start(at.plane * share), self.wide)
        self.lent = pl.ds(tile_start((1 - at.plane) * self.wide), share)
        self.inner = pl.ds(tile_start(at.plane * (width - 2 * share)), share)
        self.theirs = pl.ds(tile_start((1 - at.plane) * share), self.wide)
        self.started = {}

    def launch(self, make, *where):
        make(*where).start()
        self.started[make.__name__, where] = make

    def side(self, mine):
        return self.at.side if mine else 1 - self.at.side

    def across(self, mine):
        at = self.at
        return remote(
            self.given.at[:, self.side(mine), self.lines, self.lent], self.from_across.at[mine],
            self.sends, self.receives, mine, (at.across, at.place),
        )

    def load(self, mine):
        return pltpu.make_async_copy(
            self.given.at[:, self.side(mine), self.lines, self.own], self.acc.at[mine],
            self.local.at[mine],
        )

    def beside(self):
        at = self.at
        return remote(
            self.acc.at[0], self.from_beside, self.sends, self.receives, 2, (at.group, at.beside)
        )

    def along(self, step):
        at = self.at
        pair = at.ahead(step)
        return remote(
            self.acc.at[1, pair], self.from_along.at[step - 1],
            self.sends, self.receives, 4 + step, (at.group, at.shard(pair, at.side)),
        )

    def plane(self):
        at = self.at
        return remote(
            self.part, self.from_plane, self.sends, self.receives, 3, (at.across, at.place)
        )

    def core(self):
        at = self.at
        return remote(
            self.total.at[self.lines], self.other.at[self.lines], self.sends, self.receives,
            4, (at.group_swap, at.place),
        )

    def further(self, index, distance):
        at = self.at
        group = at.group + distance - 2 * distance * ((at.group // distance) % 2)
        return remote(
            self.total.at[self.lines], self.far.at[index], self.sends, self.receives,
            4 + at.half + index, (group, at.place),
        )

    def begin(self):
        for mine in range(2):
            self.load(mine).start()
            self.launch(self.across, mine)

    def add_across(self, mine):
        self.load(mine).wait()
        self.across(mine).wait_recv()
        held = self.acc[mine, :, :, self.inner].astype(jnp.float32)
        got = self.from_across[mine].astype(jnp.float32)
        self.acc[mine, :, :, self.inner] = (held + got).astype(jnp.bfloat16)
        if not mine:
            self.launch(self.beside)

    def add_beside(self):
        self.beside().wait_recv()
        for step in range(1, self.at.half + 1):
            pair = self.at.ahead(step)
            held = self.acc[1, pair].astype(jnp.float32)
            got = self.from_beside[pair].astype(jnp.float32)
            self.acc[1, pair] = (held + got).astype(jnp.bfloat16)
            if step < self.at.half:
                self.launch(self.along, step)

    def add_along(self):
        value = self.acc[1, self.at.pair].astype(jnp.float32)
        for step in range(1, self.at.half):
            self.along(step).wait_recv()
            value = value + self.from_along[step - 1].astype(jnp.float32)
        self.part[...] = value.astype(jnp.bfloat16)
        self.launch(self.plane)

    def add_plane(self):
        self.plane().wait_recv()
        height = self.part.shape[0]
        self.total[self.lines] = jnp.zeros((height, self.total.shape[1]), jnp.bfloat16)
        self.total[self.lines, self.own] = self.part[...]
        held = self.total[self.lines, self.theirs].astype(jnp.float32)
        got = self.from_plane[...].astype(jnp.float32)
        self.total[self.lines, self.theirs] = (held + got).astype(jnp.bfloat16)
        distance = 4
        while distance < self.at.groups:
            index = distance.bit_length() - 3
            copy = self.further(index, distance)
            copy.start()
            copy.wait()
            got = self.far[index].astype(jnp.float32)
            value = self.total[self.lines].astype(jnp.float32) + got
            self.total[self.lines] = value.astype(jnp.bfloat16)
            distance *= 2
        self.launch(self.core)

    def finish(self):
        self.core().wait_recv()
        for (unused, where), make in self.started.items():
            make(*where).wait_send()

    def stages(self):
        return [
            [functools.partial(self.add_across, 0)],
            [functools.partial(self.add_across, 1), self.add_beside],
            [self.add_along],
            [self.add_plane],
        ]


ANY = pl.BlockSpec(memory_space=pl.ANY)
ROOM = pl.BlockSpec(memory_space=pltpu.VMEM)
PAD = 16
CHUNKS, WINDOW = 4, 2
REDUCE_CHUNKS, REDUCE_WINDOW = 4, 2


def neighbours(at, step):
    place = lax.rem(at.place + at.count + step, at.count)
    return (at.group, place), (at.group_swap, place)


def chunks_of(rows):
    return max(1, min(CHUNKS, rows // 16))


def gather_sems(count, rows, number):
    chunks = chunks_of(rows)
    return [
        pltpu.SemaphoreType.DMA((number * chunks, copies_of_gather(count))),
        pltpu.SemaphoreType.DMA((number * chunks, copies_of_gather(count))),
        pltpu.SemaphoreType.DMA((number * chunks,)),
    ]


def gather_plans(at, sources, targets, shares, sends, receives, local):
    rows = sources[0].shape[0]
    chunks = chunks_of(rows)
    lines = rows // chunks
    return [
        Gather(
            at, sources[i], targets[i], pl.ds(part * lines, lines), shares[i],
            sends.at[i * chunks + part], receives.at[i * chunks + part], local.at[i * chunks + part],
        )
        for i in range(len(sources))
        for part in range(chunks)
    ]


def gather_steps(plans):
    steps = [plan.begin for plan in plans[:WINDOW]]
    for index, turn in enumerate(lagged([plan.stages() for plan in plans])):
        steps += turn
        if index + WINDOW < len(plans):
            steps.append(plans[index + WINDOW].begin)
    return steps + [plan.finish for plan in plans]


def reduce_steps(plans):
    steps = [plan.begin for plan in plans[:REDUCE_WINDOW]]
    for index, turn in enumerate(lagged([plan.stages() for plan in plans])):
        steps += turn
        if index + REDUCE_WINDOW < len(plans):
            steps.append(plans[index + REDUCE_WINDOW].begin)
    return steps + [plan.finish for plan in plans]


def gather_first_kernel(groups, count, share, *refs):
    source, tokens, target, mask = refs[:4]
    gathered, tokens_other, target_other, mask_other, rim = refs[4:9]
    sends, receives, local, swap_send, swap_recv = refs[9:]
    at = Place(groups, count)
    core = (at.group_swap, at.place)
    greet(at.partners() + [core] + list(neighbours(at, -1)), count // 2 + 4)
    swaps = [
        remote(here, there, swap_send, swap_recv, index, core)
        for index, (here, there) in enumerate(
            ((tokens, tokens_other), (target, target_other), (mask, mask_other))
        )
    ]
    length = tokens.shape[0]
    tail = tokens.at[pl.ds(length - PAD, PAD)]
    own_next, swap_next = neighbours(at, 1)
    rims = [
        remote(tail, rim.at[0], swap_send, swap_recv, 3, own_next),
        remote(tail, rim.at[1], swap_send, swap_recv, 4, swap_next),
    ]
    plans = gather_plans(at, [source], [gathered], [share], sends, receives, local)

    @pl.when(at.place < count - 1)
    def _():
        for copy in rims:
            copy.start()

    for copy in swaps:
        copy.start()
    for step in gather_steps(plans):
        step()
    for copy in swaps:
        copy.wait()

    @pl.when(at.place == 0)
    def _():
        rim[...] = jnp.zeros_like(rim)

    @pl.when(at.place > 0)
    def _():
        for copy in rims:
            copy.wait_recv()

    @pl.when(at.place < count - 1)
    def _():
        for copy in rims:
            copy.wait_send()


def gather_first(source, tokens, target, mask, share):
    groups, count = lax.axis_size("dp"), lax.axis_size("seq")
    rows, width = source.shape
    return pl.pallas_call(
        functools.partial(gather_first_kernel, groups, count, share),
        out_shape=[
            jax.ShapeDtypeStruct((count, rows, width), source.dtype),
            jax.ShapeDtypeStruct(tokens.shape, tokens.dtype),
            jax.ShapeDtypeStruct(target.shape, target.dtype),
            jax.ShapeDtypeStruct(mask.shape, mask.dtype),
            jax.ShapeDtypeStruct((2, PAD, tokens.shape[1]), tokens.dtype),
        ],
        in_specs=[ANY] * 4,
        out_specs=[ANY] * 4 + [ROOM],
        scratch_shapes=[
            *gather_sems(count, rows, 1),
            pltpu.SemaphoreType.DMA((5,)),
            pltpu.SemaphoreType.DMA((5,)),
        ],
        compiler_params=pltpu.CompilerParams(collective_id=3, has_side_effects=True),
        name="gather_first",
    )(source, tokens, target, mask)


def reduce_buffers(groups, count, rows, width, share):
    wide, half = width - share, count // 2
    steps = max(1, (groups // 4).bit_length() - 1)
    kind = jnp.bfloat16
    return [
        pltpu.VMEM((2, half, rows, wide), kind),
        pltpu.VMEM((2, half, rows, share), kind),
        pltpu.VMEM((half, rows, wide), kind),
        pltpu.VMEM((half - 1, rows, wide), kind),
        pltpu.VMEM((rows, wide), kind),
        pltpu.VMEM((rows, wide), kind),
        pltpu.VMEM((steps, rows, width), kind),
    ]


def copies_of_reduce(groups, count):
    return count // 2 + 4 + max(1, (groups // 4).bit_length() - 1)


def further_groups(at):
    found, distance = [], 4
    while distance < at.groups:
        found.append((at.group + distance - 2 * distance * ((at.group // distance) % 2), at.place))
        distance *= 2
    return found


def reduce_plans(at, givens, totals, others, shares, scratch):
    number, rows = len(shares), givens[0].shape[2]
    chunks = reduce_chunks(rows)
    lines = rows // chunks
    sends, receives, local = scratch[7 * number * chunks : 7 * number * chunks + 3]
    plans = []
    for i in range(number):
        for part in range(chunks):
            spot = i * chunks + part
            plans.append(
                Reduce(
                    at, givens[i], totals[i], others[i], pl.ds(part * lines, lines), shares[i],
                    scratch[7 * spot : 7 * spot + 7],
                    (sends.at[spot], receives.at[spot], local.at[spot]),
                )
            )
    return plans


def reduce_chunks(rows):
    return max(1, min(REDUCE_CHUNKS, rows // 16))


def reduce_scratch(groups, count, rows, widths, shares):
    scratch, chunks = [], reduce_chunks(rows)
    for width, share in zip(widths, shares):
        scratch += reduce_buffers(groups, count, rows // chunks, width, share) * chunks
    number, copies = len(widths) * chunks, copies_of_reduce(groups, count)
    return scratch + [
        pltpu.SemaphoreType.DMA((number, copies)),
        pltpu.SemaphoreType.DMA((number, copies)),
        pltpu.SemaphoreType.DMA((number, 2)),
    ]


class Relay:
    def __init__(self, at, forward, units, sending, arriving, sends, receives):
        self.at, self.units = at, units
        self.sending, self.arriving, self.sends, self.receives = sending, arriving, sends, receives
        last = at.count - 1
        step = 1 if forward else -1
        self.is_first = at.place == (0 if forward else last)
        self.is_last = at.place == (last if forward else 0)
        self.beyond = (at.group, lax.rem(at.place + at.count + step, at.count))
        self.before = (at.group, lax.rem(at.place + at.count - step, at.count))

    def copy(self, unit):
        return remote(
            self.sending.at[unit], self.arriving.at[unit], self.sends, self.receives, unit, self.beyond
        )

    def receive(self, unit, target):
        @pl.when(self.is_first)
        def _():
            target[unit] = jnp.zeros(target.shape[1:], jnp.float32)

        @pl.when(jnp.logical_not(self.is_first))
        def _():
            self.copy(unit).wait_recv()
            target[unit] = self.arriving[unit].astype(jnp.float32)

    def send(self, unit, value):
        @pl.when(jnp.logical_not(self.is_last))
        def _():
            self.sending[unit] = value().astype(jnp.bfloat16)
            self.copy(unit).start()

    def finish(self):
        @pl.when(jnp.logical_not(self.is_last))
        def _():
            for unit in range(self.units):
                self.copy(unit).wait_send()


def relay_scratch(units):
    return [
        pltpu.VMEM((units, DK, DV), jnp.bfloat16),
        pltpu.VMEM((units, DK, DV), jnp.bfloat16),
        pltpu.SemaphoreType.DMA((units,)),
        pltpu.SemaphoreType.DMA((units,)),
    ]


class Agenda:
    def __init__(self, steps):
        self.steps, self.done = steps, 0

    def take(self, upto):
        upto = max(upto, self.done)
        found, self.done = self.steps[self.done : upto], upto
        return found

    def until(self, share):
        for step in self.take(int(len(self.steps) * share)):
            step()

    def pieces(self, number, share):
        found = self.take(int(len(self.steps) * share))
        cuts = [len(found) * i // number for i in range(number + 1)]
        return [found[low:high] for low, high in zip(cuts, cuts[1:])]

    def loop(self, rounds, end, stage):
        pieces = self.pieces(rounds * PAUSES, end)
        taken = []

        def body(index, carry):
            for pause, unused in enumerate(stage(index)):
                taken.append(pause)
                for other in range(rounds):
                    found = pieces[other * PAUSES + pause]
                    if found:
                        pl.when(index == other)(functools.partial(run_steps, found))
            return carry

        lax.fori_loop(0, rounds, body, 0)
        assert len(taken) == PAUSES

    def around(self, count, turn, end, main):
        pieces = self.pieces(count, end)
        for index, found in enumerate(pieces):
            if found:
                pl.when(turn > index)(functools.partial(run_steps, found))
        main()
        for index, found in enumerate(pieces):
            if found:
                pl.when(turn <= index)(functools.partial(run_steps, found))


def run_steps(steps):
    for step in steps:
        step()


PAUSES = 9


def lockstep(stages):
    for unused in zip(*stages):
        yield


def rolled(value, shift):
    shift = shift % value.shape[0]
    return value if shift == 0 else pltpu.roll(value, shift, 0)


def silu_parts(value):
    gate = jax.nn.sigmoid(value)
    return value * gate, gate * (1.0 + value * (1.0 - gate))


class Unit:
    def __init__(self, seq, head, heads, mixed_ref, conv_ref):
        self.seq, self.head = seq, head
        self.mixed_ref, self.conv_ref = mixed_ref, conv_ref
        keys = heads * DK
        self.columns = [
            (self.head * DK, DK),
            (keys + self.head * DK, DK),
            (2 * keys + self.head * DV, DV),
        ]

    def taps(self, part):
        start, width = self.columns[part]
        span = pl.ds(start, width)
        field = self.mixed_ref[self.seq, :, span].astype(jnp.float32)
        weights = self.conv_ref[:, span]
        shifts = [rolled(field, CONV - 1 - tap)[PAD:] for tap in range(CONV)]
        value = weights[0:1] * shifts[0]
        for tap in range(1, CONV):
            value = value + weights[tap : tap + 1] * shifts[tap]
        return shifts, weights, value

    def rows(self, part):
        value = self.taps(part)[2]
        active = value * jax.nn.sigmoid(value)
        if part == 2:
            return active
        unit = active * lax.rsqrt(jnp.sum(active * active, axis=1, keepdims=True) + epsilon)
        return unit * DK ** (-0.5) if part == 0 else unit

    def taps_back(self, part, grad, grad_ref, conv_grad_ref):
        shifts, weights, value = self.taps(part)
        active, slope = silu_parts(value)
        if part < 2:
            scale = lax.rsqrt(jnp.sum(active * active, axis=1, keepdims=True) + epsilon)
            unit = active * scale
            grad = grad * DK ** (-0.5) if part == 0 else grad
            grad = scale * (grad - unit * jnp.sum(grad * unit, axis=1, keepdims=True))
        grad = grad * slope
        start, width = self.columns[part]
        span = pl.ds(start, width)
        row = lax.broadcasted_iota(jnp.int32, (8, width), 0)
        taps = jnp.zeros((8, width), jnp.float32)
        longer = jnp.concatenate([jnp.zeros((PAD, width), jnp.float32), grad], axis=0)
        total = jnp.zeros(longer.shape, jnp.float32)
        for tap in range(CONV):
            taps = taps + jnp.where(row == tap, jnp.sum(grad * shifts[tap], axis=0, keepdims=True), 0.0)
            total = total + weights[tap : tap + 1] * rolled(longer, tap - (CONV - 1))
        grad_ref[self.seq, :, span] = total.astype(jnp.bfloat16)
        conv_grad_ref[:, span] += taps


def head_tables(little_ref, head_ref, g_ref, grow_ref):
    seqs, size = little_ref.shape[0], g_ref.shape[1]
    row, col = iotas(size, size)
    below = (row >= col).astype(jnp.float32)
    above = (row <= col).astype(jnp.float32)
    for seq in range(seqs):
        forget = head_ref[0:1] * jax.nn.softplus(little_ref[seq, PAD:, :] + head_ref[1:2])
        g_ref[seq] = exact(below, forget)
        grow_ref[seq] = exact(forget, above, TN)


def head_columns(seq, head, heads, little_ref, g_ref, grow_ref):
    size = g_ref.shape[1]
    lane = lax.broadcasted_iota(jnp.int32, (size, 128), 1)
    line = lax.broadcasted_iota(jnp.int32, (128, size), 0)

    def column(table, index):
        return jnp.sum(jnp.where(lane == index, table, 0.0), axis=1, keepdims=True)

    beta = column(jax.nn.sigmoid(little_ref[seq, PAD:, :]), head)
    gcol = column(g_ref[seq], heads + head)
    grow = jnp.sum(jnp.where(line == heads + head, grow_ref[seq], 0.0), axis=0, keepdims=True)
    return beta, gcol, grow


def merged(inverses, systems, width):
    size = systems[0].shape[0]
    row, col = iotas(size, size)
    joined = (row // (2 * width) == col // (2 * width)) & (row // width != col // width)
    inner = [close(jnp.where(joined, system, 0.0), inverse) for system, inverse in zip(systems, inverses)]
    return [inverse - close(inverse, value) for inverse, value in zip(inverses, inner)]


def forward_kernel(groups, count, shares, *refs):
    number = len(shares)
    mixed_ref, little_ref, gate_ref, conv_ref, head_ref, gain_ref = refs[:6]
    sources, refs = refs[6 : 6 + number], refs[6 + number :]
    branch_ref, out_ref, t_ref, u_ref, w_ref, m_ref, e_ref, s_ref = refs[:8]
    targets, refs = refs[8 : 8 + number], refs[8 + number :]
    b_ref, g_ref, grow_ref, sending, arriving, relay_send, relay_recv = refs[:7]
    sends, receives, local = refs[7:]
    units = t_ref.shape[0]
    heads = units // 2
    size = t_ref.shape[1]
    half = size // 2
    at = Place(groups, count)
    line = Relay(at, True, units, sending, arriving, relay_send, relay_recv)
    greet(at.partners() + [line.before], count // 2 + 2)
    agenda = Agenda(gather_steps(gather_plans(at, sources, targets, shares, sends, receives, local)))
    for step in agenda.take(WINDOW):
        step()
    head_tables(little_ref, head_ref, g_ref, grow_ref)

    def local_stage(seq, head):
        unit = seq * heads + head
        own = Unit(seq, head, heads, mixed_ref, conv_ref)
        beta, gcol, grow = head_columns(seq, head, heads, little_ref, g_ref, grow_ref)
        decays = decay_table(gcol, grow)
        keys = own.rows(1)
        row, col = iotas(size, size)
        system = jnp.where(row > col, beta * close(keys, keys, NT) * decays, 0.0)
        yield
        systems = [system[:half, :half], system[half:, half:]]
        row, col = iotas(half, half)
        inverses = [
            (row == col).astype(jnp.float32) - jnp.where(row // 2 == col // 2, value, 0.0)
            for value in systems
        ]
        width = 2
        while width < half:
            inverses = merged(inverses, systems, width)
            width *= 2
            yield
        corner = -close(inverses[1], close(system[half:, :half], inverses[0]))
        t_ref[unit, :half, :half] = inverses[0]
        t_ref[unit, :half, half:] = jnp.zeros((half, half), jnp.float32)
        t_ref[unit, half:, :half] = corner
        t_ref[unit, half:, half:] = inverses[1]
        solve = t_ref[unit]
        growth = jnp.exp(gcol)
        last = gcol[size - 1 :, :]
        update = near(solve, beta * own.rows(2))
        back = near(solve, (beta * growth) * keys)
        u_ref[unit] = update
        w_ref[unit] = back
        yield
        weighted = keys * jnp.exp(last - gcol)
        drow, dcol = iotas(DK, DK)
        m_ref[unit] = jnp.where(drow == dcol, jnp.exp(last), 0.0) - near(weighted, back, TN)
        b_ref[unit] = near(weighted, update, TN)
        queries = own.rows(0)
        scores = near(queries, keys, NT) * decays
        out_ref[unit] = near(scores, update)
        e_ref[unit] = growth * queries - near(scores, back)
        yield

    agenda.loop(2, FORWARD_LOCAL, lambda seq: lockstep([local_stage(seq, h) for h in range(heads)]))

    def pass_on():
        for unit in range(units):
            line.receive(unit, s_ref)
            line.send(unit, lambda: close(m_ref[unit], s_ref[unit]) + b_ref[unit])

    agenda.around(count, at.place, FORWARD_RELAY, pass_on)

    def read_stage(seq, head):
        unit = seq * heads + head
        value = out_ref[unit] + near(e_ref[unit], s_ref[unit])
        out_ref[unit] = value
        span = pl.ds(head * DV, DV)
        scale = lax.rsqrt(jnp.mean(value * value, axis=1, keepdims=True) + epsilon)
        gate = gate_ref[seq, PAD:, span]
        branch = value * scale * gain_ref[...] * (gate * jax.nn.sigmoid(gate))
        branch_ref[seq, :, span] = branch.astype(jnp.bfloat16)

    for seq in range(2):
        for head in range(heads):
            read_stage(seq, head)
            agenda.until(
                FORWARD_RELAY + (1.0 - FORWARD_RELAY) * (seq * heads + head + 1) / units * 0.6
            )
    agenda.until(1.0)
    line.finish()


FORWARD_LOCAL, FORWARD_RELAY = 0.5, 0.8
BACK_OPEN, BACK_RELAY, BACK_GRADS = 0.15, 0.45, 0.85


def forward_block(mixed_in, little, gate_pre, conv, head, gain, sources, shares):
    groups, count = lax.axis_size("dp"), lax.axis_size("seq")
    number, rows = len(sources), sources[0].shape[0]
    length = mixed_in.shape[1] - PAD
    heads = conv.shape[1] // (2 * DK + DV)
    units = 2 * heads

    def table(*shape):
        return jax.ShapeDtypeStruct((units,) + shape, jnp.float32)

    return pl.pallas_call(
        functools.partial(forward_kernel, groups, count, shares),
        out_shape=[
            jax.ShapeDtypeStruct((2, length, heads * DV), jnp.bfloat16),
            table(length, DV),
            table(length, length),
            table(length, DV),
            table(length, DK),
            table(DK, DK),
            table(length, DK),
            table(DK, DV),
        ]
        + [jax.ShapeDtypeStruct((count,) + v.shape, v.dtype) for v in sources],
        in_specs=[ROOM] * 6 + [ANY] * number,
        out_specs=[ROOM] * 8 + [ANY] * number,
        scratch_shapes=[
            pltpu.VMEM((units, DK, DV), jnp.float32),
            pltpu.VMEM((2, length, 128), jnp.float32),
            pltpu.VMEM((2, 128, length), jnp.float32),
            *relay_scratch(units),
            *gather_sems(count, rows, number),
        ],
        compiler_params=pltpu.CompilerParams(
            collective_id=4, has_side_effects=True, vmem_limit_bytes=56 * 2**20
        ),
        name="forward_block",
    )(mixed_in, little, gate_pre, conv, head, gain, *sources)


def backward_kernel(groups, count, shares, *refs):
    number = len(shares)
    mixed_ref, little_ref, gate_ref, conv_ref, head_ref, gain_ref = refs[:6]
    out_ref, t_ref, u_ref, w_ref, m_ref, e_ref, s_ref, branch_ref = refs[6:14]
    givens, refs = refs[14 : 14 + number], refs[14 + number :]
    grad_ref, conv_grad, gain_grad, head_grad = refs[:4]
    totals, others = refs[4 : 4 + number], refs[4 + number : 4 + 2 * number]
    refs = refs[4 + 2 * number :]
    do_ref, c_ref, ds_ref, lit_ref, g_ref, grow_ref = refs[:6]
    sending, arriving, relay_send, relay_recv = refs[6:10]
    units = t_ref.shape[0]
    heads = units // 2
    size = t_ref.shape[1]
    mixed_width = mixed_ref.shape[2]
    at = Place(groups, count)
    line = Relay(at, False, units, sending, arriving, relay_send, relay_recv)
    further = further_groups(at)
    partners = at.partners() + [(at.group_swap, at.place)] + further + [line.before]
    greet(partners, count // 2 + 3 + len(further))
    plans = reduce_plans(at, givens, totals, others, shares, refs[10:])
    agenda = Agenda(reduce_steps(plans))
    for step in agenda.take(REDUCE_WINDOW):
        step()
    head_tables(little_ref, head_ref, g_ref, grow_ref)
    grad_ref[:, :PAD, mixed_width:] = jnp.zeros(
        (2, PAD, grad_ref.shape[2] - mixed_width), jnp.bfloat16
    )
    conv_grad[...] = jnp.zeros_like(conv_grad)
    gain_grad[...] = jnp.zeros_like(gain_grad)
    head_grad[...] = jnp.zeros_like(head_grad)
    lit_ref[...] = jnp.zeros_like(lit_ref)

    def gate_stage(seq, head):
        unit = seq * heads + head
        span = pl.ds(head * DV, DV)
        value = out_ref[unit]
        scale = lax.rsqrt(jnp.mean(value * value, axis=1, keepdims=True) + epsilon)
        normal = value * scale
        active, slope = silu_parts(gate_ref[seq, PAD:, span])
        grad = branch_ref[seq, :, span]
        gain = gain_ref[...]
        through = grad * active
        gain_grad[0:1] += jnp.sum(through * normal, axis=0, keepdims=True)
        gate_span = pl.ds(mixed_width + 128 + head * DV, DV)
        grad_ref[seq, PAD:, gate_span] = (grad * normal * gain * slope).astype(jnp.bfloat16)
        scaled = through * gain
        grad_out = scale * (scaled - normal * jnp.mean(scaled * normal, axis=1, keepdims=True))
        do_ref[unit] = grad_out
        c_ref[unit] = near(e_ref[unit], grad_out, TN)

    for seq in range(2):
        for head in range(heads):
            gate_stage(seq, head)
    agenda.until(BACK_OPEN)

    def pass_on():
        for unit in range(units):
            line.receive(unit, ds_ref)
            line.send(unit, lambda: close(m_ref[unit], ds_ref[unit], TN) + c_ref[unit])

    agenda.around(count, count - 1 - at.place, BACK_RELAY, pass_on)

    def grad_stage(seq, head):
        unit = seq * heads + head
        own = Unit(seq, head, heads, mixed_ref, conv_ref)
        beta, gcol, grow = head_columns(seq, head, heads, little_ref, g_ref, grow_ref)
        queries, keys, values = own.rows(0), own.rows(1), own.rows(2)
        decays = decay_table(gcol, grow)
        row, col = iotas(size, size)
        strict = row > col
        memory, after = s_ref[unit], ds_ref[unit]
        grad_out = do_ref[unit]
        growth = jnp.exp(gcol)
        last = gcol[size - 1 :, :]
        weights = jnp.exp(last - gcol)
        update = u_ref[unit] - near(w_ref[unit], memory)
        yield
        scores = near(queries, keys, NT) * decays
        keys_dot = jnp.where(strict, near(keys, keys, NT) * decays, 0.0)
        yield
        grad_update = near(scores, grad_out, TN) + near(keys * weights, after)
        yield
        grad_wanted = near(t_ref[unit], grad_update, TN)
        yield
        grad_system = -near(grad_wanted, update, NT)
        grad_scores = near(grad_out, update, NT)
        through = keys_dot * grad_system
        total = grad_scores * scores + beta * through
        yield
        query_part = growth * near(grad_out, memory, NT)
        key_read = growth * near(grad_wanted, memory, NT)
        key_part = beta * key_read
        end_part = weights * near(update, after, NT)
        yield
        grad_dot = grad_scores * decays
        grad_keys_dot = jnp.where(strict, grad_system * decays, 0.0) * beta
        grad_q = query_part + near(grad_dot, keys)
        grad_k = (
            end_part - key_part + near(grad_dot, queries, TN)
            + near(grad_keys_dot, keys) + near(grad_keys_dot, keys, TN)
        )
        yield
        own.taps_back(0, grad_q, grad_ref, conv_grad)
        own.taps_back(1, grad_k, grad_ref, conv_grad)
        own.taps_back(2, beta * grad_wanted, grad_ref, conv_grad)
        yield
        end_line = jnp.sum(keys * end_part, axis=1, keepdims=True)
        grad_beta = (
            jnp.sum(grad_wanted * values, axis=1, keepdims=True)
            - jnp.sum(keys * key_read, axis=1, keepdims=True)
            + jnp.sum(through, axis=1, keepdims=True)
        )
        grad_log = (
            jnp.sum(queries * query_part, axis=1, keepdims=True)
            - jnp.sum(keys * key_part, axis=1, keepdims=True)
            - end_line
            + jnp.sum(total, axis=1, keepdims=True)
        )
        grad_last = jnp.sum(end_line) + jnp.sum(
            jnp.exp(last) * jnp.sum(memory * after, axis=1, keepdims=True)
        )
        spot = lax.broadcasted_iota(jnp.int32, (size, 1), 0)
        grad_log = grad_log + jnp.where(spot == size - 1, grad_last, 0.0)
        later = (col >= row).astype(jnp.float32)
        lane = lax.broadcasted_iota(jnp.int32, (size, 128), 1)
        less = jnp.broadcast_to(jnp.sum(total, axis=0, keepdims=True), (128, size))
        grad_forget = exact(later, jnp.broadcast_to(grad_log, (size, 128))) - exact(later, less, NT)
        rate, bias = head_ref[0:1], head_ref[1:2]
        little = little_ref[own.seq, PAD:, :]
        on_forget = lane == heads + own.head
        grad_soft = jnp.where(on_forget, grad_forget * rate * jax.nn.sigmoid(little + bias), 0.0)
        forget = rate * jax.nn.softplus(little + bias)
        log_line = jnp.sum(jnp.where(on_forget, grad_forget * forget, 0.0), axis=0, keepdims=True)
        head_grad[0:1] += log_line
        head_grad[1:2] += jnp.sum(grad_soft, axis=0, keepdims=True)
        lit_ref[own.seq] += grad_soft + jnp.where(
            lane == own.head, grad_beta * beta * (1.0 - beta), 0.0
        )
        yield

    agenda.loop(2, BACK_GRADS, lambda seq: lockstep([grad_stage(seq, h) for h in range(heads)]))
    grad_ref[:, PAD:, mixed_width : mixed_width + 128] = lit_ref[...].astype(jnp.bfloat16)
    agenda.until(1.0)
    line.finish()


def backward_block(mixed_in, little, gate_pre, conv, head, gain, kept, grad_branch, givens, shares):
    groups, count = lax.axis_size("dp"), lax.axis_size("seq")
    number, rows = len(givens), givens[0].shape[2]
    length = mixed_in.shape[1] - PAD
    units = kept[0].shape[0]
    widths = [v.shape[3] for v in givens]
    results = [jax.ShapeDtypeStruct((rows, width), jnp.bfloat16) for width in widths]
    total_width = mixed_in.shape[2] + 128 + gate_pre.shape[2]
    return pl.pallas_call(
        functools.partial(backward_kernel, groups, count, shares),
        out_shape=[
            jax.ShapeDtypeStruct((2, length + PAD, total_width), jnp.bfloat16),
            jax.ShapeDtypeStruct(conv.shape, jnp.float32),
            jax.ShapeDtypeStruct((8, DV), jnp.float32),
            jax.ShapeDtypeStruct((8, 128), jnp.float32),
        ]
        + results * 2,
        in_specs=[ROOM] * 14 + [ANY] * number,
        out_specs=[ROOM] * (4 + 2 * number),
        scratch_shapes=[
            pltpu.VMEM((units, length, DV), jnp.float32),
            pltpu.VMEM((units, DK, DV), jnp.float32),
            pltpu.VMEM((units, DK, DV), jnp.float32),
            pltpu.VMEM((2, length, 128), jnp.float32),
            pltpu.VMEM((2, length, 128), jnp.float32),
            pltpu.VMEM((2, 128, length), jnp.float32),
            *relay_scratch(units),
            *reduce_scratch(groups, count, rows, widths, shares),
        ],
        compiler_params=pltpu.CompilerParams(
            collective_id=5, has_side_effects=True, vmem_limit_bytes=60 * 2**20
        ),
        name="backward_block",
    )(mixed_in, little, gate_pre, conv, head, gain, *kept, grad_branch, *givens)


def reduce_first_kernel(groups, count, share, *refs):
    given, swap, rims, small = refs[:4]
    total, other, swap_got, rim_got, small_sum = refs[4:9]
    scratch = refs[9:]
    small_got, small_hold, swap_send, swap_recv, small_send, small_recv = scratch[-6:]
    at = Place(groups, count)
    further = further_groups(at)
    core = (at.group_swap, at.place)
    stages = []
    distance = 1
    while distance < groups:
        stages.append((at.group + distance - 2 * distance * ((at.group // distance) % 2), at.place))
        distance *= 2
    distance = 1
    while distance < count:
        stages.append((at.group, at.place + distance - 2 * distance * ((at.place // distance) % 2)))
        distance *= 2
    partners = at.partners() + [core] + further + stages + list(neighbours(at, 1))
    greet(partners, count // 2 + 4 + len(further) + len(stages))
    own_back, swap_back = neighbours(at, -1)
    swapped = remote(swap, swap_got, swap_send, swap_recv, 0, core)
    rim_copies = [
        remote(rims.at[0], rim_got.at[0], swap_send, swap_recv, 1, own_back),
        remote(rims.at[1], rim_got.at[1], swap_send, swap_recv, 2, swap_back),
    ]
    plans = reduce_plans(at, [given], [total], [other], [share], scratch)
    steps = reduce_steps(plans)
    for step in steps[: min(REDUCE_WINDOW, len(plans))]:
        step()
    steps = steps[min(REDUCE_WINDOW, len(plans)) :]
    swapped.start()

    @pl.when(at.place > 0)
    def _():
        for copy in rim_copies:
            copy.start()

    small_hold[0] = small[...]

    def add_small(index):
        copy = remote(
            small_hold.at[index], small_got.at[index], small_send, small_recv, index, stages[index]
        )
        copy.start()
        copy.wait()
        small_hold[index + 1] = small_hold[index] + small_got[index]

    for index in range(max(len(steps), len(stages))):
        if index < len(steps):
            steps[index]()
        if index < len(stages):
            add_small(index)
    small_sum[...] = small_hold[len(stages)]
    swapped.wait()

    @pl.when(at.place == count - 1)
    def _():
        rim_got[...] = jnp.zeros_like(rim_got)

    @pl.when(at.place < count - 1)
    def _():
        for copy in rim_copies:
            copy.wait_recv()

    @pl.when(at.place > 0)
    def _():
        for copy in rim_copies:
            copy.wait_send()


def reduce_first(given, swap, rims, small, share):
    groups, count = lax.axis_size("dp"), lax.axis_size("seq")
    rows, width = given.shape[2:]
    rounds = (groups.bit_length() - 1) + (count.bit_length() - 1)
    result = jax.ShapeDtypeStruct((rows, width), jnp.bfloat16)
    return pl.pallas_call(
        functools.partial(reduce_first_kernel, groups, count, share),
        out_shape=[
            result,
            result,
            jax.ShapeDtypeStruct(swap.shape, swap.dtype),
            jax.ShapeDtypeStruct(rims.shape, rims.dtype),
            jax.ShapeDtypeStruct(small.shape, small.dtype),
        ],
        in_specs=[ANY, ROOM, ROOM, ROOM],
        out_specs=[ROOM] * 5,
        scratch_shapes=reduce_scratch(groups, count, rows, [width], [share])
        + [
            pltpu.VMEM((rounds,) + small.shape, jnp.float32),
            pltpu.VMEM((rounds + 1,) + small.shape, jnp.float32),
            pltpu.SemaphoreType.DMA((3,)),
            pltpu.SemaphoreType.DMA((3,)),
            pltpu.SemaphoreType.DMA((rounds,)),
            pltpu.SemaphoreType.DMA((rounds,)),
        ],
        compiler_params=pltpu.CompilerParams(
            collective_id=6, has_side_effects=True, vmem_limit_bytes=56 * 2**20
        ),
        name="reduce_first",
    )(given, swap, rims, small)


def third(width, weight):
    return 128 * max(1, round(width * weight / 128))


def norm_parts(field_in):
    scale = lax.rsqrt(jnp.mean(field_in * field_in, axis=-1, keepdims=True) + epsilon)
    return scale, field_in * scale


def norm_back(scale, unit, gain_vec, grad):
    scaled = grad * gain_vec
    return scale * (scaled - unit * jnp.mean(scaled * unit, axis=-1, keepdims=True))


def dense(left, right, dims):
    return lax.dot_general(left, right, (dims, ((), ())), preferred_element_type=jnp.float32)


def swiglu(gate_up):
    hidden_units = gate_up.shape[1] // 2
    return jax.nn.silu(gate_up[:, :hidden_units]) * gate_up[:, hidden_units:]


def on_device(
    tokens,
    target,
    valid,
    in_weight,
    small_weight,
    out_weight,
    ffn_in,
    ffn_out,
    gain_first,
    gain_second,
    gain_out,
    conv_weight,
    decay_log,
    decay_bias,
):
    count = lax.axis_size("seq")
    groups = lax.axis_size("dp")
    core = lax.axis_index("dp") % 2
    rows = in_weight.shape[0]
    length, model = tokens.shape[1], tokens.shape[2]
    both, padded = 2 * length, length + PAD
    heads = HEADS // 2
    keys, vals, inner = KEYS // 2, VALUES // 2, FF // 2
    mixed_width = 2 * keys + vals

    def mine(array, start, width):
        return lax.dynamic_slice_in_dim(array, start + core * width, width, array.ndim - 1)

    def qkv_half(array):
        parts = [mine(array, 0, keys), mine(array, KEYS, keys), mine(array, 2 * KEYS, vals)]
        return jnp.concatenate(parts, axis=1)

    small_half = [mine(small_weight, 0, heads), mine(small_weight, HEADS, heads)]
    spare = jnp.zeros((rows, 128 - 2 * heads), jnp.bfloat16)
    part_gate = mine(in_weight, 2 * KEYS + VALUES, vals)
    part_first = jnp.concatenate([qkv_half(in_weight)] + small_half + [spare, part_gate], axis=1)
    part_out = mine(out_weight, 0, vals)
    part_up = jnp.concatenate([mine(ffn_in, 0, inner), mine(ffn_in, FF, inner)], axis=1)
    part_down = mine(ffn_out, 0, inner)
    first_width = part_first.shape[1]

    mask_own = valid[0].astype(jnp.float32)
    mask_rows = jnp.broadcast_to(mask_own[None, :], (8, length))
    w_first, tokens_other, target_other, mask_other, rim = gather_first(
        part_first, tokens[0], target[0], mask_rows, third(first_width, 0.33)
    )
    w_first = w_first.reshape(model, first_width)

    inputs = jnp.concatenate([rim[0], tokens[0], rim[1], tokens_other], axis=0).astype(jnp.float32)
    first_scale, first_unit = norm_parts(inputs)
    normed = (first_unit * gain_first).astype(jnp.bfloat16)
    project = dense(normed, w_first, ((1,), (0,))).reshape(2, padded, first_width)
    mixed_in = project[..., :mixed_width].astype(jnp.bfloat16)
    little = project[..., mixed_width : mixed_width + 128]
    gate_pre = project[..., mixed_width + 128 :]

    own_conv = jnp.concatenate([qkv_half(conv_weight), jnp.zeros((8 - CONV, mixed_width))], axis=0)
    lanes = ((0, 0), (heads, 128 - 2 * heads))
    head = jnp.concatenate(
        [
            jnp.pad(-jnp.exp(mine(decay_log, 0, heads))[None], lanes),
            jnp.pad(mine(decay_bias, 0, heads)[None], lanes),
            jnp.zeros((6, 128), jnp.float32),
        ],
        axis=0,
    )
    gain_row = gain_out[None]
    rests = [part_out, part_up, part_down]
    branch, *kept, w_out, w_up, w_down = forward_block(
        mixed_in, little, gate_pre, own_conv, head, gain_row,
        rests, [third(v.shape[1], 0.33) for v in rests],
    )
    branch = branch.reshape(both, vals)
    w_out, w_up, w_down = (v.reshape(model, v.shape[2]) for v in (w_out, w_up, w_down))

    def core_sum(part):
        pairs = [(group, group ^ 1) for group in range(groups)]
        got = lax.ppermute(part.astype(jnp.bfloat16), "dp", pairs)
        return part + jnp.concatenate([got[length:], got[:length]], axis=0).astype(jnp.float32)

    positions = jnp.concatenate([tokens[0], tokens_other], axis=0).astype(jnp.float32)
    hidden = positions + core_sum(dense(branch, w_out, ((1,), (1,))))
    second_scale, second_unit = norm_parts(hidden)
    second = (second_unit * gain_second).astype(jnp.bfloat16)
    gate_up = dense(second, w_up, ((1,), (0,)))
    active_f, swiglu_pull = jax.vjp(swiglu, gate_up)
    active = active_f.astype(jnp.bfloat16)
    summed = hidden + core_sum(dense(active, w_down, ((1,), (1,))))
    mask = jnp.concatenate([mask_own, mask_other[0]])
    errors = summed - jnp.concatenate([target[0], target_other]).astype(jnp.float32)
    own_errors = errors[:length]
    loss_part = jnp.sum(mask_own * jnp.mean(own_errors * own_errors, axis=-1))

    grad_summed = mask[:, None] * errors
    grad_feed = grad_summed.astype(jnp.bfloat16)
    grad_active = dense(grad_feed, w_down, ((1,), (0,)))
    grad_down = dense(grad_feed, active, ((0,), (0,))).astype(jnp.bfloat16)
    grad_gate_up = swiglu_pull(grad_active)[0].astype(jnp.bfloat16)
    grad_up = dense(second, grad_gate_up, ((0,), (0,))).astype(jnp.bfloat16)
    grad_second = core_sum(dense(grad_gate_up, w_up, ((1,), (1,))))
    grad_gain_second = jnp.sum((grad_second * second_unit)[:length], axis=0)
    grad_hidden = grad_summed + norm_back(second_scale, second_unit, gain_second, grad_second)
    grad_attn = grad_hidden.astype(jnp.bfloat16)
    grad_out = dense(grad_attn, branch, ((0,), (0,))).astype(jnp.bfloat16)
    grad_branch = dense(grad_attn, w_out, ((1,), (0,))).reshape(2, length, vals)

    grad_rests = [grad_down, grad_up, grad_out]
    grad_first, grad_conv, grad_gain_out, grad_head, *reduced = backward_block(
        mixed_in, little, gate_pre, own_conv, head, gain_row, kept, grad_branch,
        [v.reshape(count // 2, 2, rows, v.shape[1]) for v in grad_rests],
        [third(v.shape[1], 0.28) for v in grad_rests],
    )
    grad_first = grad_first.reshape(2 * padded, first_width)
    grad_w_first = dense(normed, grad_first, ((0,), (0,))).astype(jnp.bfloat16)
    normed_part = dense(grad_first, w_first, ((1,), (1,)))
    grad_gain_first = jnp.sum(normed_part * first_unit, axis=0)
    normed_part = normed_part.reshape(2, padded, model)

    def place_half(array, start, width, values):
        at = array.ndim - 1
        return lax.dynamic_update_slice_in_dim(array, values, start + core * width, at)

    all_conv = jnp.zeros(conv_weight.shape, jnp.float32)
    all_conv = place_half(all_conv, 0, keys, grad_conv[:CONV, :keys])
    all_conv = place_half(all_conv, KEYS, keys, grad_conv[:CONV, keys : 2 * keys])
    all_conv = place_half(all_conv, 2 * KEYS, vals, grad_conv[:CONV, 2 * keys :])
    no_heads = jnp.zeros((HEADS,), jnp.float32)
    smalls = [
        grad_gain_first,
        grad_gain_second,
        grad_gain_out[0],
        all_conv.reshape(-1),
        place_half(no_heads, 0, heads, grad_head[0, heads : 2 * heads]),
        place_half(no_heads, 0, heads, grad_head[1, heads : 2 * heads]),
        loss_part[None],
        jnp.sum(mask_own)[None],
    ]
    sizes = [v.shape[0] for v in smalls]
    extra = -sum(sizes) % 1024
    packed = jnp.concatenate(smalls + [jnp.zeros((extra,), jnp.float32)]).reshape(-1, 128)
    total_first, other_first, swap_got, rim_got, small_sum = reduce_first(
        grad_w_first.reshape(count // 2, 2, rows, first_width),
        normed_part[1, PAD:].astype(jnp.bfloat16),
        normed_part[:, :PAD].astype(jnp.bfloat16),
        packed,
        third(first_width, 0.28),
    )
    small_flat = small_sum.reshape(-1)
    found, start = [], 0
    for size in sizes:
        found.append(small_flat[start : start + size])
        start += size
    valid_count = jnp.maximum(found[7][0], 1.0)
    loss_value = found[6][0] / valid_count
    factor = length * groups * count / valid_count

    rim_rows = jnp.sum(rim_got.astype(jnp.float32), axis=0)
    grad_normed = normed_part[0, PAD:] + swap_got.astype(jnp.float32)
    grad_normed = jnp.concatenate(
        [grad_normed[: length - PAD], grad_normed[length - PAD :] + rim_rows], axis=0
    )
    grad_tokens = grad_hidden[:length] + norm_back(
        first_scale[PAD:padded], first_unit[PAD:padded], gain_first, grad_normed
    )

    def join(own, other, start, width):
        own_part, other_part = own[:, start : start + width], other[:, start : start + width]
        low = jnp.where(core == 0, own_part, other_part)
        high = jnp.where(core == 0, other_part, own_part)
        return [low, high]

    def joined(parts):
        return jnp.concatenate(parts, axis=1).astype(jnp.float32) * factor

    pair_first = (total_first, other_first)
    pair_down, pair_up, pair_out = ((reduced[i], reduced[3 + i]) for i in range(3))
    result_in = joined(
        join(*pair_first, 0, keys)
        + join(*pair_first, keys, keys)
        + join(*pair_first, 2 * keys, vals)
        + join(*pair_first, mixed_width + 128, vals)
    )
    result_small = joined(
        join(*pair_first, mixed_width, heads) + join(*pair_first, mixed_width + heads, heads)
    )
    result_out = joined(join(*pair_out, 0, vals))
    result_up = joined(join(*pair_up, 0, inner) + join(*pair_up, inner, inner))
    result_down = joined(join(*pair_down, 0, inner))
    return (
        summed[:length].astype(jnp.bfloat16)[None],
        loss_value,
        (grad_tokens * factor)[None],
        result_in,
        result_small,
        result_out,
        result_up,
        result_down,
        found[0] * factor,
        found[1] * factor,
        found[2] * factor,
        found[3].reshape(conv_weight.shape) * factor,
        found[4] * factor,
        found[5] * factor,
    )


def solution(mesh):
    placed = (
        P("dp", "seq", None),
        P("dp", "seq", None),
        P("dp", "seq"),
        P("seq", None),
        P("seq", None),
        P("seq", None),
        P("seq", None),
        P("seq", None),
        P(),
        P(),
        P(),
        P(),
        P(),
        P(),
    )
    return jax.shard_map(
        on_device,
        mesh=mesh,
        in_specs=placed,
        out_specs=(
            P("dp", "seq", None),
            P(),
            P("dp", "seq", None),
            P("seq", None),
            P("seq", None),
            P("seq", None),
            P("seq", None),
            P("seq", None),
            P(),
            P(),
            P(),
            P(),
            P(),
            P(),
        ),
        check_vma=False,
    )
```

time: 760 us -> 540 us (0.71)
  Pallas kernels: 524 us -> 399 us
  local copies, waits for them, and re-layouts: 79.7 us -> 32.2 us
  other arithmetic: 80.9 us -> 42 us
  matrix products: 54.5 us -> 46.7 us
    pallas_call x6 -> x2, Pallas kernels: 412 us -> 250 us  [the longest x1 133 us: backward_block(): pl.pallas_call(functools.partial(backward_kernel, groups, count, shares),...]
    pallas_call x1, Pallas kernels: 64.7 us -> 93.2 us  [reduce_first(): pl.pallas_call(functools.partial(reduce_first_kernel, groups, count, shar...]
    mul x8 -> x0, other arithmetic: 14.7 us -> none  [the longest x1 7.66 us: prepare(): active = jax.nn.silu(convolved)]
    another operation x10 -> x1, other arithmetic: 11.9 us -> 0.16 us
    mul x10 -> x0, local copies, waits for them, and re-layouts: 11.3 us -> none  [the longest x8 9.61 us: unit_rows(): field_in * lax.rsqrt(jnp.sum(field_in * field_in, axis=-1, keepdims=True)...]
    reduce_sum x7 -> x0, other arithmetic: 9.5 us -> none  [the longest x1 7.57 us: prepare(): conv_weight[offset] * padded[:, offset:offset + length]]
    unnamed x210 -> x101, local copies, waits for them, and re-layouts: 18.6 us -> 9.24 us
    pallas_call x1, Pallas kernels: 47.1 us -> 55.8 us  [gather_first(): pl.pallas_call(functools.partial(gather_first_kernel, groups, count, shar...]
  transfers between devices with their start and end apart: 3 -> 3, of which waited for: 1 -> 2; matrix products, arithmetic and copies ran while one was open for 2% -> 2% of each run, Pallas kernels for 0% -> 0%
where the time goes in v3:
time: 540 us; the launch traced here: 529 us
  Pallas kernels  399 us (74%)
  matrix products  46.7 us (9%)
  other arithmetic  42 us (8%)
  local copies, waits for them, and re-layouts  32.2 us (6%)
    pallas_call x1, Pallas kernels, backward_block(): pl.pallas_call(functools.partial(backward_kernel, groups, count, shares),...  133 us
    pallas_call x1, Pallas kernels, forward_block(): pl.pallas_call(functools.partial(forward_kernel, groups, count, shares),...  118 us
    pallas_call x1, Pallas kernels, reduce_first(): pl.pallas_call(functools.partial(reduce_first_kernel, groups, count, shar...  93.2 us
    pallas_call x1, Pallas kernels, gather_first(): pl.pallas_call(functools.partial(gather_first_kernel, groups, count, shar...  55.8 us
    dot_general x12, matrix products, dense(): lax.dot_general(left, right, (dims, ((), ())), preferred_element_type=jnp...  46.7 us
  transfers between devices with their start and end apart: 3, of which 2 were waited for; matrix products, arithmetic and copies ran while one was open for 2% of the time, Pallas kernels for 0%

profile of v3, /device:TPU:0, one launch (start us, length us, event | category | flops | bytes accessed | tf_op | source)
XLA Modules:
  0.0 529.1 jit_solution(13976078238898951245)
XLA Ops:
  6.1 55.8 %gather_first.1 = (bf16[8,128,2432]{2,1,0:T(8,128)(2,1)}, bf16[256,1024]{1,0:T(8,128)(2,1)}, bf16[256,1024]{1,0:T(8,128)(2,1)}, f32[8,256]{1,0:T(8,128)}, bf16[2,16,1024]{2,1,0:T(8,128)(2,1)}) custom-call(bf16[128,2432]{1,0:T(8,128)(2,1)} %concatenate.57.refs_0_, bf16[256,1024]{1,0:T(8,128)(2,1)} %bitcast.77, bf16[256,1024]{1,0:T(8,128)(2,1)} %bitcast.91, ...), custom_call_target="tpu_custom_call" | custom-call | tf_op jit(solution)/shard_map/gather_first/pallas_call | solution.py:451
  62.7 1.5 fusion.3
  64.3 2.9 convert_multiply_fusion.1
  67.2 3.1 fusion.26
  71.5 1.4 slice.331.refs_0_
  78.7 117.9 %forward_block.1 = (bf16[2,256,768]{2,1,0:T(8,128)(2,1)}, f32[6,256,256]{2,1,0:T(8,128)}, f32[6,256,256]{2,1,0:T(8,128)}, f32[6,256,256]{2,1,0:T(8,128)}, f32[6,...) custom-call(bf16[2,272,1536]{2,1,0:T(8,128)(2,1)} %slice.331.refs_0_, ...), custom_call_target="tpu_custom_call" | custom-call | tf_op jit(solution)/shard_map/forward_block/pallas_call | solution.py:841
  196.7 2.7 fusion.23
  199.4 2.6 collective-permute-done
  203.8 2.7 copy-done.39
  206.5 3.1 fusion.11
  210.6 2.1 copy-done.11
  213.6 3.5 fusion.24
  221.6 3.3 convert_subtract_fusion
  225.1 4.0 fusion.12
  229.1 5.1 fusion.25
  235.9 3.6 convolution_convert_fusion.2
  239.5 5.2 convolution_convert_fusion
  246.6 2.2 convolution_convert_fusion.3
  248.8 2.1 fusion.27.refs_13_
  250.9 132.5 %backward_block.1 = (bf16[2,272,2432]{2,1,0:T(8,128)(2,1)}, f32[8,1536]{1,0:T(8,128)}, f32[8,256]{1,0:T(8,128)}, f32[8,128]{1,0:T(8,128)}, bf16[128,1408]{1,0:T(...) custom-call(bf16[2,272,1536]{2,1,0:T(8,128)(2,1)} %slice.331.refs_0_, ...), custom_call_target="tpu_custom_call" | custom-call | tf_op jit(solution)/shard_map/backward_block/pallas_call | solution.py:1024
  383.4 6.1 %multiply_reduce_fusion = (f32[1024]{0:T(1024)S(1)}, f32[544,1024]{1,0:T(8,128)S(1)}) fusion(f32[544]{0:T(1024)S(1)} %add_rsqrt_fusion, bf16[256,1024]{1,0:T(8,128)(2,1)S(1)} %copy-done.5, bf16[16,1024]{1,0:T(8,128)(2,1)S(1)} %get-tuple-element.125, bf16[256,1024]{1,0:T(8,128)(2,1)S(1)} %bitcast.83, bf16[16,1024]{1,0:T(8,128)(2,1)S(1)} %get-tuple-element.124, ...), kind=kOutput, calls=%fused_computation.16 | convolution fusion | flops 2715646976 | bytes 10975360 | tf_op jit(solution)/shard_map/dot_general | solution.py:1169
  392.6 6.0 %convolution_convert_fusion.1 = bf16[1024,2432]{1,0:T(8,128)(2,1)} fusion(bf16[544,1024]{1,0:T(8,128)(2,1)S(1)} %copy-done.20, bf16[544,2432]{1,0:T(8,128)(2,1)S(1)} %bitcast.121), kind=kOutput, calls=%fused_computation.2 | convolution fusion | flops 2712010752 | bytes 8740864 | tf_op jit(solution)/shard_map/dot_general | solution.py:1169
  401.1 2.0 concatenate.69
  403.1 93.2 %reduce_first.1 = (bf16[128,2432]{1,0:T(8,128)(2,1)}, bf16[128,2432]{1,0:T(8,128)(2,1)}, bf16[256,1024]{1,0:T(8,128)(2,1)}, bf16[2,16,1024]{2,1,0:T(8,128)(2,1)}, f32[120,128]{1,0:T(8,128)}) custom-call(bf16[4,2,128,2432]{3,2,1,0:T(8,128)(2,1)} %bitcast.87, bf16[256,1024]{1,0:T(8,128)(2,1)} %slice_bitcast_fusion.1.refs_1_, ...), custom_call_target="tpu_custom_call" | custom-call | tf_op jit(solution)/shard_map/reduce_first/pallas_call | solution.py:1127
  504.1 1.6 select_dynamic-update-slice_fusion.7
  506.7 1.6 select_dynamic-update-slice_fusion.6
  508.3 1.6 select_dynamic-update-slice_fusion.5
  509.9 1.6 select_dynamic-update-slice_fusion.4
  511.5 1.7 select_dynamic-update-slice_fusion.3
  515.4 2.9 convert_multiply_fusion.3
  518.4 1.5 fusion.4
  525.1 1.9 convert_multiply_fusion
  (185 shorter events, 45.6 us)
Async XLA Ops:
  0.6 75.9 %copy-start = (bf16[128,2816]{1,0:T(8,128)(2,1)S(1)}, bf16[128,2816]{1,0:T(8,128)(2,1)}, u32[]{:S(2)}) copy-start(bf16[128,2816]{1,0:T(8,128)(2,1)} %param.21) | copy-start | bytes 2162692
  2.4 60.3 %copy-start.4 = (bf16[1,256,1024]{2,1,0:T(8,128)(2,1)S(1)}, bf16[1,256,1024]{2,1,0:T(8,128)(2,1)}, u32[]{:S(2)}) copy-start(bf16[1,256,1024]{2,1,0:T(8,128)(2,1)} %param.14) | copy-start | bytes 1572868
  4.5 59.7 %copy-start.32 = (f32[1024]{0:T(1024)S(1)}, f32[1024]{0:T(1024)}, u32[]{:S(2)}) copy-start(f32[1024]{0:T(1024)} %param.22) | copy-start | bytes 12292
  62.7 4.4 copy-start.40
  67.2 3.1 copy-start.19
  73.7 4.3 copy-start.37
  73.7 4.3 copy-start.38
  199.4 2.7 collective-permute-start
  203.1 3.4 copy-start.39
  203.5 6.2 %copy-start.2 = (f32[512,1024]{1,0:T(8,128)}, f32[512,1024]{1,0:T(8,128)S(1)}, u32[]{:S(2)}) copy-start(f32[512,1024]{1,0:T(8,128)S(1)} %broadcast_multiply_fusion) | copy-start | bytes 6291460
  209.7 3.9 copy-start.41
  212.6 4.5 copy-start.17
  213.6 4.5 copy-start.36
  217.1 3.0 collective-permute-start.1
  217.3 4.3 copy-start.8
  217.3 4.3 copy-start.10
  217.3 4.3 copy-start.15
  217.3 4.3 copy-start.24
  220.1 4.9 slice-start
  221.6 3.5 slice-start.1
  221.6 3.5 copy-start.42
  224.9 4.2 slice-start.2
  225.1 4.0 slice-start.3
  229.1 6.8 %copy-start.18 = (bf16[512,1408]{1,0:T(8,128)(2,1)S(1)}, bf16[512,1408]{1,0:T(8,128)(2,1)}, u32[]{:S(2)}) copy-start(bf16[512,1408]{1,0:T(8,128)(2,1)} %copy-done.17) | copy-start | bytes 4325380
  234.3 10.4 %collective-permute-start.2 = (bf16[512,1024]{1,0:T(8,128)(2,1)S(1)}, bf16[512,1024]{1,0:T(8,128)(2,1)S(1)}, u32[]{:S(2)}, u32[]{:S(2)}) collective-permute-start(bf16[512,1024]{1,0:T(8,128)(2,1)S(1)} %get-tuple-element.140), channel_id=1, source_target_pairs={{0,8},{8,0},{16,24},{24,16},{1,9},{9,1},{17,25},{25,17},{2,10},{10... | collective-permute-start | bytes 3145736 | tf_op jit(solution)/shard_map/ppermute | solution.py:1255
  235.9 3.6 copy-start.3
  235.9 3.6 copy-start.44
  389.5 3.1 copy-start.43
  392.6 6.0 %copy-start.35 = (f32[8,1536]{1,0:T(8,128)S(1)}, f32[8,1536]{1,0:T(8,128)}, u32[]{:S(2)}) copy-start(f32[8,1536]{1,0:T(8,128)} %get-tuple-element.63) | copy-start | bytes 147460
  496.3 16.9 %copy-start.13 = (bf16[128,2432]{1,0:T(8,128)(2,1)S(1)}, bf16[128,2432]{1,0:T(8,128)(2,1)}, u32[]{:S(2)}) copy-start(bf16[128,2432]{1,0:T(8,128)(2,1)} %get-tuple-element.68) | copy-start | bytes 1867780
  496.3 16.9 %copy-start.14 = (bf16[128,2432]{1,0:T(8,128)(2,1)S(1)}, bf16[128,2432]{1,0:T(8,128)(2,1)}, u32[]{:S(2)}) copy-start(bf16[128,2432]{1,0:T(8,128)(2,1)} %get-tuple-element.69) | copy-start | bytes 1867780
  514.7 3.6 copy-start.25
  (20 other events, 36.8 us)

commit v4 on v3

--- a/solution.py
+++ b/solution.py
@@ -170,50 +170,59 @@
         self.arrived(at.half - 1 + step, at.shard(at.behind(step), 1 - at.side), self.own)
         self.launch(self.across, step, 1)
 
-    def finish(self):
+    def take_across(self):
         at = self.at
         for step in range(at.half):
             for side in range(2):
                 if step or side:
                     shard = at.shard(at.behind(step), at.side if side == 0 else 1 - at.side)
                     self.arrived(2 * at.half - 1 + 2 * step + side - 1, shard, self.borrowed)
+        self.keep().wait()
+
+    def finish(self):
         for (unused, where), make in self.started.items():
             make(*where).wait_send()
-        self.keep().wait()
 
     def stages(self):
         half = self.at.half
         first = [functools.partial(self.pass_along, step) for step in range(1, half)]
         second = [functools.partial(self.pass_beside, step) for step in range(half)]
-        return first, second
+        return [first, second, [self.take_across]]
 
 
 def copies_of_gather(count):
     return 2 * count - 2
 
 
-def lagged(plans):
+def lagged(plans, lag):
     depth = max(len(plan) for plan in plans)
     turns = []
-    for turn in range(len(plans) + depth - 1):
+    for turn in range(len(plans) + lag * (depth - 1)):
         steps = []
         for index, plan in enumerate(plans):
-            if 0 <= turn - index < len(plan):
-                steps = plan[turn - index] + steps
+            stage, rest = divmod(turn - index, lag)
+            if rest == 0 and 0 <= stage < len(plan):
+                steps = plan[stage] + steps
         turns.append(steps)
     return turns
 
 
+class Work:
+    def __init__(self, given, base, width, share, spots):
+        self.given, self.base, self.width, self.share, self.spots = given, base, width, share, spots
+
+
 class Reduce:
-    def __init__(self, at, given, total, other, lines, share, buffers, sems):
-        self.at, self.given, self.total, self.other = at, given, total, other
-        self.lines, self.share = lines, share
-        self.acc, self.from_across, self.from_beside, self.from_along, self.part, self.from_plane, self.far = buffers
+    def __init__(self, at, work, lines, buffers, sems):
+        self.at, self.given, self.spots, self.lines = at, work.given, work.spots, lines
+        self.acc, self.from_across, self.from_beside, self.from_along = buffers[:4]
+        self.part, self.from_plane, self.total, self.other, self.far = buffers[4:]
         self.sends, self.receives, self.local = sems
-        width = total.shape[1]
+        width, share = work.width, work.share
         self.wide = width - share
         self.own = pl.ds(tile_start(at.plane * share), self.wide)
-        self.lent = pl.ds(tile_start((1 - at.plane) * self.wide), share)
+        self.given_own = pl.ds(tile_start(work.base + at.plane * share), self.wide)
+        self.given_lent = pl.ds(tile_start(work.base + (1 - at.plane) * self.wide), share)
         self.inner = pl.ds(tile_start(at.plane * (width - 2 * share)), share)
         self.theirs = pl.ds(tile_start((1 - at.plane) * share), self.wide)
         self.started = {}
@@ -228,13 +237,13 @@
     def across(self, mine):
         at = self.at
         return remote(
-            self.given.at[:, self.side(mine), self.lines, self.lent], self.from_across.at[mine],
+            self.given.at[:, self.side(mine), self.lines, self.given_lent], self.from_across.at[mine],
             self.sends, self.receives, mine, (at.across, at.place),
         )
 
     def load(self, mine):
         return pltpu.make_async_copy(
-            self.given.at[:, self.side(mine), self.lines, self.own], self.acc.at[mine],
+            self.given.at[:, self.side(mine), self.lines, self.given_own], self.acc.at[mine],
             self.local.at[mine],
         )
 
@@ -261,15 +270,14 @@
     def core(self):
         at = self.at
         return remote(
-            self.total.at[self.lines], self.other.at[self.lines], self.sends, self.receives,
-            4, (at.group_swap, at.place),
+            self.total, self.other, self.sends, self.receives, 4, (at.group_swap, at.place)
         )
 
     def further(self, index, distance):
         at = self.at
         group = at.group + distance - 2 * distance * ((at.group // distance) % 2)
         return remote(
-            self.total.at[self.lines], self.far.at[index], self.sends, self.receives,
+            self.total, self.far.at[index], self.sends, self.receives,
             4 + at.half + index, (group, at.place),
         )
 
@@ -307,12 +315,11 @@
 
     def add_plane(self):
         self.plane().wait_recv()
-        height = self.part.shape[0]
-        self.total[self.lines] = jnp.zeros((height, self.total.shape[1]), jnp.bfloat16)
-        self.total[self.lines, self.own] = self.part[...]
-        held = self.total[self.lines, self.theirs].astype(jnp.float32)
+        self.total[...] = jnp.zeros_like(self.total)
+        self.total[:, self.own] = self.part[...]
+        held = self.total[:, self.theirs].astype(jnp.float32)
         got = self.from_plane[...].astype(jnp.float32)
-        self.total[self.lines, self.theirs] = (held + got).astype(jnp.bfloat16)
+        self.total[:, self.theirs] = (held + got).astype(jnp.bfloat16)
         distance = 4
         while distance < self.at.groups:
             index = distance.bit_length() - 3
@@ -320,13 +327,19 @@
             copy.start()
             copy.wait()
             got = self.far[index].astype(jnp.float32)
-            value = self.total[self.lines].astype(jnp.float32) + got
-            self.total[self.lines] = value.astype(jnp.bfloat16)
+            self.total[...] = (self.total[...].astype(jnp.float32) + got).astype(jnp.bfloat16)
             distance *= 2
         self.launch(self.core)
 
+    def deliver(self):
+        self.core().wait_recv()
+        core = self.at.group % 2
+        for target, start, width, source in self.spots:
+            for held, which in ((self.total, core), (self.other, 1 - core)):
+                span = pl.ds(tile_start(start + which * width), width)
+                target[self.lines, span] = held[:, source : source + width]
+
     def finish(self):
-        self.core().wait_recv()
         for (unused, where), make in self.started.items():
             make(*where).wait_send()
 
@@ -336,14 +349,15 @@
             [functools.partial(self.add_across, 1), self.add_beside],
             [self.add_along],
             [self.add_plane],
+            [self.deliver],
         ]
 
 
 ANY = pl.BlockSpec(memory_space=pl.ANY)
 ROOM = pl.BlockSpec(memory_space=pltpu.VMEM)
 PAD = 16
-CHUNKS, WINDOW = 4, 2
-REDUCE_CHUNKS, REDUCE_WINDOW = 4, 2
+CHUNKS, WINDOW, GATHER_LAG = 4, 2, 1
+REDUCE_CHUNKS, REDUCE_WINDOW, REDUCE_LAG = 4, 2, 1
 
 
 def neighbours(at, step):
@@ -380,7 +394,7 @@
 
 def gather_steps(plans):
     steps = [plan.begin for plan in plans[:WINDOW]]
-    for index, turn in enumerate(lagged([plan.stages() for plan in plans])):
+    for index, turn in enumerate(lagged([plan.stages() for plan in plans], GATHER_LAG)):
         steps += turn
         if index + WINDOW < len(plans):
             steps.append(plans[index + WINDOW].begin)
@@ -389,90 +403,17 @@
 
 def reduce_steps(plans):
     steps = [plan.begin for plan in plans[:REDUCE_WINDOW]]
-    for index, turn in enumerate(lagged([plan.stages() for plan in plans])):
+    for index, turn in enumerate(lagged([plan.stages() for plan in plans], REDUCE_LAG)):
         steps += turn
         if index + REDUCE_WINDOW < len(plans):
             steps.append(plans[index + REDUCE_WINDOW].begin)
     return steps + [plan.finish for plan in plans]
 
 
-def gather_first_kernel(groups, count, share, *refs):
-    source, tokens, target, mask = refs[:4]
-    gathered, tokens_other, target_other, mask_other, rim = refs[4:9]
-    sends, receives, local, swap_send, swap_recv = refs[9:]
-    at = Place(groups, count)
-    core = (at.group_swap, at.place)
-    greet(at.partners() + [core] + list(neighbours(at, -1)), count // 2 + 4)
-    swaps = [
-        remote(here, there, swap_send, swap_recv, index, core)
-        for index, (here, there) in enumerate(
-            ((tokens, tokens_other), (target, target_other), (mask, mask_other))
-        )
-    ]
-    length = tokens.shape[0]
-    tail = tokens.at[pl.ds(length - PAD, PAD)]
-    own_next, swap_next = neighbours(at, 1)
-    rims = [
-        remote(tail, rim.at[0], swap_send, swap_recv, 3, own_next),
-        remote(tail, rim.at[1], swap_send, swap_recv, 4, swap_next),
-    ]
-    plans = gather_plans(at, [source], [gathered], [share], sends, receives, local)
-
-    @pl.when(at.place < count - 1)
-    def _():
-        for copy in rims:
-            copy.start()
-
-    for copy in swaps:
-        copy.start()
-    for step in gather_steps(plans):
-        step()
-    for copy in swaps:
-        copy.wait()
-
-    @pl.when(at.place == 0)
-    def _():
-        rim[...] = jnp.zeros_like(rim)
-
-    @pl.when(at.place > 0)
-    def _():
-        for copy in rims:
-            copy.wait_recv()
-
-    @pl.when(at.place < count - 1)
-    def _():
-        for copy in rims:
-            copy.wait_send()
-
-
-def gather_first(source, tokens, target, mask, share):
-    groups, count = lax.axis_size("dp"), lax.axis_size("seq")
-    rows, width = source.shape
-    return pl.pallas_call(
-        functools.partial(gather_first_kernel, groups, count, share),
-        out_shape=[
-            jax.ShapeDtypeStruct((count, rows, width), source.dtype),
-            jax.ShapeDtypeStruct(tokens.shape, tokens.dtype),
-            jax.ShapeDtypeStruct(target.shape, target.dtype),
-            jax.ShapeDtypeStruct(mask.shape, mask.dtype),
-            jax.ShapeDtypeStruct((2, PAD, tokens.shape[1]), tokens.dtype),
-        ],
-        in_specs=[ANY] * 4,
-        out_specs=[ANY] * 4 + [ROOM],
-        scratch_shapes=[
-            *gather_sems(count, rows, 1),
-            pltpu.SemaphoreType.DMA((5,)),
-            pltpu.SemaphoreType.DMA((5,)),
-        ],
-        compiler_params=pltpu.CompilerParams(collective_id=3, has_side_effects=True),
-        name="gather_first",
-    )(source, tokens, target, mask)
-
-
 def reduce_buffers(groups, count, rows, width, share):
     wide, half = width - share, count // 2
-    steps = max(1, (groups // 4).bit_length() - 1)
     kind = jnp.bfloat16
+    far = (max(1, (groups // 4).bit_length() - 1), rows, width) if groups > 4 else (1, 16, 128)
     return [
         pltpu.VMEM((2, half, rows, wide), kind),
         pltpu.VMEM((2, half, rows, share), kind),
@@ -480,7 +421,9 @@
         pltpu.VMEM((half - 1, rows, wide), kind),
         pltpu.VMEM((rows, wide), kind),
         pltpu.VMEM((rows, wide), kind),
-        pltpu.VMEM((steps, rows, width), kind),
+        pltpu.VMEM((rows, width), kind),
+        pltpu.VMEM((rows, width), kind),
+        pltpu.VMEM(far, kind),
     ]
 
 
@@ -496,19 +439,18 @@
     return found
 
 
-def reduce_plans(at, givens, totals, others, shares, scratch):
-    number, rows = len(shares), givens[0].shape[2]
+def reduce_plans(at, works, scratch):
+    rows = works[0].given.shape[2]
     chunks = reduce_chunks(rows)
     lines = rows // chunks
-    sends, receives, local = scratch[7 * number * chunks : 7 * number * chunks + 3]
+    sends, receives, local = scratch[9 * len(works) * chunks : 9 * len(works) * chunks + 3]
     plans = []
-    for i in range(number):
+    for work in works:
         for part in range(chunks):
-            spot = i * chunks + part
+            spot = len(plans)
             plans.append(
                 Reduce(
-                    at, givens[i], totals[i], others[i], pl.ds(part * lines, lines), shares[i],
-                    scratch[7 * spot : 7 * spot + 7],
+                    at, work, pl.ds(part * lines, lines), scratch[9 * spot : 9 * spot + 9],
                     (sends.at[spot], receives.at[spot], local.at[spot]),
                 )
             )
@@ -519,16 +461,20 @@
     return max(1, min(REDUCE_CHUNKS, rows // 16))
 
 
-def reduce_scratch(groups, count, rows, widths, shares):
+def reduce_scratch(groups, count, rows, widths):
     scratch, chunks = [], reduce_chunks(rows)
-    for width, share in zip(widths, shares):
-        scratch += reduce_buffers(groups, count, rows // chunks, width, share) * chunks
+    for width in widths:
+        scratch += reduce_buffers(groups, count, rows // chunks, width, reduce_share(width)) * chunks
     number, copies = len(widths) * chunks, copies_of_reduce(groups, count)
     return scratch + [
         pltpu.SemaphoreType.DMA((number, copies)),
         pltpu.SemaphoreType.DMA((number, copies)),
         pltpu.SemaphoreType.DMA((number, 2)),
     ]
+
+
+def reduce_share(width):
+    return third(width, 0.28)
 
 
 class Relay:
@@ -613,15 +559,20 @@
         lax.fori_loop(0, rounds, body, 0)
         assert len(taken) == PAUSES
 
-    def around(self, count, turn, end, main):
-        pieces = self.pieces(count, end)
-        for index, found in enumerate(pieces):
-            if found:
-                pl.when(turn > index)(functools.partial(run_steps, found))
+    def around(self, rounds, turn, end, stage, main):
+        pieces = self.pieces(rounds, end)
+
+        def body(index, carry):
+            stage(index)
+            for other, found in enumerate(pieces):
+                if found:
+                    pl.when(index == other)(functools.partial(run_steps, found))
+            return carry
+
+        split = jnp.minimum(turn, rounds)
+        lax.fori_loop(0, split, body, 0)
         main()
-        for index, found in enumerate(pieces):
-            if found:
-                pl.when(turn <= index)(functools.partial(run_steps, found))
+        lax.fori_loop(split, rounds, body, 0)
 
 
 def run_steps(steps):
@@ -645,6 +596,10 @@
 def silu_parts(value):
     gate = jax.nn.sigmoid(value)
     return value * gate, gate * (1.0 + value * (1.0 - gate))
+
+
+def lane_start(start):
+    return start if isinstance(start, int) else tile_start(start)
 
 
 class Unit:
@@ -653,9 +608,9 @@
         self.mixed_ref, self.conv_ref = mixed_ref, conv_ref
         keys = heads * DK
         self.columns = [
-            (self.head * DK, DK),
-            (keys + self.head * DK, DK),
-            (2 * keys + self.head * DV, DV),
+            (lane_start(self.head * DK), DK),
+            (lane_start(keys + self.head * DK), DK),
+            (lane_start(2 * keys + self.head * DV), DV),
         ]
 
     def taps(self, part):
@@ -734,22 +689,82 @@
 
 def forward_kernel(groups, count, shares, *refs):
     number = len(shares)
-    mixed_ref, little_ref, gate_ref, conv_ref, head_ref, gain_ref = refs[:6]
-    sources, refs = refs[6 : 6 + number], refs[6 + number :]
-    branch_ref, out_ref, t_ref, u_ref, w_ref, m_ref, e_ref, s_ref = refs[:8]
-    targets, refs = refs[8 : 8 + number], refs[8 + number :]
-    b_ref, g_ref, grow_ref, sending, arriving, relay_send, relay_recv = refs[:7]
-    sends, receives, local = refs[7:]
+    tokens_ref, target_ref, mask_ref, norm_ref, conv_ref, head_ref, gain_ref = refs[:7]
+    sources, refs = refs[7 : 7 + number], refs[7 + number :]
+    inputs_ref, target_other, mask_other, mixed_ref, little_ref, gate_ref = refs[:6]
+    branch_ref, out_ref, t_ref, u_ref, w_ref, m_ref, e_ref, s_ref = refs[6:14]
+    targets, refs = refs[14 : 14 + number], refs[14 + number :]
+    normed, b_ref, g_ref, grow_ref, sending, arriving, relay_send, relay_recv = refs[:8]
+    swap_send, swap_recv, sends, receives, local = refs[8:]
     units = t_ref.shape[0]
     heads = units // 2
     size = t_ref.shape[1]
     half = size // 2
     at = Place(groups, count)
     line = Relay(at, True, units, sending, arriving, relay_send, relay_recv)
-    greet(at.partners() + [line.before], count // 2 + 2)
-    agenda = Agenda(gather_steps(gather_plans(at, sources, targets, shares, sends, receives, local)))
-    for step in agenda.take(WINDOW):
-        step()
+    core = (at.group_swap, at.place)
+    greet(at.partners() + [line.before, core] + list(neighbours(at, -1)), count // 2 + 5)
+    padded = size + PAD
+    swaps = [
+        remote(here, there, swap_send, swap_recv, index, core)
+        for index, (here, there) in enumerate((
+            (tokens_ref, inputs_ref.at[pl.ds(padded + PAD, size)]),
+            (target_ref, target_other),
+            (mask_ref, mask_other),
+        ))
+    ]
+    tail = tokens_ref.at[pl.ds(size - PAD, PAD)]
+    own_next, swap_next = neighbours(at, 1)
+    rims = [
+        remote(tail, inputs_ref.at[pl.ds(0, PAD)], swap_send, swap_recv, 3, own_next),
+        remote(tail, inputs_ref.at[pl.ds(padded, PAD)], swap_send, swap_recv, 4, swap_next),
+    ]
+    swaps[0].start()
+
+    @pl.when(at.place < count - 1)
+    def _():
+        for copy in rims:
+            copy.start()
+
+    plans = gather_plans(at, sources, targets, shares, sends, receives, local)
+    agenda = Agenda(gather_steps(plans))
+    run_steps(agenda.take(WINDOW))
+    for copy in swaps[1:]:
+        copy.start()
+    inputs_ref[PAD:padded] = tokens_ref[...]
+
+    @pl.when(at.place == 0)
+    def _():
+        inputs_ref[:PAD] = jnp.zeros((PAD, inputs_ref.shape[1]), jnp.bfloat16)
+        inputs_ref[padded : padded + PAD] = jnp.zeros((PAD, inputs_ref.shape[1]), jnp.bfloat16)
+
+    @pl.when(at.place > 0)
+    def _():
+        for copy in rims:
+            copy.wait_recv()
+
+    swaps[0].wait()
+    for seq in range(2):
+        value = inputs_ref[seq * padded : (seq + 1) * padded].astype(jnp.float32)
+        scale = lax.rsqrt(jnp.mean(value * value, axis=1, keepdims=True) + epsilon)
+        normed[seq * padded : (seq + 1) * padded] = (value * scale * norm_ref[...]).astype(jnp.bfloat16)
+    first_chunks = len(plans) // number
+    run_steps(agenda.take(agenda.steps.index(plans[first_chunks - 1].take_across) + 1))
+
+    weight = targets[0]
+    model = normed.shape[1]
+    mixed_width = mixed_ref.shape[2]
+    cuts = [0, mixed_width // 2, mixed_width, mixed_width + 128, weight.shape[2]]
+    for start, end in zip(cuts, cuts[1:]):
+        value = dense(normed[...], weight[:, :, start:end].reshape(model, end - start), ((1,), (0,)))
+        value = value.reshape(2, padded, end - start)
+        if end <= mixed_width:
+            mixed_ref[:, :, start:end] = value.astype(jnp.bfloat16)
+        elif end == mixed_width + 128:
+            little_ref[...] = value
+        else:
+            gate_ref[...] = value
+        agenda.until(agenda.done / len(agenda.steps) + FORWARD_PROJECT / 4)
     head_tables(little_ref, head_ref, g_ref, grow_ref)
 
     def local_stage(seq, head):
@@ -789,10 +804,6 @@
         drow, dcol = iotas(DK, DK)
         m_ref[unit] = jnp.where(drow == dcol, jnp.exp(last), 0.0) - near(weighted, back, TN)
         b_ref[unit] = near(weighted, update, TN)
-        queries = own.rows(0)
-        scores = near(queries, keys, NT) * decays
-        out_ref[unit] = near(scores, update)
-        e_ref[unit] = growth * queries - near(scores, back)
         yield
 
     agenda.loop(2, FORWARD_LOCAL, lambda seq: lockstep([local_stage(seq, h) for h in range(heads)]))
@@ -802,7 +813,16 @@
             line.receive(unit, s_ref)
             line.send(unit, lambda: close(m_ref[unit], s_ref[unit]) + b_ref[unit])
 
-    agenda.around(count, at.place, FORWARD_RELAY, pass_on)
+    def score_stage(unit):
+        seq, head = unit // heads, unit % heads
+        own = Unit(seq, head, heads, mixed_ref, conv_ref)
+        unused, gcol, grow = head_columns(seq, head, heads, little_ref, g_ref, grow_ref)
+        queries = own.rows(0)
+        scores = near(queries, own.rows(1), NT) * decay_table(gcol, grow)
+        out_ref[unit] = near(scores, u_ref[unit])
+        e_ref[unit] = jnp.exp(gcol) * queries - near(scores, w_ref[unit])
+
+    agenda.around(units, at.place, FORWARD_RELAY, score_stage, pass_on)
 
     def read_stage(seq, head):
         unit = seq * heads + head
@@ -818,22 +838,31 @@
         for head in range(heads):
             read_stage(seq, head)
             agenda.until(
-                FORWARD_RELAY + (1.0 - FORWARD_RELAY) * (seq * heads + head + 1) / units * 0.6
+                FORWARD_RELAY + (FORWARD_READ - FORWARD_RELAY) * (seq * heads + head + 1) / units
             )
     agenda.until(1.0)
     line.finish()
-
-
-FORWARD_LOCAL, FORWARD_RELAY = 0.5, 0.8
+    for copy in swaps[1:]:
+        copy.wait()
+
+    @pl.when(at.place < count - 1)
+    def _():
+        for copy in rims:
+            copy.wait_send()
+
+
+FORWARD_PROJECT, FORWARD_LOCAL, FORWARD_RELAY, FORWARD_READ = 0.04, 0.65, 0.85, 0.92
 BACK_OPEN, BACK_RELAY, BACK_GRADS = 0.15, 0.45, 0.85
 
 
-def forward_block(mixed_in, little, gate_pre, conv, head, gain, sources, shares):
+def forward_block(tokens, target, mask, norm_gain, conv, head, gain, sources, shares):
     groups, count = lax.axis_size("dp"), lax.axis_size("seq")
     number, rows = len(sources), sources[0].shape[0]
-    length = mixed_in.shape[1] - PAD
-    heads = conv.shape[1] // (2 * DK + DV)
+    length, model = tokens.shape
+    mixed_width = conv.shape[1]
+    heads = mixed_width // (2 * DK + DV)
     units = 2 * heads
+    padded = length + PAD
 
     def table(*shape):
         return jax.ShapeDtypeStruct((units,) + shape, jnp.float32)
@@ -841,6 +870,12 @@
     return pl.pallas_call(
         functools.partial(forward_kernel, groups, count, shares),
         out_shape=[
+            jax.ShapeDtypeStruct((2 * padded, model), tokens.dtype),
+            jax.ShapeDtypeStruct(target.shape, target.dtype),
+            jax.ShapeDtypeStruct(mask.shape, mask.dtype),
+            jax.ShapeDtypeStruct((2, padded, mixed_width), jnp.bfloat16),
+            jax.ShapeDtypeStruct((2, padded, 128), jnp.float32),
+            jax.ShapeDtypeStruct((2, padded, heads * DV), jnp.float32),
             jax.ShapeDtypeStruct((2, length, heads * DV), jnp.bfloat16),
             table(length, DV),
             table(length, length),
@@ -851,42 +886,49 @@
             table(DK, DV),
         ]
         + [jax.ShapeDtypeStruct((count,) + v.shape, v.dtype) for v in sources],
-        in_specs=[ROOM] * 6 + [ANY] * number,
-        out_specs=[ROOM] * 8 + [ANY] * number,
+        in_specs=[ROOM, ANY, ANY] + [ROOM] * 4 + [ANY] * number,
+        out_specs=[ROOM, ANY, ANY] + [ROOM] * 11 + [ROOM] + [ANY] * (number - 1),
         scratch_shapes=[
+            pltpu.VMEM((2 * padded, model), jnp.bfloat16),
             pltpu.VMEM((units, DK, DV), jnp.float32),
             pltpu.VMEM((2, length, 128), jnp.float32),
             pltpu.VMEM((2, 128, length), jnp.float32),
             *relay_scratch(units),
+            pltpu.SemaphoreType.DMA((5,)),
+            pltpu.SemaphoreType.DMA((5,)),
             *gather_sems(count, rows, number),
         ],
         compiler_params=pltpu.CompilerParams(
-            collective_id=4, has_side_effects=True, vmem_limit_bytes=56 * 2**20
+            collective_id=3, has_side_effects=True, vmem_limit_bytes=56 * 2**20
         ),
         name="forward_block",
-    )(mixed_in, little, gate_pre, conv, head, gain, *sources)
-
-
-def backward_kernel(groups, count, shares, *refs):
-    number = len(shares)
+    )(tokens, target, mask, norm_gain, conv, head, gain, *sources)
+
+
+def backward_kernel(groups, count, inner, *refs):
     mixed_ref, little_ref, gate_ref, conv_ref, head_ref, gain_ref = refs[:6]
     out_ref, t_ref, u_ref, w_ref, m_ref, e_ref, s_ref, branch_ref = refs[6:14]
-    givens, refs = refs[14 : 14 + number], refs[14 + number :]
-    grad_ref, conv_grad, gain_grad, head_grad = refs[:4]
-    totals, others = refs[4 : 4 + number], refs[4 + number : 4 + 2 * number]
-    refs = refs[4 + 2 * number :]
+    down_ref, up_ref, out_grad = refs[14:17]
+    grad_ref, conv_grad, gain_grad, head_grad, down_sum, gate_sum, out_sum = refs[17:24]
+    refs = refs[24:]
     do_ref, c_ref, ds_ref, lit_ref, g_ref, grow_ref = refs[:6]
-    sending, arriving, relay_send, relay_recv = refs[6:10]
+    x_ref, ahead_ref, k_ref, log_ref, less_ref = refs[6:11]
+    sending, arriving, relay_send, relay_recv = refs[11:15]
     units = t_ref.shape[0]
     heads = units // 2
     size = t_ref.shape[1]
-    mixed_width = mixed_ref.shape[2]
+    mixed_width, vals = mixed_ref.shape[2], branch_ref.shape[2]
     at = Place(groups, count)
     line = Relay(at, False, units, sending, arriving, relay_send, relay_recv)
     further = further_groups(at)
     partners = at.partners() + [(at.group_swap, at.place)] + further + [line.before]
     greet(partners, count // 2 + 3 + len(further))
-    plans = reduce_plans(at, givens, totals, others, shares, refs[10:])
+    works = [
+        Work(down_ref, 0, inner, reduce_share(inner), [(down_sum, 0, inner, 0)]),
+        Work(up_ref, 0, inner, reduce_share(inner), [(gate_sum, 0, inner, 0)]),
+        Work(out_grad, 0, vals, reduce_share(vals), [(out_sum, 0, vals, 0)]),
+    ]
+    plans = reduce_plans(at, works, refs[15:])
     agenda = Agenda(reduce_steps(plans))
     for step in agenda.take(REDUCE_WINDOW):
         step()
@@ -898,6 +940,7 @@
     gain_grad[...] = jnp.zeros_like(gain_grad)
     head_grad[...] = jnp.zeros_like(head_grad)
     lit_ref[...] = jnp.zeros_like(lit_ref)
+    log_ref[...] = jnp.zeros_like(log_ref)
 
     def gate_stage(seq, head):
         unit = seq * heads + head
@@ -927,50 +970,67 @@
             line.receive(unit, ds_ref)
             line.send(unit, lambda: close(m_ref[unit], ds_ref[unit], TN) + c_ref[unit])
 
-    agenda.around(count, count - 1 - at.place, BACK_RELAY, pass_on)
+    def score_stage(unit):
+        seq, head = unit // heads, unit % heads
+        own = Unit(seq, head, heads, mixed_ref, conv_ref)
+        unused, gcol, grow = head_columns(seq, head, heads, little_ref, g_ref, grow_ref)
+        queries, keys = own.rows(0), own.rows(1)
+        decays = decay_table(gcol, grow)
+        memory, grad_out = s_ref[unit], do_ref[unit]
+        update = u_ref[unit] - near(w_ref[unit], memory)
+        x_ref[unit] = update.astype(jnp.bfloat16)
+        scores = near(queries, keys, NT) * decays
+        ahead_ref[unit] = near(scores, grad_out, TN)
+        grad_scores = near(grad_out, update, NT)
+        total = grad_scores * scores
+        query_part = jnp.exp(gcol) * near(grad_out, memory, NT)
+        grad_dot = grad_scores * decays
+        own.taps_back(0, query_part + near(grad_dot, keys), grad_ref, conv_grad)
+        k_ref[unit] = near(grad_dot, queries, TN)
+        lane = lax.broadcasted_iota(jnp.int32, (size, 128), 1)
+        log_line = jnp.sum(queries * query_part, axis=1, keepdims=True) + jnp.sum(
+            total, axis=1, keepdims=True
+        )
+        log_ref[seq] += jnp.where(lane == head, log_line, 0.0)
+        less_ref[unit] = jnp.broadcast_to(jnp.sum(total, axis=0, keepdims=True), (8, size))
+
+    agenda.around(units, count - 1 - at.place, BACK_RELAY, score_stage, pass_on)
 
     def grad_stage(seq, head):
         unit = seq * heads + head
         own = Unit(seq, head, heads, mixed_ref, conv_ref)
         beta, gcol, grow = head_columns(seq, head, heads, little_ref, g_ref, grow_ref)
-        queries, keys, values = own.rows(0), own.rows(1), own.rows(2)
+        keys, values = own.rows(1), own.rows(2)
         decays = decay_table(gcol, grow)
         row, col = iotas(size, size)
         strict = row > col
         memory, after = s_ref[unit], ds_ref[unit]
-        grad_out = do_ref[unit]
         growth = jnp.exp(gcol)
         last = gcol[size - 1 :, :]
         weights = jnp.exp(last - gcol)
-        update = u_ref[unit] - near(w_ref[unit], memory)
+        update = x_ref[unit]
         yield
-        scores = near(queries, keys, NT) * decays
         keys_dot = jnp.where(strict, near(keys, keys, NT) * decays, 0.0)
-        yield
-        grad_update = near(scores, grad_out, TN) + near(keys * weights, after)
+        grad_update = ahead_ref[unit] + near(keys * weights, after)
         yield
         grad_wanted = near(t_ref[unit], grad_update, TN)
         yield
         grad_system = -near(grad_wanted, update, NT)
-        grad_scores = near(grad_out, update, NT)
         through = keys_dot * grad_system
-        total = grad_scores * scores + beta * through
+        total = beta * through
         yield
-        query_part = growth * near(grad_out, memory, NT)
         key_read = growth * near(grad_wanted, memory, NT)
         key_part = beta * key_read
         end_part = weights * near(update, after, NT)
         yield
-        grad_dot = grad_scores * decays
         grad_keys_dot = jnp.where(strict, grad_system * decays, 0.0) * beta
-        grad_q = query_part + near(grad_dot, keys)
         grad_k = (
-            end_part - key_part + near(grad_dot, queries, TN)
+            end_part - key_part + k_ref[unit]
             + near(grad_keys_dot, keys) + near(grad_keys_dot, keys, TN)
         )
         yield
-        own.taps_back(0, grad_q, grad_ref, conv_grad)
         own.taps_back(1, grad_k, grad_ref, conv_grad)
+        yield
         own.taps_back(2, beta * grad_wanted, grad_ref, conv_grad)
         yield
         end_line = jnp.sum(keys * end_part, axis=1, keepdims=True)
@@ -979,8 +1039,9 @@
             - jnp.sum(keys * key_read, axis=1, keepdims=True)
             + jnp.sum(through, axis=1, keepdims=True)
         )
+        lane = lax.broadcasted_iota(jnp.int32, (size, 128), 1)
         grad_log = (
-            jnp.sum(queries * query_part, axis=1, keepdims=True)
+            jnp.sum(jnp.where(lane == head, log_ref[seq], 0.0), axis=1, keepdims=True)
             - jnp.sum(keys * key_part, axis=1, keepdims=True)
             - end_line
             + jnp.sum(total, axis=1, keepdims=True)
@@ -991,16 +1052,16 @@
         spot = lax.broadcasted_iota(jnp.int32, (size, 1), 0)
         grad_log = grad_log + jnp.where(spot == size - 1, grad_last, 0.0)
         later = (col >= row).astype(jnp.float32)
-        lane = lax.broadcasted_iota(jnp.int32, (size, 128), 1)
-        less = jnp.broadcast_to(jnp.sum(total, axis=0, keepdims=True), (128, size))
+        less = jnp.sum(total, axis=0, keepdims=True) + less_ref[unit][0:1]
+        less = jnp.broadcast_to(less, (128, size))
         grad_forget = exact(later, jnp.broadcast_to(grad_log, (size, 128))) - exact(later, less, NT)
         rate, bias = head_ref[0:1], head_ref[1:2]
         little = little_ref[own.seq, PAD:, :]
         on_forget = lane == heads + own.head
         grad_soft = jnp.where(on_forget, grad_forget * rate * jax.nn.sigmoid(little + bias), 0.0)
         forget = rate * jax.nn.softplus(little + bias)
-        log_line = jnp.sum(jnp.where(on_forget, grad_forget * forget, 0.0), axis=0, keepdims=True)
-        head_grad[0:1] += log_line
+        log_total = jnp.sum(jnp.where(on_forget, grad_forget * forget, 0.0), axis=0, keepdims=True)
+        head_grad[0:1] += log_total
         head_grad[1:2] += jnp.sum(grad_soft, axis=0, keepdims=True)
         lit_ref[own.seq] += grad_soft + jnp.where(
             lane == own.head, grad_beta * beta * (1.0 - beta), 0.0
@@ -1013,25 +1074,27 @@
     line.finish()
 
 
-def backward_block(mixed_in, little, gate_pre, conv, head, gain, kept, grad_branch, givens, shares):
+def backward_block(mixed_in, little, gate_pre, conv, head, gain, kept, grad_branch, grad_down, grad_up, grad_out):
     groups, count = lax.axis_size("dp"), lax.axis_size("seq")
-    number, rows = len(givens), givens[0].shape[2]
+    rows, inner = grad_down.shape[2:]
     length = mixed_in.shape[1] - PAD
     units = kept[0].shape[0]
-    widths = [v.shape[3] for v in givens]
-    results = [jax.ShapeDtypeStruct((rows, width), jnp.bfloat16) for width in widths]
-    total_width = mixed_in.shape[2] + 128 + gate_pre.shape[2]
+    vals = gate_pre.shape[2]
+    total_width = mixed_in.shape[2] + 128 + vals
+    joined = jax.ShapeDtypeStruct((rows, 2 * inner), jnp.bfloat16)
     return pl.pallas_call(
-        functools.partial(backward_kernel, groups, count, shares),
+        functools.partial(backward_kernel, groups, count, inner),
         out_shape=[
             jax.ShapeDtypeStruct((2, length + PAD, total_width), jnp.bfloat16),
             jax.ShapeDtypeStruct(conv.shape, jnp.float32),
             jax.ShapeDtypeStruct((8, DV), jnp.float32),
             jax.ShapeDtypeStruct((8, 128), jnp.float32),
-        ]
-        + results * 2,
-        in_specs=[ROOM] * 14 + [ANY] * number,
-        out_specs=[ROOM] * (4 + 2 * number),
+            joined,
+            joined,
+            jax.ShapeDtypeStruct((rows, 2 * vals), jnp.bfloat16),
+        ],
+        in_specs=[ROOM] * 14 + [ANY] * 3,
+        out_specs=[ROOM] * 7,
         scratch_shapes=[
             pltpu.VMEM((units, length, DV), jnp.float32),
             pltpu.VMEM((units, DK, DV), jnp.float32),
@@ -1039,46 +1102,108 @@
             pltpu.VMEM((2, length, 128), jnp.float32),
             pltpu.VMEM((2, length, 128), jnp.float32),
             pltpu.VMEM((2, 128, length), jnp.float32),
+            pltpu.VMEM((units, length, DV), jnp.bfloat16),
+            pltpu.VMEM((units, length, DV), jnp.float32),
+            pltpu.VMEM((units, length, DK), jnp.float32),
+            pltpu.VMEM((2, length, 128), jnp.float32),
+            pltpu.VMEM((units, 8, length), jnp.float32),
             *relay_scratch(units),
-            *reduce_scratch(groups, count, rows, widths, shares),
+            *reduce_scratch(groups, count, rows, [inner, inner, vals]),
         ],
         compiler_params=pltpu.CompilerParams(
             collective_id=5, has_side_effects=True, vmem_limit_bytes=60 * 2**20
         ),
         name="backward_block",
-    )(mixed_in, little, gate_pre, conv, head, gain, *kept, grad_branch, *givens)
-
-
-def reduce_first_kernel(groups, count, share, *refs):
-    given, swap, rims, small = refs[:4]
-    total, other, swap_got, rim_got, small_sum = refs[4:9]
-    scratch = refs[9:]
-    small_got, small_hold, swap_send, swap_recv, small_send, small_recv = scratch[-6:]
+    )(mixed_in, little, gate_pre, conv, head, gain, *kept, grad_branch, grad_down, grad_up, grad_out)
+
+
+def final_kernel(groups, count, widths, *refs):
+    keys, vals, inner = widths
+    tokens_ref, gain_ref, first_ref, weight_ref, hidden_ref = refs[:5]
+    conv_grad, gain_grad, head_grad, second_grad, loss_ref = refs[5:10]
+    up_ref = refs[10]
+    token_grad, small_sum, up_sum, in_sum, little_sum = refs[11:16]
+    normed, wide_grad, part_ref, weight, given = refs[16:21]
+    swap, swap_got, rims, rim_got, small_got, small_hold = refs[21:27]
+    weight_sem, swap_send, swap_recv, small_send, small_recv = refs[27:32]
     at = Place(groups, count)
+    core = at.group % 2
     further = further_groups(at)
-    core = (at.group_swap, at.place)
-    stages = []
-    distance = 1
+    pair = (at.group_swap, at.place)
+    rounds, distance = [], 1
     while distance < groups:
-        stages.append((at.group + distance - 2 * distance * ((at.group // distance) % 2), at.place))
+        rounds.append((at.group + distance - 2 * distance * ((at.group // distance) % 2), at.place))
         distance *= 2
     distance = 1
     while distance < count:
-        stages.append((at.group, at.place + distance - 2 * distance * ((at.place // distance) % 2)))
+        rounds.append((at.group, at.place + distance - 2 * distance * ((at.place // distance) % 2)))
         distance *= 2
-    partners = at.partners() + [core] + further + stages + list(neighbours(at, 1))
-    greet(partners, count // 2 + 4 + len(further) + len(stages))
+    partners = at.partners() + [pair] + further + rounds + list(neighbours(at, 1))
+    greet(partners, count // 2 + 4 + len(further) + len(rounds))
+
+    mixed = 2 * keys + vals
+    first_width = first_ref.shape[1]
+    works = [
+        Work(up_ref, inner, inner, reduce_share(inner), [(up_sum, 0, inner, 0)]),
+        Work(
+            given, 0, first_width, reduce_share(first_width),
+            [
+                (in_sum, 0, keys, 0),
+                (in_sum, 2 * keys, keys, keys),
+                (in_sum, 4 * keys, vals, 2 * keys),
+                (little_sum, 0, 128, mixed),
+                (in_sum, 4 * keys + 2 * vals, vals, mixed + 128),
+            ],
+        ),
+    ]
+    plans = reduce_plans(at, works, refs[32:])
+    chunks = len(plans) // len(works)
+    agenda = Agenda(reduce_steps(plans))
+    opening = agenda.steps.index(plans[chunks].begin)
+    run_steps(agenda.take(REDUCE_WINDOW))
+    fetch = pltpu.make_async_copy(weight_ref, weight, weight_sem)
+    fetch.start()
+
+    gain = gain_ref[...]
+
+    def norm_rows(first, number):
+        value = tokens_ref[first : first + number].astype(jnp.float32)
+        scale = lax.rsqrt(jnp.mean(value * value, axis=1, keepdims=True) + epsilon)
+        return scale, value * scale
+
+    height = tokens_ref.shape[0]
+    for first in range(0, height, height // 2):
+        normed[first : first + height // 2] = (norm_rows(first, height // 2)[1] * gain).astype(jnp.bfloat16)
+    half, unused, rows, unused = given.shape
+    blocks = [(start, min(640, first_width - start)) for start in range(0, first_width, 640)]
+    for index, (start, width) in enumerate(blocks):
+        wide_grad[:, :width] = dense(
+            normed[...], first_ref[:, start : start + width], ((0,), (0,))
+        ).astype(jnp.bfloat16)
+        for place in range(2 * half):
+            given[place // 2, place % 2, :, start : start + width] = wide_grad[
+                place * rows : (place + 1) * rows, :width
+            ]
+        run_steps(agenda.take(opening * FINAL_BLOCKS * (index + 1) // (100 * len(blocks))))
+    fetch.wait()
+    model = tokens_ref.shape[1]
+    for start in range(0, model, model // 4):
+        part_ref[:, start : start + model // 4] = dense(
+            first_ref[...], weight[start : start + model // 4], ((1,), (1,))
+        )
+        run_steps(agenda.take(
+            opening * (FINAL_BLOCKS + (100 - FINAL_BLOCKS) * (start + model // 4) // model) // 100
+        ))
+    length = height // 2 - PAD
+    swap[...] = part_ref[length + 2 * PAD :].astype(jnp.bfloat16)
+    rims[0] = part_ref[:PAD].astype(jnp.bfloat16)
+    rims[1] = part_ref[length + PAD : length + 2 * PAD].astype(jnp.bfloat16)
     own_back, swap_back = neighbours(at, -1)
-    swapped = remote(swap, swap_got, swap_send, swap_recv, 0, core)
+    swapped = remote(swap, swap_got, swap_send, swap_recv, 0, pair)
     rim_copies = [
         remote(rims.at[0], rim_got.at[0], swap_send, swap_recv, 1, own_back),
         remote(rims.at[1], rim_got.at[1], swap_send, swap_recv, 2, swap_back),
     ]
-    plans = reduce_plans(at, [given], [total], [other], [share], scratch)
-    steps = reduce_steps(plans)
-    for step in steps[: min(REDUCE_WINDOW, len(plans))]:
-        step()
-    steps = steps[min(REDUCE_WINDOW, len(plans)) :]
     swapped.start()
 
     @pl.when(at.place > 0)
@@ -1086,32 +1211,63 @@
         for copy in rim_copies:
             copy.start()
 
-    small_hold[0] = small[...]
+    gain_first = jnp.zeros((1, model), jnp.float32)
+    for first in range(0, height, height // 2):
+        unit = norm_rows(first, height // 2)[1]
+        product = unit * part_ref[first : first + height // 2]
+        gain_first = gain_first + jnp.sum(product, axis=0, keepdims=True)
+    small_hold[0] = jnp.zeros(small_hold.shape[1:], jnp.float32)
+    for start, width, source in ((0, keys, 0), (2 * keys, keys, keys), (4 * keys, vals, 2 * keys)):
+        span = pl.ds(tile_start(start + core * width), width)
+        small_hold[0, 0:CONV, span] = conv_grad[0:CONV, source : source + width]
+    small_hold[0, 4:5, 0:model] = gain_first
+    small_hold[0, 4:5, model : 2 * model] = second_grad[...]
+    small_hold[0, 4:5, 2 * model : 2 * model + DV] = gain_grad[0:1]
+    heads = keys // DK
+    for line in range(2):
+        found = head_grad[line : line + 1]
+        moved = pltpu.roll(head_grad[...], 128 - heads, 1)[line : line + 1]
+        small_hold[0, 5:6, 128 * line : 128 * line + 128] = jnp.where(core == 0, moved, found)
+    small_hold[0, 5:6, 256:384] = loss_ref[...]
 
     def add_small(index):
-        copy = remote(
-            small_hold.at[index], small_got.at[index], small_send, small_recv, index, stages[index]
-        )
-        copy.start()
-        copy.wait()
-        small_hold[index + 1] = small_hold[index] + small_got[index]
-
-    for index in range(max(len(steps), len(stages))):
-        if index < len(steps):
-            steps[index]()
-        if index < len(stages):
-            add_small(index)
-    small_sum[...] = small_hold[len(stages)]
-    swapped.wait()
-
-    @pl.when(at.place == count - 1)
-    def _():
-        rim_got[...] = jnp.zeros_like(rim_got)
-
-    @pl.when(at.place < count - 1)
-    def _():
-        for copy in rim_copies:
-            copy.wait_recv()
+        return remote(
+            small_hold.at[index], small_got.at[index], small_send, small_recv, index, rounds[index]
+        )
+
+    left = agenda.pieces(len(rounds) + 1, 1.0)
+    for index, found in enumerate(left):
+        if index > 0:
+            add_small(index - 1).wait()
+            small_hold[index] = small_hold[index - 1] + small_got[index - 1]
+        if index < len(rounds):
+            add_small(index).start()
+        if index == 1:
+            swapped.wait()
+
+            @pl.when(at.place == count - 1)
+            def _():
+                rim_got[...] = jnp.zeros_like(rim_got)
+
+            @pl.when(at.place < count - 1)
+            def _():
+                for copy in rim_copies:
+                    copy.wait_recv()
+
+            edge = rim_got[0].astype(jnp.float32) + rim_got[1].astype(jnp.float32)
+            step = length // 4
+            for first in range(0, length, step):
+                scale, unit = norm_rows(PAD + first, step)
+                grad = part_ref[PAD + first : PAD + first + step] + swap_got[
+                    first : first + step
+                ].astype(jnp.float32)
+                if first + step == length:
+                    grad = jnp.concatenate([grad[: step - PAD], grad[step - PAD :] + edge], axis=0)
+                scaled = grad * gain
+                back = scale * (scaled - unit * jnp.mean(scaled * unit, axis=1, keepdims=True))
+                token_grad[first : first + step] = hidden_ref[first : first + step] + back
+        run_steps(found)
+    small_sum[...] = small_hold[len(rounds)]
 
     @pl.when(at.place > 0)
     def _():
@@ -1119,36 +1275,65 @@
             copy.wait_send()
 
 
-def reduce_first(given, swap, rims, small, share):
+FINAL_BLOCKS = 60
+
+
+def final_block(
+    inputs, gain, grad_first, w_first, grad_hidden, grad_conv, grad_gain, grad_head, grad_second,
+    loss_row, grad_up, vals,
+):
     groups, count = lax.axis_size("dp"), lax.axis_size("seq")
-    rows, width = given.shape[2:]
+    rows = grad_up.shape[2]
+    inner = grad_up.shape[3] // 2
+    first_width = grad_first.shape[1]
+    keys = (first_width - 128 - 2 * vals) // 2
+    height, model = inputs.shape
+    length = height // 2 - PAD
     rounds = (groups.bit_length() - 1) + (count.bit_length() - 1)
-    result = jax.ShapeDtypeStruct((rows, width), jnp.bfloat16)
+    small = (8, 4 * keys + 2 * vals)
+    kind = jnp.bfloat16
+
+    def joined(width):
+        return jax.ShapeDtypeStruct((rows, width), kind)
+
     return pl.pallas_call(
-        functools.partial(reduce_first_kernel, groups, count, share),
+        functools.partial(final_kernel, groups, count, (keys, vals, inner)),
         out_shape=[
-            result,
-            result,
-            jax.ShapeDtypeStruct(swap.shape, swap.dtype),
-            jax.ShapeDtypeStruct(rims.shape, rims.dtype),
-            jax.ShapeDtypeStruct(small.shape, small.dtype),
+            jax.ShapeDtypeStruct((length, model), jnp.float32),
+            jax.ShapeDtypeStruct(small, jnp.float32),
+            joined(2 * inner),
+            joined(4 * keys + 4 * vals),
+            joined(256),
         ],
-        in_specs=[ANY, ROOM, ROOM, ROOM],
+        in_specs=[ROOM] * 3 + [ANY] + [ROOM] * 6 + [ANY],
         out_specs=[ROOM] * 5,
-        scratch_shapes=reduce_scratch(groups, count, rows, [width], [share])
-        + [
-            pltpu.VMEM((rounds,) + small.shape, jnp.float32),
-            pltpu.VMEM((rounds + 1,) + small.shape, jnp.float32),
+        scratch_shapes=[
+            pltpu.VMEM((height, model), kind),
+            pltpu.VMEM((model, 640), kind),
+            pltpu.VMEM((height, model), jnp.float32),
+            pltpu.VMEM((model, first_width), kind),
+            pltpu.VMEM((count // 2, 2, rows, first_width), kind),
+            pltpu.VMEM((length, model), kind),
+            pltpu.VMEM((length, model), kind),
+            pltpu.VMEM((2, PAD, model), kind),
+            pltpu.VMEM((2, PAD, model), kind),
+            pltpu.VMEM((rounds,) + small, jnp.float32),
+            pltpu.VMEM((rounds + 1,) + small, jnp.float32),
+            pltpu.SemaphoreType.DMA,
             pltpu.SemaphoreType.DMA((3,)),
             pltpu.SemaphoreType.DMA((3,)),
             pltpu.SemaphoreType.DMA((rounds,)),
             pltpu.SemaphoreType.DMA((rounds,)),
+            *reduce_scratch(groups, count, rows, [inner, first_width]),
         ],
         compiler_params=pltpu.CompilerParams(
-            collective_id=6, has_side_effects=True, vmem_limit_bytes=56 * 2**20
+            collective_id=6, has_side_effects=True, vmem_limit_bytes=60 * 2**20
         ),
-        name="reduce_first",
-    )(given, swap, rims, small)
+        name="final_block",
+    )(
+        inputs, gain, grad_first, w_first, grad_hidden, grad_conv, grad_gain, grad_head,
+        grad_second, loss_row, grad_up,
+    )
 
 
 def third(width, weight):
@@ -1218,19 +1403,6 @@
 
     mask_own = valid[0].astype(jnp.float32)
     mask_rows = jnp.broadcast_to(mask_own[None, :], (8, length))
-    w_first, tokens_other, target_other, mask_other, rim = gather_first(
-        part_first, tokens[0], target[0], mask_rows, third(first_width, 0.33)
-    )
-    w_first = w_first.reshape(model, first_width)
-
-    inputs = jnp.concatenate([rim[0], tokens[0], rim[1], tokens_other], axis=0).astype(jnp.float32)
-    first_scale, first_unit = norm_parts(inputs)
-    normed = (first_unit * gain_first).astype(jnp.bfloat16)
-    project = dense(normed, w_first, ((1,), (0,))).reshape(2, padded, first_width)
-    mixed_in = project[..., :mixed_width].astype(jnp.bfloat16)
-    little = project[..., mixed_width : mixed_width + 128]
-    gate_pre = project[..., mixed_width + 128 :]
-
     own_conv = jnp.concatenate([qkv_half(conv_weight), jnp.zeros((8 - CONV, mixed_width))], axis=0)
     lanes = ((0, 0), (heads, 128 - 2 * heads))
     head = jnp.concatenate(
@@ -1242,20 +1414,25 @@
         axis=0,
     )
     gain_row = gain_out[None]
-    rests = [part_out, part_up, part_down]
-    branch, *kept, w_out, w_up, w_down = forward_block(
-        mixed_in, little, gate_pre, own_conv, head, gain_row,
-        rests, [third(v.shape[1], 0.33) for v in rests],
+    parts = [part_first, part_out, part_up, part_down]
+    (
+        inputs, target_other, mask_other, mixed_in, little, gate_pre, branch, *kept,
+        w_first, w_out, w_up, w_down,
+    ) = forward_block(
+        tokens[0], target[0], mask_rows, gain_first[None], own_conv, head, gain_row,
+        parts, [third(v.shape[1], 0.33) for v in parts],
     )
     branch = branch.reshape(both, vals)
-    w_out, w_up, w_down = (v.reshape(model, v.shape[2]) for v in (w_out, w_up, w_down))
+    w_first, w_out, w_up, w_down = (
+        v.reshape(model, v.shape[2]) for v in (w_first, w_out, w_up, w_down)
+    )
 
     def core_sum(part):
         pairs = [(group, group ^ 1) for group in range(groups)]
         got = lax.ppermute(part.astype(jnp.bfloat16), "dp", pairs)
         return part + jnp.concatenate([got[length:], got[:length]], axis=0).astype(jnp.float32)
 
-    positions = jnp.concatenate([tokens[0], tokens_other], axis=0).astype(jnp.float32)
+    positions = jnp.concatenate([tokens[0], inputs[padded + PAD :]], axis=0).astype(jnp.float32)
     hidden = positions + core_sum(dense(branch, w_out, ((1,), (1,))))
     second_scale, second_unit = norm_parts(hidden)
     second = (second_unit * gain_second).astype(jnp.bfloat16)
@@ -1281,103 +1458,53 @@
     grad_out = dense(grad_attn, branch, ((0,), (0,))).astype(jnp.bfloat16)
     grad_branch = dense(grad_attn, w_out, ((1,), (0,))).reshape(2, length, vals)
 
-    grad_rests = [grad_down, grad_up, grad_out]
-    grad_first, grad_conv, grad_gain_out, grad_head, *reduced = backward_block(
+    def by_place(array):
+        return array.reshape(count // 2, 2, rows, array.shape[1])
+
+    grad_up = by_place(grad_up)
+    grad_first, grad_conv, grad_gain_out, grad_head, sum_down, sum_gate, sum_out = backward_block(
         mixed_in, little, gate_pre, own_conv, head, gain_row, kept, grad_branch,
-        [v.reshape(count // 2, 2, rows, v.shape[1]) for v in grad_rests],
-        [third(v.shape[1], 0.28) for v in grad_rests],
+        by_place(grad_down), grad_up, by_place(grad_out),
     )
-    grad_first = grad_first.reshape(2 * padded, first_width)
-    grad_w_first = dense(normed, grad_first, ((0,), (0,))).astype(jnp.bfloat16)
-    normed_part = dense(grad_first, w_first, ((1,), (1,)))
-    grad_gain_first = jnp.sum(normed_part * first_unit, axis=0)
-    normed_part = normed_part.reshape(2, padded, model)
-
-    def place_half(array, start, width, values):
-        at = array.ndim - 1
-        return lax.dynamic_update_slice_in_dim(array, values, start + core * width, at)
-
-    all_conv = jnp.zeros(conv_weight.shape, jnp.float32)
-    all_conv = place_half(all_conv, 0, keys, grad_conv[:CONV, :keys])
-    all_conv = place_half(all_conv, KEYS, keys, grad_conv[:CONV, keys : 2 * keys])
-    all_conv = place_half(all_conv, 2 * KEYS, vals, grad_conv[:CONV, 2 * keys :])
-    no_heads = jnp.zeros((HEADS,), jnp.float32)
-    smalls = [
-        grad_gain_first,
-        grad_gain_second,
-        grad_gain_out[0],
-        all_conv.reshape(-1),
-        place_half(no_heads, 0, heads, grad_head[0, heads : 2 * heads]),
-        place_half(no_heads, 0, heads, grad_head[1, heads : 2 * heads]),
-        loss_part[None],
-        jnp.sum(mask_own)[None],
-    ]
-    sizes = [v.shape[0] for v in smalls]
-    extra = -sum(sizes) % 1024
-    packed = jnp.concatenate(smalls + [jnp.zeros((extra,), jnp.float32)]).reshape(-1, 128)
-    total_first, other_first, swap_got, rim_got, small_sum = reduce_first(
-        grad_w_first.reshape(count // 2, 2, rows, first_width),
-        normed_part[1, PAD:].astype(jnp.bfloat16),
-        normed_part[:, :PAD].astype(jnp.bfloat16),
-        packed,
-        third(first_width, 0.28),
+    loss_row = jnp.concatenate(
+        [loss_part[None], jnp.sum(mask_own)[None], jnp.zeros((126,), jnp.float32)]
+    )[None]
+    grad_tokens, small_sum, sum_up, sum_in, sum_small = final_block(
+        inputs, gain_first[None], grad_first.reshape(2 * padded, first_width), w_first,
+        grad_hidden[:length], grad_conv, grad_gain_out, grad_head, grad_gain_second[None],
+        loss_row, grad_up, vals,
     )
-    small_flat = small_sum.reshape(-1)
-    found, start = [], 0
-    for size in sizes:
-        found.append(small_flat[start : start + size])
-        start += size
-    valid_count = jnp.maximum(found[7][0], 1.0)
-    loss_value = found[6][0] / valid_count
+    valid_count = jnp.maximum(small_sum[5, 257], 1.0)
+    loss_value = small_sum[5, 256] / valid_count
     factor = length * groups * count / valid_count
-
-    rim_rows = jnp.sum(rim_got.astype(jnp.float32), axis=0)
-    grad_normed = normed_part[0, PAD:] + swap_got.astype(jnp.float32)
-    grad_normed = jnp.concatenate(
-        [grad_normed[: length - PAD], grad_normed[length - PAD :] + rim_rows], axis=0
+    sum_small = jnp.concatenate(
+        [
+            sum_small[:, 0:heads],
+            sum_small[:, 128 : 128 + heads],
+            sum_small[:, heads : 2 * heads],
+            sum_small[:, 128 + heads : 128 + 2 * heads],
+        ],
+        axis=1,
     )
-    grad_tokens = grad_hidden[:length] + norm_back(
-        first_scale[PAD:padded], first_unit[PAD:padded], gain_first, grad_normed
-    )
-
-    def join(own, other, start, width):
-        own_part, other_part = own[:, start : start + width], other[:, start : start + width]
-        low = jnp.where(core == 0, own_part, other_part)
-        high = jnp.where(core == 0, other_part, own_part)
-        return [low, high]
-
-    def joined(parts):
-        return jnp.concatenate(parts, axis=1).astype(jnp.float32) * factor
-
-    pair_first = (total_first, other_first)
-    pair_down, pair_up, pair_out = ((reduced[i], reduced[3 + i]) for i in range(3))
-    result_in = joined(
-        join(*pair_first, 0, keys)
-        + join(*pair_first, keys, keys)
-        + join(*pair_first, 2 * keys, vals)
-        + join(*pair_first, mixed_width + 128, vals)
-    )
-    result_small = joined(
-        join(*pair_first, mixed_width, heads) + join(*pair_first, mixed_width + heads, heads)
-    )
-    result_out = joined(join(*pair_out, 0, vals))
-    result_up = joined(join(*pair_up, 0, inner) + join(*pair_up, inner, inner))
-    result_down = joined(join(*pair_down, 0, inner))
+
+    def scaled(array):
+        return array.astype(jnp.float32) * factor
+
     return (
         summed[:length].astype(jnp.bfloat16)[None],
         loss_value,
-        (grad_tokens * factor)[None],
-        result_in,
-        result_small,
-        result_out,
-        result_up,
-        result_down,
-        found[0] * factor,
-        found[1] * factor,
-        found[2] * factor,
-        found[3].reshape(conv_weight.shape) * factor,
-        found[4] * factor,
-        found[5] * factor,
+        scaled(grad_tokens)[None],
+        scaled(sum_in),
+        scaled(sum_small),
+        scaled(sum_out),
+        scaled(jnp.concatenate([sum_gate, sum_up], axis=1)),
+        scaled(sum_down),
+        scaled(small_sum[4, :model]),
+        scaled(small_sum[4, model : 2 * model]),
+        scaled(small_sum[4, 2 * model : 2 * model + DV]),
+        scaled(small_sum[:CONV]),
+        scaled(small_sum[5, :HEADS]),
+        scaled(small_sum[5, 128 : 128 + HEADS]),
     )
 
 

time: 540 us -> 476 us (0.88)
  matrix products: 46.7 us -> 30 us
  other arithmetic: 42 us -> 25.6 us
  local copies, waits for them, and re-layouts: 32.2 us -> 16.6 us
  Pallas kernels: 399 us -> 388 us
    pallas_call x3 -> x2, Pallas kernels: 282 us -> 223 us  [the longest x1 125 us: backward_block(): pl.pallas_call(functools.partial(backward_kernel, groups, count, inner),...]
    pallas_call x1, Pallas kernels: 118 us -> 165 us  [forward_block(): pl.pallas_call(functools.partial(forward_kernel, groups, count, shares),...]
    dot_general x12 -> x9, matrix products: 46.7 us -> 30 us  [dense(): lax.dot_general(left, right, (dims, ((), ())), preferred_element_type=jnp...]
    unnamed x9 -> x1, other arithmetic: 9.66 us -> 0.01 us
    unnamed x101 -> x46, local copies, waits for them, and re-layouts: 9.24 us -> 2.41 us
  transfers between devices with their start and end apart: 3 -> 3, of which waited for: 2 -> 2; matrix products, arithmetic and copies ran while one was open for 2% -> 3% of each run, Pallas kernels for 0% -> 0%
where the time goes in v4:
time: 476 us; the launch traced here: 467 us
  Pallas kernels  388 us (82%)
  matrix products  30 us (6%)
  other arithmetic  25.6 us (5%)
  local copies, waits for them, and re-layouts  16.6 us (3%)
    pallas_call x1, Pallas kernels, forward_block(): pl.pallas_call(functools.partial(forward_kernel, groups, count, shares),...  165 us
    pallas_call x1, Pallas kernels, backward_block(): pl.pallas_call(functools.partial(backward_kernel, groups, count, inner),...  125 us
    pallas_call x1, Pallas kernels, final_block(): pl.pallas_call(functools.partial(final_kernel, groups, count, (keys, vals...  98.1 us
    dot_general x9, matrix products, dense(): lax.dot_general(left, right, (dims, ((), ())), preferred_element_type=jnp...  30 us
    mul x9, other arithmetic, scaled(): return array.astype(jnp.float32) * factor  11.6 us
  transfers between devices with their start and end apart: 3, of which 2 were waited for; matrix products, arithmetic and copies ran while one was open for 3% of the time, Pallas kernels for 0%

profile of v4, /device:TPU:0, one launch (start us, length us, event | category | flops | bytes accessed | tf_op | source)
XLA Modules:
  0.0 467.2 jit_solution(16236590070965322541)
XLA Ops:
  4.1 1.6 constant_dynamic-slice_fusion.3.refs_8_
  6.5 1.0 constant_dynamic-slice_fusion.8
  7.5 1.1 constant_dynamic-slice_fusion.4
  12.5 165.3 %forward_block.1 = (bf16[544,1024]{1,0:T(8,128)(2,1)}, bf16[256,1024]{1,0:T(8,128)(2,1)}, f32[8,256]{1,0:T(8,128)}, bf16[2,272,1536]{2,1,0:T(8,128)(2,1)}, f32[2...) custom-call(bf16[256,1024]{1,0:T(8,128)(2,1)} %bitcast.54, ...), custom_call_target="tpu_custom_call" | custom-call | tf_op jit(solution)/shard_map/forward_block/pallas_call | solution.py:870
  177.8 2.7 fusion.20
  180.6 1.2 slice.79
  181.8 1.4 collective-permute-done
  184.7 3.2 fusion.7
  188.7 1.0 copy-done.18
  189.7 1.8 fusion.21
  193.2 1.1 collective-permute-done.1
  194.4 1.8 convert_subtract_fusion
  196.3 4.0 fusion.8
  201.7 5.0 %fusion.22 = (bf16[512,1024]{1,0:T(8,128)(2,1)S(1)}, f32[512,1024]{1,0:T(8,128)S(1)}) fusion(bf16[1024,2816]{1,0:T(8,128)(2,1)S(1)} %bitcast.84, f32[512,1408]{1,0:T(8,128)} %get-tuple-element.95, f32[512,1408]{1,0:T(8,128)S(1)} %get-tuple-element.94), kind=kOutput, calls=%fused_computation.83 | convolution fusion | flops 2956197888 | bytes 14680064 | tf_op jit(solution)/shard_map/dot_general | solution.py:1354
  207.0 1.9 maximum_bitcast_fusion.refs_9_
  208.9 3.6 convolution_convert_fusion.1
  212.5 5.4 %convolution_convert_fusion = bf16[1024,2816]{1,0:T(8,128)(2,1)} fusion(f32[512,1408]{1,0:T(8,128)S(1)} %copy-done.19, f32[512,1408]{1,0:T(8,128)S(1)} %get-tuple-element.94, f32[512,1024]{1,0:T(8,128)S(1)} %broadcast_multiply_fusion, f32[1024]{0:T(1024)S(1)} %copy-done.14), kind=kOutput, calls=%fused_computation.1 | convolution fusion | flops 2959605760 | bytes 13635584 | tf_op jit(solution)/shard_map/dot_general | solution.py:1354
  219.8 1.0 slice.114.refs_4_
  221.3 2.2 convolution_convert_fusion.2
  223.4 2.1 fusion.23.refs_13_
  225.6 124.7 %backward_block.1 = (bf16[2,272,2432]{2,1,0:T(8,128)(2,1)}, f32[8,1536]{1,0:T(8,128)}, f32[8,256]{1,0:T(8,128)}, f32[8,128]{1,0:T(8,128)}, bf16[128,2816]{1,0:T(...) custom-call(bf16[2,272,1536]{2,1,0:T(8,128)(2,1)} %get-tuple-element.49.refs_0_, ...), custom_call_target="tpu_custom_call" | custom-call | tf_op jit(solution)/shard_map/backward_block/pallas_call | solution.py:1085
  350.3 98.1 %final_block.1 = (f32[256,1024]{1,0:T(8,128)}, f32[8,3072]{1,0:T(8,128)}, bf16[128,2816]{1,0:T(8,128)(2,1)}, bf16[128,4608]{1,0:T(8,128)(2,1)}, bf16[128,256]{1,0:T(8,128)(2,1)}) custom-call(bf16[544,1024]{1,0:T(8,128)(2,1)} %get-tuple-element.44.refs_0_, f32[1,1024]{1,0:T(1,128)} %bitcast.73, bf16[544,2432]{1,0:T(8,128)(2,1)} %bitcast.60, ...), custom_call_target="tpu_custom_call" | custom-call | tf_op jit(solution)/shard_map/final_block/pallas_call | solution.py:1299
  448.4 1.4 fusion.18
  450.4 1.3 slice_multiply_fusion.5
  451.7 1.2 multiply_bitcast_fusion.1
  452.9 1.4 slice_multiply_fusion.3
  454.2 1.5 slice_multiply_fusion.2
  456.4 2.3 multiply_bitcast_fusion
  459.2 1.0 convert_multiply_fusion.3
  460.2 1.2 convert_multiply_fusion.2
  461.4 1.6 convert_multiply_fusion.1
  463.1 1.9 convert_multiply_fusion
  (89 shorter events, 17.4 us)
Async XLA Ops:
  0.6 5.1 %copy-start = (bf16[128,2816]{1,0:T(8,128)(2,1)S(1)}, bf16[128,2816]{1,0:T(8,128)(2,1)}, u32[]{:S(2)}) copy-start(bf16[128,2816]{1,0:T(8,128)(2,1)} %param.21) | copy-start | bytes 2162692
  0.7 7.9 %copy-start.12 = (bf16[128,5632]{1,0:T(8,128)(2,1)S(1)}, bf16[128,5632]{1,0:T(8,128)(2,1)}, u32[]{:S(2)}) copy-start(bf16[128,5632]{1,0:T(8,128)(2,1)} %param.20) | copy-start | bytes 4325380
  6.5 3.1 copy-start.16
  6.5 3.1 copy-start.17
  180.5 2.8 copy-start.2
  180.5 2.7 collective-permute-start
  180.6 3.6 slice-start
  183.3 1.4 slice-start.1
  183.8 0.9 copy-start.14
  187.9 1.8 copy-start.18
  189.7 2.9 copy-start.15
  191.6 2.8 copy-start.3
  191.6 2.8 copy-start.10
  191.6 2.7 collective-permute-start.1
  206.8 11.1 %collective-permute-start.2 = (bf16[512,1024]{1,0:T(8,128)(2,1)S(1)}, bf16[512,1024]{1,0:T(8,128)(2,1)S(1)}, u32[]{:S(2)}, u32[]{:S(2)}) collective-permute-start(bf16[512,1024]{1,0:T(8,128)(2,1)S(1)} %get-tuple-element.126), channel_id=1, source_target_pairs={{0,8},{8,0},{16,24},{24,16},{1,9},{9,1},{17,25},{25,17},{2,10},{10... | collective-permute-start | bytes 3145736 | tf_op jit(solution)/shard_map/ppermute | solution.py:1432
  208.9 3.6 copy-start.19
  219.8 1.5 copy-start.6
  221.3 2.2 copy-start.4
  448.3 10.4 %copy-start.13 = (bf16[128,256]{1,0:T(8,128)(2,1)S(1)}, bf16[128,256]{1,0:T(8,128)(2,1)}, u32[]{:S(2)}) copy-start(bf16[128,256]{1,0:T(8,128)(2,1)} %get-tuple-element.69) | copy-start | bytes 196612
  448.3 10.8 %copy-start.11 = (bf16[128,1536]{1,0:T(8,128)(2,1)S(1)}, bf16[128,1536]{1,0:T(8,128)(2,1)}, u32[]{:S(2)}) copy-start(bf16[128,1536]{1,0:T(8,128)(2,1)} %get-tuple-element.70) | copy-start | bytes 1179652
  448.3 11.8 %copy-start.9 = (bf16[128,2816]{1,0:T(8,128)(2,1)S(1)}, bf16[128,2816]{1,0:T(8,128)(2,1)}, u32[]{:S(2)}) copy-start(bf16[128,2816]{1,0:T(8,128)(2,1)} %get-tuple-element.73) | copy-start | bytes 2162692
  458.7 2.6 copy-start.5
  461.4 1.7 copy-start.7
  461.4 1.8 copy-start.8
  463.0 2.6 copy-start.1

commit v5 on v4

--- a/solution.py
+++ b/solution.py
@@ -215,21 +215,21 @@
 class Reduce:
     def __init__(self, at, work, lines, buffers, sems):
         self.at, self.given, self.spots, self.lines = at, work.given, work.spots, lines
-        self.acc, self.from_across, self.from_beside, self.from_along = buffers[:4]
-        self.part, self.from_plane, self.total, self.other, self.far = buffers[4:]
         self.sends, self.receives, self.local = sems
         width, share = work.width, work.share
         self.wide = width - share
+        wide, narrow, full = pl.ds(0, self.wide), pl.ds(0, share), pl.ds(0, width)
+        self.acc = buffers[0].at[:, :, :, wide]
+        self.from_across = buffers[1].at[:, :, :, narrow]
+        self.from_beside, self.from_along = buffers[2].at[:, :, wide], buffers[3].at[:, :, wide]
+        self.part, self.from_plane = buffers[4].at[:, wide], buffers[5].at[:, wide]
+        self.total, self.other = buffers[6].at[:, full], buffers[7].at[:, full]
+        self.far = buffers[8].at[:, :, full] if at.groups > 4 else None
         self.own = pl.ds(tile_start(at.plane * share), self.wide)
         self.given_own = pl.ds(tile_start(work.base + at.plane * share), self.wide)
         self.given_lent = pl.ds(tile_start(work.base + (1 - at.plane) * self.wide), share)
         self.inner = pl.ds(tile_start(at.plane * (width - 2 * share)), share)
         self.theirs = pl.ds(tile_start((1 - at.plane) * share), self.wide)
-        self.started = {}
-
-    def launch(self, make, *where):
-        make(*where).start()
-        self.started[make.__name__, where] = make
 
     def side(self, mine):
         return self.at.side if mine else 1 - self.at.side
@@ -284,7 +284,7 @@
     def begin(self):
         for mine in range(2):
             self.load(mine).start()
-            self.launch(self.across, mine)
+            self.across(mine).start()
 
     def add_across(self, mine):
         self.load(mine).wait()
@@ -293,7 +293,7 @@
         got = self.from_across[mine].astype(jnp.float32)
         self.acc[mine, :, :, self.inner] = (held + got).astype(jnp.bfloat16)
         if not mine:
-            self.launch(self.beside)
+            self.beside().start()
 
     def add_beside(self):
         self.beside().wait_recv()
@@ -303,7 +303,7 @@
             got = self.from_beside[pair].astype(jnp.float32)
             self.acc[1, pair] = (held + got).astype(jnp.bfloat16)
             if step < self.at.half:
-                self.launch(self.along, step)
+                self.along(step).start()
 
     def add_along(self):
         value = self.acc[1, self.at.pair].astype(jnp.float32)
@@ -311,7 +311,7 @@
             self.along(step).wait_recv()
             value = value + self.from_along[step - 1].astype(jnp.float32)
         self.part[...] = value.astype(jnp.bfloat16)
-        self.launch(self.plane)
+        self.plane().start()
 
     def add_plane(self):
         self.plane().wait_recv()
@@ -329,19 +329,21 @@
             got = self.far[index].astype(jnp.float32)
             self.total[...] = (self.total[...].astype(jnp.float32) + got).astype(jnp.bfloat16)
             distance *= 2
-        self.launch(self.core)
+        self.core().start()
 
     def deliver(self):
         self.core().wait_recv()
         core = self.at.group % 2
-        for target, start, width, source in self.spots:
+        for target, start, stride, width, source in self.spots:
             for held, which in ((self.total, core), (self.other, 1 - core)):
-                span = pl.ds(tile_start(start + which * width), width)
+                span = pl.ds(tile_start(start + which * stride), width)
                 target[self.lines, span] = held[:, source : source + width]
 
     def finish(self):
-        for (unused, where), make in self.started.items():
-            make(*where).wait_send()
+        copies = [self.across(0), self.across(1), self.beside(), self.plane(), self.core()]
+        copies += [self.along(step) for step in range(1, self.at.half)]
+        for copy in copies:
+            copy.wait_send()
 
     def stages(self):
         return [
@@ -357,7 +359,7 @@
 ROOM = pl.BlockSpec(memory_space=pltpu.VMEM)
 PAD = 16
 CHUNKS, WINDOW, GATHER_LAG = 4, 2, 1
-REDUCE_CHUNKS, REDUCE_WINDOW, REDUCE_LAG = 4, 2, 1
+REDUCE_CHUNKS, REDUCE_WINDOW, REDUCE_LAG, POOL = 4, 2, 1, 6
 
 
 def neighbours(at, step):
@@ -405,9 +407,12 @@
     steps = [plan.begin for plan in plans[:REDUCE_WINDOW]]
     for index, turn in enumerate(lagged([plan.stages() for plan in plans], REDUCE_LAG)):
         steps += turn
-        if index + REDUCE_WINDOW < len(plans):
-            steps.append(plans[index + REDUCE_WINDOW].begin)
-    return steps + [plan.finish for plan in plans]
+        later = index + REDUCE_WINDOW
+        if later < len(plans):
+            if later >= POOL:
+                steps.append(plans[later - POOL].finish)
+            steps.append(plans[later].begin)
+    return steps + [plan.finish for plan in plans[-POOL:]]
 
 
 def reduce_buffers(groups, count, rows, width, share):
@@ -443,14 +448,15 @@
     rows = works[0].given.shape[2]
     chunks = reduce_chunks(rows)
     lines = rows // chunks
-    sends, receives, local = scratch[9 * len(works) * chunks : 9 * len(works) * chunks + 3]
+    sends, receives, local = scratch[9 * POOL : 9 * POOL + 3]
     plans = []
     for work in works:
         for part in range(chunks):
             spot = len(plans)
+            slot = spot % POOL
             plans.append(
                 Reduce(
-                    at, work, pl.ds(part * lines, lines), scratch[9 * spot : 9 * spot + 9],
+                    at, work, pl.ds(part * lines, lines), scratch[9 * slot : 9 * slot + 9],
                     (sends.at[spot], receives.at[spot], local.at[spot]),
                 )
             )
@@ -462,9 +468,9 @@
 
 
 def reduce_scratch(groups, count, rows, widths):
-    scratch, chunks = [], reduce_chunks(rows)
-    for width in widths:
-        scratch += reduce_buffers(groups, count, rows // chunks, width, reduce_share(width)) * chunks
+    chunks = reduce_chunks(rows)
+    width = max(widths)
+    scratch = reduce_buffers(groups, count, rows // chunks, width, reduce_share(width)) * POOL
     number, copies = len(widths) * chunks, copies_of_reduce(groups, count)
     return scratch + [
         pltpu.SemaphoreType.DMA((number, copies)),
@@ -852,7 +858,7 @@
 
 
 FORWARD_PROJECT, FORWARD_LOCAL, FORWARD_RELAY, FORWARD_READ = 0.04, 0.65, 0.85, 0.92
-BACK_OPEN, BACK_RELAY, BACK_GRADS = 0.15, 0.45, 0.85
+BACK_OPEN, BACK_RELAY, BACK_GRADS, BACK_BLOCKS, BACK_PART = 0.06, 0.22, 0.42, 0.5, 0.58
 
 
 def forward_block(tokens, target, mask, norm_gain, conv, head, gain, sources, shares):
@@ -905,33 +911,70 @@
     )(tokens, target, mask, norm_gain, conv, head, gain, *sources)
 
 
-def backward_kernel(groups, count, inner, *refs):
+def backward_kernel(groups, count, *refs):
     mixed_ref, little_ref, gate_ref, conv_ref, head_ref, gain_ref = refs[:6]
     out_ref, t_ref, u_ref, w_ref, m_ref, e_ref, s_ref, branch_ref = refs[6:14]
-    down_ref, up_ref, out_grad = refs[14:17]
-    grad_ref, conv_grad, gain_grad, head_grad, down_sum, gate_sum, out_sum = refs[17:24]
-    refs = refs[24:]
+    tokens_ref, norm_ref, hidden_ref, second_grad, loss_ref = refs[14:19]
+    weight_ref, down_ref, up_ref, out_grad = refs[19:23]
+    token_grad, small_sum, down_sum, gate_sum, up_sum, out_sum, in_sum, little_sum, given = refs[23:32]
+    refs = refs[32:]
     do_ref, c_ref, ds_ref, lit_ref, g_ref, grow_ref = refs[:6]
     x_ref, ahead_ref, k_ref, log_ref, less_ref = refs[6:11]
     sending, arriving, relay_send, relay_recv = refs[11:15]
+    grad_ref, conv_grad, gain_grad, head_grad = refs[15:19]
+    normed, wide_grad, part_ref, weight = refs[19:23]
+    swap, swap_got, rims, rim_got, small_got = refs[23:28]
+    wide_sem, weight_sem, swap_send, swap_recv, small_send, small_recv = refs[28:34]
+    scratch = refs[34:]
     units = t_ref.shape[0]
     heads = units // 2
     size = t_ref.shape[1]
     mixed_width, vals = mixed_ref.shape[2], branch_ref.shape[2]
     at = Place(groups, count)
     line = Relay(at, False, units, sending, arriving, relay_send, relay_recv)
+    core = at.group % 2
     further = further_groups(at)
-    partners = at.partners() + [(at.group_swap, at.place)] + further + [line.before]
-    greet(partners, count // 2 + 3 + len(further))
+    pair = (at.group_swap, at.place)
+    rounds, distance = [], 1
+    while distance < groups:
+        rounds.append((at.group + distance - 2 * distance * ((at.group // distance) % 2), at.place))
+        distance *= 2
+    distance = 1
+    while distance < count:
+        rounds.append((at.group, at.place + distance - 2 * distance * ((at.place // distance) % 2)))
+        distance *= 2
+    partners = at.partners() + [pair, line.before] + further + rounds + list(neighbours(at, 1))
+    greet(partners, count // 2 + 5 + len(further) + len(rounds))
+    keys_width, inner = heads * DK, down_ref.shape[3]
+    first_width = grad_ref.shape[2]
+    cut = 2 * FINAL_COLUMNS
     works = [
-        Work(down_ref, 0, inner, reduce_share(inner), [(down_sum, 0, inner, 0)]),
-        Work(up_ref, 0, inner, reduce_share(inner), [(gate_sum, 0, inner, 0)]),
-        Work(out_grad, 0, vals, reduce_share(vals), [(out_sum, 0, vals, 0)]),
+        Work(down_ref, 0, inner, reduce_share(inner), [(down_sum, 0, inner, inner, 0)]),
+        Work(up_ref, 0, inner, reduce_share(inner), [(gate_sum, 0, inner, inner, 0)]),
+        Work(out_grad, 0, vals, reduce_share(vals), [(out_sum, 0, vals, vals, 0)]),
+        Work(up_ref, inner, inner, reduce_share(inner), [(up_sum, 0, inner, inner, 0)]),
+        Work(
+            given, 0, cut, reduce_share(cut),
+            [
+                (in_sum, 0, keys_width, keys_width, 0),
+                (in_sum, 2 * keys_width, keys_width, keys_width, keys_width),
+                (in_sum, 4 * keys_width, vals, cut - 2 * keys_width, 2 * keys_width),
+            ],
+        ),
+        Work(
+            given, cut, first_width - cut, reduce_share(first_width - cut),
+            [
+                (in_sum, 2 * keys_width + cut, vals, mixed_width - cut, 0),
+                (little_sum, 0, 128, 128, mixed_width - cut),
+                (in_sum, 4 * keys_width + 2 * vals, vals, vals, mixed_width + 128 - cut),
+            ],
+        ),
     ]
-    plans = reduce_plans(at, works, refs[15:])
+    plans = reduce_plans(at, works, scratch)
+    chunks = len(plans) // len(works)
     agenda = Agenda(reduce_steps(plans))
-    for step in agenda.take(REDUCE_WINDOW):
-        step()
+    openings = [agenda.steps.index(plans[chunks * 4].begin), agenda.steps.index(plans[chunks * 5].begin)]
+    run_steps(agenda.take(REDUCE_WINDOW))
     head_tables(little_ref, head_ref, g_ref, grow_ref)
     grad_ref[:, :PAD, mixed_width:] = jnp.zeros(
         (2, PAD, grad_ref.shape[2] - mixed_width), jnp.bfloat16
@@ -1070,101 +1113,9 @@
 
     agenda.loop(2, BACK_GRADS, lambda seq: lockstep([grad_stage(seq, h) for h in range(heads)]))
     grad_ref[:, PAD:, mixed_width : mixed_width + 128] = lit_ref[...].astype(jnp.bfloat16)
-    agenda.until(1.0)
     line.finish()
 
-
-def backward_block(mixed_in, little, gate_pre, conv, head, gain, kept, grad_branch, grad_down, grad_up, grad_out):
-    groups, count = lax.axis_size("dp"), lax.axis_size("seq")
-    rows, inner = grad_down.shape[2:]
-    length = mixed_in.shape[1] - PAD
-    units = kept[0].shape[0]
-    vals = gate_pre.shape[2]
-    total_width = mixed_in.shape[2] + 128 + vals
-    joined = jax.ShapeDtypeStruct((rows, 2 * inner), jnp.bfloat16)
-    return pl.pallas_call(
-        functools.partial(backward_kernel, groups, count, inner),
-        out_shape=[
-            jax.ShapeDtypeStruct((2, length + PAD, total_width), jnp.bfloat16),
-            jax.ShapeDtypeStruct(conv.shape, jnp.float32),
-            jax.ShapeDtypeStruct((8, DV), jnp.float32),
-            jax.ShapeDtypeStruct((8, 128), jnp.float32),
-            joined,
-            joined,
-            jax.ShapeDtypeStruct((rows, 2 * vals), jnp.bfloat16),
-        ],
-        in_specs=[ROOM] * 14 + [ANY] * 3,
-        out_specs=[ROOM] * 7,
-        scratch_shapes=[
-            pltpu.VMEM((units, length, DV), jnp.float32),
-            pltpu.VMEM((units, DK, DV), jnp.float32),
-            pltpu.VMEM((units, DK, DV), jnp.float32),
-            pltpu.VMEM((2, length, 128), jnp.float32),
-            pltpu.VMEM((2, length, 128), jnp.float32),
-            pltpu.VMEM((2, 128, length), jnp.float32),
-            pltpu.VMEM((units, length, DV), jnp.bfloat16),
-            pltpu.VMEM((units, length, DV), jnp.float32),
-            pltpu.VMEM((units, length, DK), jnp.float32),
-            pltpu.VMEM((2, length, 128), jnp.float32),
-            pltpu.VMEM((units, 8, length), jnp.float32),
-            *relay_scratch(units),
-            *reduce_scratch(groups, count, rows, [inner, inner, vals]),
-        ],
-        compiler_params=pltpu.CompilerParams(
-            collective_id=5, has_side_effects=True, vmem_limit_bytes=60 * 2**20
-        ),
-        name="backward_block",
-    )(mixed_in, little, gate_pre, conv, head, gain, *kept, grad_branch, grad_down, grad_up, grad_out)
-
-
-def final_kernel(groups, count, widths, *refs):
-    keys, vals, inner = widths
-    tokens_ref, gain_ref, first_ref, weight_ref, hidden_ref = refs[:5]
-    conv_grad, gain_grad, head_grad, second_grad, loss_ref = refs[5:10]
-    up_ref = refs[10]
-    token_grad, small_sum, up_sum, in_sum, little_sum = refs[11:16]
-    normed, wide_grad, part_ref, weight, given = refs[16:21]
-    swap, swap_got, rims, rim_got, small_got, small_hold = refs[21:27]
-    weight_sem, swap_send, swap_recv, small_send, small_recv = refs[27:32]
-    at = Place(groups, count)
-    core = at.group % 2
-    further = further_groups(at)
-    pair = (at.group_swap, at.place)
-    rounds, distance = [], 1
-    while distance < groups:
-        rounds.append((at.group + distance - 2 * distance * ((at.group // distance) % 2), at.place))
-        distance *= 2
-    distance = 1
-    while distance < count:
-        rounds.append((at.group, at.place + distance - 2 * distance * ((at.place // distance) % 2)))
-        distance *= 2
-    partners = at.partners() + [pair] + further + rounds + list(neighbours(at, 1))
-    greet(partners, count // 2 + 4 + len(further) + len(rounds))
-
-    mixed = 2 * keys + vals
-    first_width = first_ref.shape[1]
-    works = [
-        Work(up_ref, inner, inner, reduce_share(inner), [(up_sum, 0, inner, 0)]),
-        Work(
-            given, 0, first_width, reduce_share(first_width),
-            [
-                (in_sum, 0, keys, 0),
-                (in_sum, 2 * keys, keys, keys),
-                (in_sum, 4 * keys, vals, 2 * keys),
-                (little_sum, 0, 128, mixed),
-                (in_sum, 4 * keys + 2 * vals, vals, mixed + 128),
-            ],
-        ),
-    ]
-    plans = reduce_plans(at, works, refs[32:])
-    chunks = len(plans) // len(works)
-    agenda = Agenda(reduce_steps(plans))
-    opening = agenda.steps.index(plans[chunks].begin)
-    run_steps(agenda.take(REDUCE_WINDOW))
-    fetch = pltpu.make_async_copy(weight_ref, weight, weight_sem)
-    fetch.start()
-
-    gain = gain_ref[...]
+    gain = norm_ref[...]
 
     def norm_rows(first, number):
         value = tokens_ref[first : first + number].astype(jnp.float32)
@@ -1174,26 +1125,55 @@
     height = tokens_ref.shape[0]
     for first in range(0, height, height // 2):
         normed[first : first + height // 2] = (norm_rows(first, height // 2)[1] * gain).astype(jnp.bfloat16)
+    model = tokens_ref.shape[1]
+    quarter = model // 4
+
+    def fetch(index):
+        return pltpu.make_async_copy(
+            weight_ref.at[pl.ds(index * quarter, quarter)], weight.at[index % 2], weight_sem.at[index % 2]
+        )
+
+    def store(start, width):
+        return pltpu.make_async_copy(
+            wide_grad.at[:, :, :, pl.ds(0, width)], given.at[:, :, :, pl.ds(start, width)], wide_sem
+        )
+
+    padded = height // 2
+    fetch(0).start()
+    fetch(1).start()
     half, unused, rows, unused = given.shape
-    blocks = [(start, min(640, first_width - start)) for start in range(0, first_width, 640)]
+    blocks = [
+        (start, min(FINAL_COLUMNS, first_width - start))
+        for start in range(0, first_width, FINAL_COLUMNS)
+    ]
     for index, (start, width) in enumerate(blocks):
-        wide_grad[:, :width] = dense(
-            normed[...], first_ref[:, start : start + width], ((0,), (0,))
-        ).astype(jnp.bfloat16)
-        for place in range(2 * half):
-            given[place // 2, place % 2, :, start : start + width] = wide_grad[
-                place * rows : (place + 1) * rows, :width
-            ]
-        run_steps(agenda.take(opening * FINAL_BLOCKS * (index + 1) // (100 * len(blocks))))
-    fetch.wait()
-    model = tokens_ref.shape[1]
-    for start in range(0, model, model // 4):
-        part_ref[:, start : start + model // 4] = dense(
-            first_ref[...], weight[start : start + model // 4], ((1,), (1,))
-        )
-        run_steps(agenda.take(
-            opening * (FINAL_BLOCKS + (100 - FINAL_BLOCKS) * (start + model // 4) // model) // 100
-        ))
+        if index > 0:
+            store(*blocks[index - 1]).wait()
+        for part in range(4):
+            value = sum(
+                dense(
+                    normed[seq * padded : (seq + 1) * padded, part * quarter : (part + 1) * quarter],
+                    grad_ref[seq, :, start : start + width],
+                    ((0,), (0,)),
+                )
+                for seq in range(2)
+            ).astype(jnp.bfloat16)
+            for line in range(quarter // rows):
+                place = part * (quarter // rows) + line
+                wide_grad[place // 2, place % 2, :, :width] = value[line * rows : (line + 1) * rows]
+        store(start, width).start()
+        aim = BACK_GRADS + (BACK_BLOCKS - BACK_GRADS) * (index + 1) / len(blocks)
+        run_steps(agenda.take(min(int(len(agenda.steps) * aim), openings[0])))
+    store(*blocks[-1]).wait()
+    for index in range(4):
+        fetch(index).wait()
+        for seq in range(2):
+            part_ref[
+                seq * padded : (seq + 1) * padded, index * quarter : (index + 1) * quarter
+            ] = dense(grad_ref[seq], weight[index % 2], ((1,), (1,)))
+        if index + 2 < 4:
+            fetch(index + 2).start()
+        agenda.until(BACK_BLOCKS + (BACK_PART - BACK_BLOCKS) * (index + 1) / 4)
     length = height // 2 - PAD
     swap[...] = part_ref[length + 2 * PAD :].astype(jnp.bfloat16)
     rims[0] = part_ref[:PAD].astype(jnp.bfloat16)
@@ -1216,30 +1196,33 @@
         unit = norm_rows(first, height // 2)[1]
         product = unit * part_ref[first : first + height // 2]
         gain_first = gain_first + jnp.sum(product, axis=0, keepdims=True)
-    small_hold[0] = jnp.zeros(small_hold.shape[1:], jnp.float32)
-    for start, width, source in ((0, keys, 0), (2 * keys, keys, keys), (4 * keys, vals, 2 * keys)):
+    small_sum[...] = jnp.zeros_like(small_sum)
+    for start, width, source in (
+        (0, keys_width, 0),
+        (2 * keys_width, keys_width, keys_width),
+        (4 * keys_width, vals, 2 * keys_width),
+    ):
         span = pl.ds(tile_start(start + core * width), width)
-        small_hold[0, 0:CONV, span] = conv_grad[0:CONV, source : source + width]
-    small_hold[0, 4:5, 0:model] = gain_first
-    small_hold[0, 4:5, model : 2 * model] = second_grad[...]
-    small_hold[0, 4:5, 2 * model : 2 * model + DV] = gain_grad[0:1]
-    heads = keys // DK
+        small_sum[0:CONV, span] = conv_grad[0:CONV, source : source + width]
+    small_sum[4:5, 0:model] = gain_first
+    small_sum[4:5, model : 2 * model] = second_grad[...]
+    small_sum[4:5, 2 * model : 2 * model + DV] = gain_grad[0:1]
     for line in range(2):
         found = head_grad[line : line + 1]
         moved = pltpu.roll(head_grad[...], 128 - heads, 1)[line : line + 1]
-        small_hold[0, 5:6, 128 * line : 128 * line + 128] = jnp.where(core == 0, moved, found)
-    small_hold[0, 5:6, 256:384] = loss_ref[...]
+        small_sum[5:6, 128 * line : 128 * line + 128] = jnp.where(core == 0, moved, found)
+    small_sum[5:6, 256:384] = loss_ref[...]
 
     def add_small(index):
         return remote(
-            small_hold.at[index], small_got.at[index], small_send, small_recv, index, rounds[index]
+            small_sum, small_got.at[index], small_send, small_recv, index, rounds[index]
         )
 
     left = agenda.pieces(len(rounds) + 1, 1.0)
     for index, found in enumerate(left):
         if index > 0:
             add_small(index - 1).wait()
-            small_hold[index] = small_hold[index - 1] + small_got[index - 1]
+            small_sum[...] += small_got[index - 1]
         if index < len(rounds):
             add_small(index).start()
         if index == 1:
@@ -1267,7 +1250,6 @@
                 back = scale * (scaled - unit * jnp.mean(scaled * unit, axis=1, keepdims=True))
                 token_grad[first : first + step] = hidden_ref[first : first + step] + back
         run_steps(found)
-    small_sum[...] = small_hold[len(rounds)]
 
     @pl.when(at.place > 0)
     def _():
@@ -1275,20 +1257,21 @@
             copy.wait_send()
 
 
-FINAL_BLOCKS = 60
-
-
-def final_block(
-    inputs, gain, grad_first, w_first, grad_hidden, grad_conv, grad_gain, grad_head, grad_second,
-    loss_row, grad_up, vals,
+FINAL_COLUMNS = 640
+
+
+def backward_block(
+    mixed_in, little, gate_pre, conv, head, gain, kept, grad_branch, inputs, norm_gain, grad_hidden,
+    grad_second, loss_row, w_first, grad_down, grad_up, grad_out,
 ):
     groups, count = lax.axis_size("dp"), lax.axis_size("seq")
-    rows = grad_up.shape[2]
-    inner = grad_up.shape[3] // 2
-    first_width = grad_first.shape[1]
-    keys = (first_width - 128 - 2 * vals) // 2
+    rows, inner = grad_down.shape[2:]
+    length = mixed_in.shape[1] - PAD
+    units = kept[0].shape[0]
+    mixed_width, vals = mixed_in.shape[2], gate_pre.shape[2]
+    first_width = mixed_width + 128 + vals
+    keys = (mixed_width - vals) // 2
     height, model = inputs.shape
-    length = height // 2 - PAD
     rounds = (groups.bit_length() - 1) + (count.bit_length() - 1)
     small = (8, 4 * keys + 2 * vals)
     kind = jnp.bfloat16
@@ -1297,42 +1280,61 @@
         return jax.ShapeDtypeStruct((rows, width), kind)
 
     return pl.pallas_call(
-        functools.partial(final_kernel, groups, count, (keys, vals, inner)),
+        functools.partial(backward_kernel, groups, count),
         out_shape=[
             jax.ShapeDtypeStruct((length, model), jnp.float32),
             jax.ShapeDtypeStruct(small, jnp.float32),
             joined(2 * inner),
+            joined(2 * inner),
+            joined(2 * inner),
+            joined(2 * vals),
             joined(4 * keys + 4 * vals),
             joined(256),
+            jax.ShapeDtypeStruct((count // 2, 2, rows, first_width), kind),
         ],
-        in_specs=[ROOM] * 3 + [ANY] + [ROOM] * 6 + [ANY],
-        out_specs=[ROOM] * 5,
+        in_specs=[ROOM] * 19 + [ANY] * 4,
+        out_specs=[ROOM] * 8 + [ANY],
         scratch_shapes=[
+            pltpu.VMEM((units, length, DV), jnp.float32),
+            pltpu.VMEM((units, DK, DV), jnp.float32),
+            pltpu.VMEM((units, DK, DV), jnp.float32),
+            pltpu.VMEM((2, length, 128), jnp.float32),
+            pltpu.VMEM((2, length, 128), jnp.float32),
+            pltpu.VMEM((2, 128, length), jnp.float32),
+            pltpu.VMEM((units, length, DV), kind),
+            pltpu.VMEM((units, length, DV), jnp.float32),
+            pltpu.VMEM((units, length, DK), jnp.float32),
+            pltpu.VMEM((2, length, 128), jnp.float32),
+            pltpu.VMEM((units, 8, length), jnp.float32),
+            *relay_scratch(units),
+            pltpu.VMEM((2, length + PAD, first_width), kind),
+            pltpu.VMEM(conv.shape, jnp.float32),
+            pltpu.VMEM((8, DV), jnp.float32),
+            pltpu.VMEM((8, 128), jnp.float32),
             pltpu.VMEM((height, model), kind),
-            pltpu.VMEM((model, 640), kind),
+            pltpu.VMEM((count // 2, 2, rows, FINAL_COLUMNS), kind),
             pltpu.VMEM((height, model), jnp.float32),
-            pltpu.VMEM((model, first_width), kind),
-            pltpu.VMEM((count // 2, 2, rows, first_width), kind),
+            pltpu.VMEM((2, model // 4, first_width), kind),
             pltpu.VMEM((length, model), kind),
             pltpu.VMEM((length, model), kind),
             pltpu.VMEM((2, PAD, model), kind),
             pltpu.VMEM((2, PAD, model), kind),
             pltpu.VMEM((rounds,) + small, jnp.float32),
-            pltpu.VMEM((rounds + 1,) + small, jnp.float32),
             pltpu.SemaphoreType.DMA,
+            pltpu.SemaphoreType.DMA((2,)),
             pltpu.SemaphoreType.DMA((3,)),
             pltpu.SemaphoreType.DMA((3,)),
             pltpu.SemaphoreType.DMA((rounds,)),
             pltpu.SemaphoreType.DMA((rounds,)),
-            *reduce_scratch(groups, count, rows, [inner, first_width]),
+            *reduce_scratch(groups, count, rows, [inner] * 4 + [first_width // 2] * 2),
         ],
         compiler_params=pltpu.CompilerParams(
-            collective_id=6, has_side_effects=True, vmem_limit_bytes=60 * 2**20
+            collective_id=5, has_side_effects=True, vmem_limit_bytes=62 * 2**20
         ),
-        name="final_block",
+        name="backward_block",
     )(
-        inputs, gain, grad_first, w_first, grad_hidden, grad_conv, grad_gain, grad_head,
-        grad_second, loss_row, grad_up,
+        mixed_in, little, gate_pre, conv, head, gain, *kept, grad_branch, inputs, norm_gain,
+        grad_hidden, grad_second, loss_row, w_first, grad_down, grad_up, grad_out,
     )
 
 
@@ -1462,17 +1464,13 @@
         return array.reshape(count // 2, 2, rows, array.shape[1])
 
     grad_up = by_place(grad_up)
-    grad_first, grad_conv, grad_gain_out, grad_head, sum_down, sum_gate, sum_out = backward_block(
-        mixed_in, little, gate_pre, own_conv, head, gain_row, kept, grad_branch,
-        by_place(grad_down), grad_up, by_place(grad_out),
-    )
     loss_row = jnp.concatenate(
         [loss_part[None], jnp.sum(mask_own)[None], jnp.zeros((126,), jnp.float32)]
     )[None]
-    grad_tokens, small_sum, sum_up, sum_in, sum_small = final_block(
-        inputs, gain_first[None], grad_first.reshape(2 * padded, first_width), w_first,
-        grad_hidden[:length], grad_conv, grad_gain_out, grad_head, grad_gain_second[None],
-        loss_row, grad_up, vals,
+    grad_tokens, small_sum, sum_down, sum_gate, sum_up, sum_out, sum_in, sum_small, unused = backward_block(
+        mixed_in, little, gate_pre, own_conv, head, gain_row, kept, grad_branch,
+        inputs, gain_first[None], grad_hidden[:length], grad_gain_second[None], loss_row, w_first,
+        by_place(grad_down), grad_up, by_place(grad_out),
     )
     valid_count = jnp.maximum(small_sum[5, 257], 1.0)
     loss_value = small_sum[5, 256] / valid_count

time: 476 us -> 445 us (0.935)
  Pallas kernels: 388 us -> 357 us
    pallas_call x2 -> x1, Pallas kernels: 223 us -> 192 us  [backward_block(): pl.pallas_call(functools.partial(backward_kernel, groups, count), out_sha...]
where the time goes in v5:
time: 445 us; the launch traced here: 436 us
  Pallas kernels  357 us (80%)
  matrix products  29.8 us (7%)
  other arithmetic  25.5 us (6%)
  local copies, waits for them, and re-layouts  16.7 us (4%)
    pallas_call x1, Pallas kernels, backward_block(): pl.pallas_call(functools.partial(backward_kernel, groups, count), out_sha...  192 us
    pallas_call x1, Pallas kernels, forward_block(): pl.pallas_call(functools.partial(forward_kernel, groups, count, shares),...  165 us
    dot_general x9, matrix products, dense(): lax.dot_general(left, right, (dims, ((), ())), preferred_element_type=jnp...  29.8 us
    mul x9, other arithmetic, scaled(): return array.astype(jnp.float32) * factor  11.7 us
  transfers between devices with their start and end apart: 3, of which 2 were waited for; matrix products, arithmetic and copies ran while one was open for 3% of the time, Pallas kernels for 0%

profile of v5, /device:TPU:0, one launch (start us, length us, event | category | flops | bytes accessed | tf_op | source)
XLA Modules:
  0.0 436.5 jit_solution(3251248590485998731)
XLA Ops:
  4.1 1.6 constant_dynamic-slice_fusion.3.refs_8_
  6.5 1.0 constant_dynamic-slice_fusion.8
  7.5 1.1 constant_dynamic-slice_fusion.4
  10.9 1.0 concatenate.45.refs_7_
  12.5 165.1 %forward_block.1 = (bf16[544,1024]{1,0:T(8,128)(2,1)}, bf16[256,1024]{1,0:T(8,128)(2,1)}, f32[8,256]{1,0:T(8,128)}, bf16[2,272,1536]{2,1,0:T(8,128)(2,1)}, f32[2...) custom-call(bf16[256,1024]{1,0:T(8,128)(2,1)} %bitcast.51, ...), custom_call_target="tpu_custom_call" | custom-call | tf_op jit(solution)/shard_map/forward_block/pallas_call | solution.py:876
  177.6 2.7 fusion.20
  180.4 1.2 slice.79
  181.6 1.4 collective-permute-done
  184.5 3.2 fusion.7
  188.6 1.0 copy-done.18
  189.5 1.8 fusion.21
  193.0 1.1 collective-permute-done.1
  194.2 1.8 convert_subtract_fusion
  196.1 4.0 fusion.8
  201.5 5.0 %fusion.22 = (bf16[512,1024]{1,0:T(8,128)(2,1)S(1)}, f32[512,1024]{1,0:T(8,128)S(1)}) fusion(bf16[1024,2816]{1,0:T(8,128)(2,1)S(1)} %bitcast.81, f32[512,1408]{1,0:T(8,128)} %get-tuple-element.87, f32[512,1408]{1,0:T(8,128)S(1)} %get-tuple-element.86), kind=kOutput, calls=%fused_computation.83 | convolution fusion | flops 2956197888 | bytes 14680064 | tf_op jit(solution)/shard_map/dot_general | solution.py:1356
  206.8 1.9 maximum_bitcast_fusion.refs_18_
  208.7 3.5 convolution_convert_fusion.1
  212.2 5.4 %convolution_convert_fusion = bf16[1024,2816]{1,0:T(8,128)(2,1)} fusion(f32[512,1408]{1,0:T(8,128)S(1)} %copy-done.19, f32[512,1408]{1,0:T(8,128)S(1)} %get-tuple-element.86, f32[512,1024]{1,0:T(8,128)S(1)} %broadcast_multiply_fusion, f32[1024]{0:T(1024)S(1)} %copy-done.14), kind=kOutput, calls=%fused_computation.1 | convolution fusion | flops 2959605760 | bytes 13635584 | tf_op jit(solution)/shard_map/dot_general | solution.py:1356
  219.5 1.0 slice.114.refs_16_
  221.0 2.2 convolution_convert_fusion.2
  223.1 2.1 fusion.23.refs_13_
  225.2 192.3 %backward_block.1 = (f32[256,1024]{1,0:T(8,128)}, f32[8,3072]{1,0:T(8,128)}, bf16[128,2816]{1,0:T(8,128)(2,1)}, bf16[128,2816]{1,0:T(8,128)(2,1)}, bf16[128,2816...) custom-call(bf16[2,272,1536]{2,1,0:T(8,128)(2,1)} %get-tuple-element, ...), custom_call_target="tpu_custom_call" | custom-call | tf_op jit(solution)/shard_map/backward_block/pallas_call | solution.py:1282
  417.6 1.3 fusion.18
  419.6 1.3 slice_multiply_fusion.5
  420.9 1.2 multiply_bitcast_fusion.1
  422.1 1.4 slice_multiply_fusion.3
  423.5 1.5 slice_multiply_fusion.2
  425.7 2.3 multiply_bitcast_fusion
  428.4 1.0 convert_multiply_fusion.3
  429.4 1.2 convert_multiply_fusion.2
  430.6 1.6 convert_multiply_fusion.1
  432.4 1.9 convert_multiply_fusion
  (88 shorter events, 16.5 us)
Async XLA Ops:
  0.6 5.1 %copy-start = (bf16[128,2816]{1,0:T(8,128)(2,1)S(1)}, bf16[128,2816]{1,0:T(8,128)(2,1)}, u32[]{:S(2)}) copy-start(bf16[128,2816]{1,0:T(8,128)(2,1)} %param.21) | copy-start | bytes 2162692
  2.5 6.0 %copy-start.12 = (bf16[128,5632]{1,0:T(8,128)(2,1)S(1)}, bf16[128,5632]{1,0:T(8,128)(2,1)}, u32[]{:S(2)}) copy-start(bf16[128,5632]{1,0:T(8,128)(2,1)} %param.20) | copy-start | bytes 4325380
  6.5 3.1 copy-start.16
  6.5 3.1 copy-start.17
  180.3 2.8 copy-start.2
  180.3 2.7 collective-permute-start
  180.4 3.6 slice-start
  183.1 1.4 slice-start.1
  183.6 0.9 copy-start.14
  187.7 1.8 copy-start.18
  189.5 2.9 copy-start.15
  191.4 2.8 copy-start.3
  191.4 2.8 copy-start.10
  191.4 2.7 collective-permute-start.1
  206.6 11.0 %collective-permute-start.2 = (bf16[512,1024]{1,0:T(8,128)(2,1)S(1)}, bf16[512,1024]{1,0:T(8,128)(2,1)S(1)}, u32[]{:S(2)}, u32[]{:S(2)}) collective-permute-start(bf16[512,1024]{1,0:T(8,128)(2,1)S(1)} %get-tuple-element.118), channel_id=1, source_target_pairs={{0,8},{8,0},{16,24},{24,16},{1,9},{9,1},{17,25},{25,17},{2,10},{10... | collective-permute-start | bytes 3145736 | tf_op jit(solution)/shard_map/ppermute | solution.py:1434
  208.7 3.5 copy-start.19
  219.5 1.5 copy-start.6
  221.0 2.2 copy-start.4
  417.6 10.4 %copy-start.13 = (bf16[128,256]{1,0:T(8,128)(2,1)S(1)}, bf16[128,256]{1,0:T(8,128)(2,1)}, u32[]{:S(2)}) copy-start(bf16[128,256]{1,0:T(8,128)(2,1)} %get-tuple-element.61) | copy-start | bytes 196612
  417.6 10.8 %copy-start.11 = (bf16[128,1536]{1,0:T(8,128)(2,1)S(1)}, bf16[128,1536]{1,0:T(8,128)(2,1)}, u32[]{:S(2)}) copy-start(bf16[128,1536]{1,0:T(8,128)(2,1)} %get-tuple-element.62) | copy-start | bytes 1179652
  417.6 11.8 %copy-start.9 = (bf16[128,2816]{1,0:T(8,128)(2,1)S(1)}, bf16[128,2816]{1,0:T(8,128)(2,1)}, u32[]{:S(2)}) copy-start(bf16[128,2816]{1,0:T(8,128)(2,1)} %get-tuple-element.65) | copy-start | bytes 2162692
  428.0 2.6 copy-start.5
  430.6 1.7 copy-start.7
  430.6 1.8 copy-start.8
  432.3 2.6 copy-start.1
